TPU v7x, 32 devices: a whole 2x2x4 slice. The times are simulated.
32 devices in a mesh: req: 4 (over y, x), kv: 8 (over z, core).
Axes of the slice: x: 2, y: 2, z: 4, core: 2. Of those that a mesh axis runs over, the one named last changes fastest.
Arguments:
- stream: bfloat16 [4096, 2048], P(('req', 'kv')), may hold values from -40 to 40
- projections: bfloat16 [4096, 6144], P(('req', 'kv')), may hold values from -32 to 32
- key_cache: bfloat16 [32768, 2048], P(('req', 'kv')), may hold values from -12 to 12
- value_cache: bfloat16 [32768, 2048], P(('req', 'kv')), may hold values from -6 to 6
- cache_range: int32 [4, 2], replicated, may hold values from 0 to 8192, as said below
- norm_gain: float32 [2048], replicated, may hold values from 0.5 to 1.5
- out_weight: bfloat16 [2048, 2048], P(('req', 'kv')), may hold values from -0.125 to 0.125
- up_weight: bfloat16 [8192, 2048], P(('req', 'kv')), may hold values from -0.125 to 0.125
- down_weight: bfloat16 [8192, 2048], P(('req', 'kv')), may hold values from -0.0625 to 0.0625
Outputs:
- layer_out: bfloat16 [4096, 2048], P(('req', 'kv'))
Inputs may be any that keep to these rules, and one draw needn't show every extreme that they name: `cache_range`: row r holds the first and the end of the cached positions that request r attends to: 0 <= first < 2048, first < end <= 8192, and end = 8192 for some request.
All inputs are finite; a program needn't handle non-finite values.
Results may differ from a plain program's by a relative error of at most 0.011.
Values may be sent and summed in bfloat16 or wider, within the bound.
A program may use at most 192 MiB of HBM per device.

v0:
```python
import math

import jax
import jax.numpy as jnp
from jax import lax
from jax.sharding import PartitionSpec as P

HD = 256
SPAN = 8


NEG_FILL = -1e30
NORM_EPS = 1e-05


def partner_2(value, axis, stride):
    mask = 2**stride
    pairs = [(source, source ^ mask) for source in range(lax.axis_size(axis))]
    return lax.ppermute(value, axis, pairs)


def shortened(array):

    def short(part):
        return part.astype(jnp.bfloat16) if part.dtype == jnp.float32 else part

    return jax.tree.map(short, array)


def layer_norm(stream, norm_gain):
    values = stream.astype(jnp.float32)
    centred = values - jnp.mean(values, axis=-1, keepdims=True)
    spread = jnp.mean(centred * centred, axis=-1, keepdims=True)
    return (centred * lax.rsqrt(spread + NORM_EPS) * norm_gain).astype(jnp.bfloat16)


def attend_block(query_block, key_rows, value_rows, visible):
    head_count = key_rows.shape[1]
    head_size = key_rows.shape[2]
    scores = jnp.einsum(
        "qhd,khd->hqk", query_block, key_rows, preferred_element_type=jnp.float32
    ) * (1.0 / math.sqrt(head_size))
    scores = jnp.where(visible[None], scores, NEG_FILL)
    row_max = jnp.max(scores, axis=-1)
    weights = jnp.where(visible[None], jnp.exp(scores - row_max[..., None]), 0.0)
    denominator = jnp.sum(weights, axis=-1)
    numerator = jnp.einsum(
        "hqk,khd->qhd", weights.astype(jnp.bfloat16), value_rows, preferred_element_type=jnp.float32
    )
    return (
        numerator.reshape(query_block.shape[0], head_count * head_size),
        row_max.T,
        denominator.T,
    )


def combine_partials(earlier, later):
    numerator_one, maximum_one, denominator_one = earlier
    numerator_two, maximum_two, denominator_two = later
    joint_max = jnp.maximum(maximum_one, maximum_two)
    factor_one = jnp.exp(maximum_one - joint_max)
    factor_two = jnp.exp(maximum_two - joint_max)
    row_count, head_count = maximum_one.shape
    merged = (
        numerator_one.reshape(row_count, head_count, -1) * factor_one[..., None]
        + numerator_two.reshape(row_count, head_count, -1) * factor_two[..., None]
    )
    return (
        merged.reshape(row_count, -1),
        joint_max,
        denominator_one * factor_one + denominator_two * factor_two,
    )


def unit_adder(inputs, pieces):
    gates = lax.dot_general(
        inputs, pieces[0], (((1,), (1,)), ((), ())), preferred_element_type=jnp.float32
    )
    hidden = jax.nn.gelu(gates, approximate=False).astype(jnp.bfloat16)
    return jnp.dot(hidden, pieces[1], preferred_element_type=jnp.float32)


def on_device(
    stream,
    projections,
    key_cache,
    value_cache,
    cache_range,
    norm_gain,
    out_weight,
    up_weight,
    down_weight,
):
    token_count, model_width = stream.shape
    cache_rows = key_cache.shape[0]
    head_size = HD
    head_count = model_width // head_size
    group_size = SPAN
    levels = group_size.bit_length() - 1
    kv_count = lax.axis_size("kv")
    kv_place = lax.axis_index("kv")
    req_place = lax.axis_index("req")
    member = kv_place % group_size
    request = (req_place * kv_count + kv_place) // group_size
    queries = projections[:, :model_width]
    for level in range(levels):
        partner = partner_2(queries, "kv", level)
        lower = kv_place >> level & 1 == 0
        queries = jnp.where(
            lower, jnp.concatenate([queries, partner], 0), jnp.concatenate([partner, queries], 0)
        )
    new_total = queries.shape[0]
    block_rows = min(512, new_total)
    block_count = new_total // block_rows
    query_blocks = queries.reshape(block_count, block_rows, head_count, head_size)
    block_starts = jnp.arange(block_count, dtype=jnp.int32) * block_rows
    pick = (jnp.arange(cache_range.shape[0], dtype=jnp.int32) == request)[:, None]
    bounds = jnp.sum(jnp.where(pick, cache_range, 0), axis=0)
    positions = member * cache_rows + jnp.arange(cache_rows, dtype=jnp.int32)
    cache_visible = (positions >= bounds[0]) & (positions < bounds[1])
    new_positions = member * token_count + jnp.arange(token_count, dtype=jnp.int32)
    new_keys = projections[:, model_width : 2 * model_width].reshape(
        token_count, head_count, head_size
    )
    new_values = projections[:, 2 * model_width :].reshape(token_count, head_count, head_size)
    cached_keys = key_cache.reshape(cache_rows, head_count, head_size)
    cached_values = value_cache.reshape(cache_rows, head_count, head_size)

    def new_visible(offset):
        query_positions = offset + jnp.arange(block_rows, dtype=jnp.int32)
        return new_positions[None, :] <= query_positions[:, None]

    all_keys = jnp.concatenate([cached_keys, new_keys], 0)
    all_values = jnp.concatenate([cached_values, new_values], 0)

    def one_block(item):
        query_block, offset = item
        visible = jnp.concatenate(
            [
                jnp.broadcast_to(cache_visible[None, :], (block_rows, cache_rows)),
                new_visible(offset),
            ],
            1,
        )
        return attend_block(query_block, all_keys, all_values, visible)

    partial_sums = lax.map(one_block, (query_blocks, block_starts))
    numerator = partial_sums[0].reshape(new_total, model_width)
    row_max = partial_sums[1].reshape(new_total, head_count)
    denominator = partial_sums[2].reshape(new_total, head_count)
    row_count = new_total
    for level in reversed(range(levels)):
        half_rows = row_count // 2
        upper = kv_place >> level & 1
        kept = tuple(
            (
                lax.dynamic_slice_in_dim(member_part, upper * half_rows, half_rows, 0)
                for member_part in (numerator, row_max, denominator)
            )
        )
        given = tuple(
            (
                lax.dynamic_slice_in_dim(member_part, (1 - upper) * half_rows, half_rows, 0)
                for member_part in (numerator, row_max, denominator)
            )
        )
        received = partner_2(
            (shortened(given[0]), shortened(given[1]), shortened(given[2])), "kv", level
        )
        numerator, row_max, denominator = combine_partials(kept, received)
        row_count = half_rows
    attention = (
        (numerator.reshape(token_count, head_count, head_size) / denominator[..., None])
        .reshape(token_count, model_width)
        .astype(jnp.bfloat16)
    )
    normed = layer_norm(stream, norm_gain)
    head_part = lax.all_to_all(attention, "req", split_axis=1, concat_axis=0, tiled=True)
    projected = jnp.dot(
        head_part,
        lax.all_gather(out_weight, "kv", axis=0, tiled=True),
        preferred_element_type=jnp.float32,
    )
    row_inputs = lax.all_gather(normed, "req", axis=0, tiled=True)
    units = unit_adder(
        row_inputs,
        (
            lax.all_gather(up_weight, "kv", axis=0, tiled=True),
            lax.all_gather(down_weight, "kv", axis=0, tiled=True),
        ),
    )
    summed = lax.psum_scatter(
        projected.astype(jnp.bfloat16), "req", scatter_dimension=0, tiled=True
    ).astype(jnp.float32) + lax.psum_scatter(
        units.astype(jnp.bfloat16), "req", scatter_dimension=0, tiled=True
    ).astype(
        jnp.float32
    )
    return (stream.astype(jnp.float32) + summed).astype(jnp.bfloat16)


def solution(mesh):
    in_specs = (
        P(("req", "kv"), None),
        P(("req", "kv"), None),
        P(("req", "kv"), None),
        P(("req", "kv"), None),
        P(),
        P(),
        P(("req", "kv"), None),
        P(("req", "kv"), None),
        P(("req", "kv"), None),
    )
    out_specs = P(("req", "kv"), None)
    return jax.shard_map(
        on_device, mesh=mesh, in_specs=in_specs, out_specs=out_specs, check_vma=False
    )
```

profile of v0, /device:TPU:0, one launch (start us, length us, event | category | flops | bytes accessed | tf_op | source)
XLA Modules:
  0.0 563.4 jit_solution(8266842765267841770)
XLA Ops:
  16.2 3.0 collective-permute-start.1
  19.3 40.4 %collective-permute-done.1 = bf16[256,2048]{1,0:T(8,128)(2,1)} collective-permute-done((bf16[256,2048]{1,0:T(8,128)(2,1)S(1)}, bf16[256,2048]{1,0:T(8,128)(2,1)}, u32[]{:S(2)}, u32[]{:S(2)}) %collective-permute-start.1) | collective-permute-done | bytes 1048608 | tf_op jit(solution)/shard_map/ppermute | solution.py:19
  66.4 6.7 %copy.12 = bf16[1024,2048]{0,1:T(8,128)(2,1)} copy(bf16[1024,2048]{1,0:T(8,128)(2,1)} %param.13) | data formatting | bytes 8388608 | tf_op args[2]
  73.1 4.9 pad_maximum_fusion
  78.0 6.7 %copy.17 = bf16[1152,8,256]{2,0,1:T(8,128)(2,1)} copy(bf16[1152,8,256]{0,2,1:T(8,128)(2,1)} %pad_maximum_fusion) | data formatting | bytes 9437184
  85.0 6.4 %copy.14 = bf16[1024,2048]{0,1:T(8,128)(2,1)} copy(bf16[1024,2048]{1,0:T(8,128)(2,1)} %param.14) | data formatting | bytes 8388608 | tf_op args[3]
  92.3 4.9 pad_maximum_fusion.1
  97.1 126.0 %collective-permute-done.2 = bf16[512,2048]{1,0:T(8,128)(2,1)} collective-permute-done((bf16[512,2048]{1,0:T(8,128)(2,1)S(1)}, bf16[512,2048]{1,0:T(8,128)(2,1)}, u32[]{:S(2)}, u32[]{:S(2)}) %collective-permute-start.2) | collective-permute-done | bytes 2097184 | tf_op jit(solution)/shard_map/ppermute | solution.py:19
  223.1 4.0 maximum_select_fusion
  227.1 3.4 copy.34
  230.5 85.9 %while.15 = (s32[]{:T(128)}, f32[2,512,2048]{2,1,0:T(8,128)}, f32[2,512,8]{1,2,0:T(8,128)S(1)}, f32[2,512,8]{1,2,0:T(8,128)S(1)}, s32[2]{0:T(128)S(1)}, /*index=...) while((s32[]{:T(128)}, f32[2,512,2048]{2,1,0:T(8,128)}, ...), condition=%wide.region_4.5_spmd.clone, body=%wide.region_1.4_spmd.clone.sunk | while | flops 4874957824 | bytes 128985080 | solution.py:147
  235.8 9.0 %fusion.128 = (f32[8,512]{1,0:T(8,128)S(1)}, f32[8,512,1152]{2,1,0:T(8,128)}) fusion(bf16[1152,8,256]{2,0,1:T(8,128)(2,1)S(1)} %copy-done.6, bf16[1,512,8,256]{3,2,1,0:T(8,128)(2,1)S(1)} %constant_dynamic-slice_fusion.6, pred[512,1152]{1,0:T(8,128)(4,1)S(1)} %pad_add_fusion.2), kind=kOutput, calls=%fused_computation.158.clone.1 | convolution fusion | flops 2430070784 | bytes 26296320 | tf_op jit(solution)/shard_map/while/body/eval_jaxpr/qhd,khd->hqk/dot_general | solution.py:40
  244.8 8.6 %fusion.130 = f32[8,512]{1,0:T(8,128)S(1)} fusion(f32[8,512,1152]{2,1,0:T(8,128)} %get-tuple-element.226, f32[8,512]{1,0:T(8,128)S(1)} %get-tuple-element.227, pred[512,1152]{1,0:T(8,128)(4,1)S(1)} %pad_add_fusion.2), kind=kLoop, calls=%fused_computation.5.clone.1 | loop fusion | flops 14151680 | bytes 19496960 | tf_op jit(solution)/shard_map/while/body/eval_jaxpr/reduce_sum | solution.py:46
  253.5 9.8 %fusion.129 = f32[8,512,256]{1,2,0:T(8,128)} fusion(bf16[1152,8,256]{0,2,1:T(8,128)(2,1)S(1)} %bitcast.83, f32[8,512,1152]{2,1,0:T(8,128)} %get-tuple-element.226, f32[8,512]{1,0:T(8,128)S(1)} %get-tuple-element.227, pred[512,1152]{1,0:T(8,128)(4,1)S(1)} %pad_add_fusion.2), kind=kOutput, calls=%fused_computation.7.clone.1 | convolution fusion | flops 2430074880 | bytes 28393472 | tf_op jit(solution)/shard_map/while/body/eval_jaxpr/hqk,khd->qhd/dot_general | solution.py:47
  263.3 5.5 copy.51
  268.8 4.8 constant_dynamic-update-slice_fusion.2
  278.8 8.9 %fusion.128 = (f32[8,512]{1,0:T(8,128)S(1)}, f32[8,512,1152]{2,1,0:T(8,128)}) fusion(bf16[1152,8,256]{2,0,1:T(8,128)(2,1)S(1)} %copy-done.6, bf16[1,512,8,256]{3,2,1,0:T(8,128)(2,1)S(1)} %constant_dynamic-slice_fusion.6, pred[512,1152]{1,0:T(8,128)(4,1)S(1)} %pad_add_fusion.2), kind=kOutput, calls=%fused_computation.158.clone.1 | convolution fusion | flops 2430070784 | bytes 26296320 | tf_op jit(solution)/shard_map/while/body/eval_jaxpr/qhd,khd->hqk/dot_general | solution.py:40
  287.7 8.6 %fusion.130 = f32[8,512]{1,0:T(8,128)S(1)} fusion(f32[8,512,1152]{2,1,0:T(8,128)} %get-tuple-element.226, f32[8,512]{1,0:T(8,128)S(1)} %get-tuple-element.227, pred[512,1152]{1,0:T(8,128)(4,1)S(1)} %pad_add_fusion.2), kind=kLoop, calls=%fused_computation.5.clone.1 | loop fusion | flops 14151680 | bytes 19496960 | tf_op jit(solution)/shard_map/while/body/eval_jaxpr/reduce_sum | solution.py:46
  296.4 9.5 %fusion.129 = f32[8,512,256]{1,2,0:T(8,128)} fusion(bf16[1152,8,256]{0,2,1:T(8,128)(2,1)S(1)} %bitcast.83, f32[8,512,1152]{2,1,0:T(8,128)} %get-tuple-element.226, f32[8,512]{1,0:T(8,128)S(1)} %get-tuple-element.227, pred[512,1152]{1,0:T(8,128)(4,1)S(1)} %pad_add_fusion.2), kind=kOutput, calls=%fused_computation.7.clone.1 | convolution fusion | flops 2430074880 | bytes 28393472 | tf_op jit(solution)/shard_map/while/body/eval_jaxpr/hqk,khd->qhd/dot_general | solution.py:47
  305.9 5.5 copy.51
  311.4 4.7 constant_dynamic-update-slice_fusion.2
  319.0 2.9 collective-permute-start.3
  322.0 89.4 %collective-permute-done.3 = bf16[512,8]{0,1:T(8,128)(2,1)S(1)} collective-permute-done((bf16[512,8]{0,1:T(8,128)(2,1)S(1)}, bf16[512,8]{0,1:T(8,128)(2,1)S(1)}, u32[]{:S(2)}, u32[]{:S(2)}) %collective-permute-start.3) | collective-permute-done | bytes 8224 | tf_op jit(solution)/shard_map/ppermute | solution.py:19
  412.3 3.9 copy.35
  419.1 4.5 multiply_add_fusion
  428.8 21.3 %collective-permute-done.5 = bf16[256,8]{0,1:T(8,128)(2,1)S(1)} collective-permute-done((bf16[256,8]{0,1:T(8,128)(2,1)S(1)}, bf16[256,8]{0,1:T(8,128)(2,1)S(1)}, u32[]{:S(2)}, u32[]{:S(2)}) %collective-permute-start.5) | collective-permute-done | bytes 4128 | tf_op jit(solution)/shard_map/ppermute | solution.py:19
  464.2 3.5 all-to-all-start
  467.8 8.5 %all-to-all-done = bf16[128,4,512]{2,0,1:T(8,128)(2,1)S(1)} async-done(((bf16[128,4,512]{2,0,1:T(8,128)(2,1)}), bf16[128,4,512]{2,0,1:T(8,128)(2,1)S(1)}, u32[]{:S(2)}, u32[]{:S(2)}) %all-to-all-start) | async-done | bytes 524320 | tf_op jit(solution)/shard_map/all_to_all | solution.py:178
  476.3 4.2 convolution_convert_fusion.1
  480.8 22.7 %convolution_convert_fusion = bf16[512,2048]{1,0:T(8,128)(2,1)} fusion(bf16[2048,2048]{1,0:T(8,128)(2,1)} %all-gather.11.cloned.1.call-done, bf16[512,2048]{1,0:T(8,128)(2,1)} %all-gather.7.cloned.1.call-done, bf16[2048,2048]{1,0:T(8,128)(2,1)} %all-gather.9.cloned.1.call-done), kind=kOutput, calls=%fused_computation.49 | convolution fusion | flops 8659140608 | bytes 20971520 | tf_op jit(solution)/shard_map/dot_general | solution.py:80
  503.5 12.3 %reduce-scatter.3.cloned.1.call-done = bf16[128,2048]{1,0:T(8,128)(2,1)} async-done(((bf16[512,2048]{1,0:T(8,128)(2,1)}), bf16[128,2048]{1,0:T(8,128)(2,1)}) %reduce-scatter.3.cloned.1.call-update) | async-done | bytes 524304 | tf_op jit(solution)/shard_map/reduce_scatter | solution.py:192
  515.8 38.3 %reduce-scatter.5.cloned.1.call-done = bf16[128,2048]{1,0:T(8,128)(2,1)} async-done(((bf16[512,2048]{1,0:T(8,128)(2,1)}), bf16[128,2048]{1,0:T(8,128)(2,1)}) %reduce-scatter.5.cloned.1.call-update) | async-done | bytes 524304 | tf_op jit(solution)/shard_map/reduce_scatter | solution.py:194
  (137 shorter events, 55.9 us)
Async XLA Ops:
  6.5 6.3 %copy-start.8 = (bf16[128,6144]{1,0:T(8,128)(2,1)S(1)}, bf16[128,6144]{1,0:T(8,128)(2,1)}, u32[]{:S(2)}) copy-start(bf16[128,6144]{1,0:T(8,128)(2,1)} %param.12) | copy-start | bytes 4718596
  6.5 461.2 %all-gather.5.cloned.1.call-start = ((), (), s32[]{:S(2)}) async-start(), calls=%async_computation.3 | async-start | bytes 2359296 | tf_op jit(solution)/shard_map/all_gather | solution.py:181
  7.3 473.5 %all-gather.7.cloned.1.call-start = ((), (), s32[]{:S(2)}) async-start(), calls=%async_computation.5 | async-start | bytes 2621440 | tf_op jit(solution)/shard_map/all_gather | solution.py:184
  12.1 468.7 %all-gather.11.cloned.1.call-start = ((), (), s32[]{:S(2)}) async-start(), calls=%async_computation.7 | async-start | bytes 9437184 | tf_op jit(solution)/shard_map/all_gather | solution.py:189
  12.8 468.0 %all-gather.9.cloned.1.call-start = ((), (), s32[]{:S(2)}) async-start(), calls=%async_computation.6 | async-start | bytes 9437184 | tf_op jit(solution)/shard_map/all_gather | solution.py:188
  14.0 2.0 collective-permute-start
  16.2 43.4 %collective-permute-start.1 = (bf16[256,2048]{1,0:T(8,128)(2,1)S(1)}, bf16[256,2048]{1,0:T(8,128)(2,1)}, u32[]{:S(2)}, u32[]{:S(2)}) collective-permute-start(bf16[256,2048]{1,0:T(8,128)(2,1)S(1)} %maximum_select_fusion.2), channel_id=1, source_target_pairs={{0,2},{1,3},{2,0},{3,1},{4,6},{5,7},{6,4},{7,5},{8,10},{9,11},{10,... | collective-permute-start | bytes 3145736 | tf_op jit(solution)/shard_map/ppermute | solution.py:19
  62.1 161.0 %collective-permute-start.2 = (bf16[512,2048]{1,0:T(8,128)(2,1)S(1)}, bf16[512,2048]{1,0:T(8,128)(2,1)}, u32[]{:S(2)}, u32[]{:S(2)}) collective-permute-start(bf16[512,2048]{1,0:T(8,128)(2,1)S(1)} %maximum_select_fusion.1), channel_id=1, source_target_pairs={{0,4},{1,5},{2,6},{3,7},{4,0},{5,1},{6,2},{7,3},{8,12},{9,13},{10,... | collective-permute-start | bytes 6291464 | tf_op jit(solution)/shard_map/ppermute | solution.py:19
  78.0 6.8 %copy-start.7 = (bf16[128,2048]{1,0:T(8,128)(2,1)S(1)}, bf16[128,2048]{1,0:T(8,128)(2,1)}, u32[]{:S(2)}) copy-start(bf16[128,2048]{1,0:T(8,128)(2,1)} %get-tuple-element.144) | copy-start | bytes 1572868
  85.0 6.4 %copy-start.9 = (s32[4,2]{0,1:T(2,128)S(1)}, s32[4,2]{0,1:T(2,128)}, u32[]{:S(2)}) copy-start(s32[4,2]{0,1:T(2,128)} %param.15) | copy-start | bytes 100
  230.5 5.3 copy-start.6
  233.8 19.6 %slice-start = ((s8[4718592]{0:T(1024)(128)(4,1)}), s8[4194304]{0:T(1024)(128)(4,1)S(1)}, s32[]{:S(2)}) async-start(s8[4718592]{0:T(1024)(128)(4,1)} %bitcast.82), calls=%async_computation.9 | async-start | bytes 8388608 | tf_op jit(solution)/shard_map/while
  235.7 17.7 %slice-start.1 = ((s8[4718592]{0:T(1024)(128)(4,1)}), s8[524288]{0:T(1024)(128)(4,1)S(1)}, s32[]{:S(2)}) async-start(s8[4718592]{0:T(1024)(128)(4,1)} %bitcast.82), calls=%async_computation.10 | async-start | bytes 1048576 | tf_op jit(solution)/shard_map/while
  273.6 5.2 copy-start.6
  276.9 19.4 %slice-start = ((s8[4718592]{0:T(1024)(128)(4,1)}), s8[4194304]{0:T(1024)(128)(4,1)S(1)}, s32[]{:S(2)}) async-start(s8[4718592]{0:T(1024)(128)(4,1)} %bitcast.82), calls=%async_computation.9 | async-start | bytes 8388608 | tf_op jit(solution)/shard_map/while
  278.8 17.5 %slice-start.1 = ((s8[4718592]{0:T(1024)(128)(4,1)}), s8[524288]{0:T(1024)(128)(4,1)S(1)}, s32[]{:S(2)}) async-start(s8[4718592]{0:T(1024)(128)(4,1)} %bitcast.82), calls=%async_computation.10 | async-start | bytes 1048576 | tf_op jit(solution)/shard_map/while
  318.9 100.0 %collective-permute-start.4 = (bf16[512,2048]{1,0:T(8,128)(2,1)S(1)}, bf16[512,2048]{1,0:T(8,128)(2,1)}, u32[]{:S(2)}, u32[]{:S(2)}) collective-permute-start(bf16[512,2048]{1,0:T(8,128)(2,1)S(1)} %dynamic-slice_convert_fusion), channel_id=1, source_target_pairs={{0,4},{1,5},{2,6},{3,7},{4,0},{5,1},{6,2},{7,3},{8,12},{9,13},{10,... | collective-permute-start | bytes 6291464 | tf_op jit(solution)/shard_map/ppermute | solution.py:19
  319.0 92.4 %collective-permute-start.3 = (bf16[512,8]{0,1:T(8,128)(2,1)S(1)}, bf16[512,8]{0,1:T(8,128)(2,1)S(1)}, u32[]{:S(2)}, u32[]{:S(2)}) collective-permute-start(bf16[512,8]{0,1:T(8,128)(2,1)S(1)} %dynamic-slice_convert_fusion.4), channel_id=1, source_target_pairs={{0,4},{1,5},{2,6},{3,7},{4,0},{5,1},{6,2},{7,3},{8,12},{9,13},{10,... | collective-permute-start | bytes 24584 | tf_op jit(solution)/shard_map/ppermute | solution.py:19
  321.9 89.6 %collective-permute-start.9 = (bf16[512,8]{0,1:T(8,128)(2,1)S(1)}, bf16[512,8]{0,1:T(8,128)(2,1)S(1)}, u32[]{:S(2)}, u32[]{:S(2)}) collective-permute-start(bf16[512,8]{0,1:T(8,128)(2,1)S(1)} %dynamic-slice_convert_fusion.3), channel_id=1, source_target_pairs={{0,4},{1,5},{2,6},{3,7},{4,0},{5,1},{6,2},{7,3},{8,12},{9,13},{10,... | collective-permute-start | bytes 24584 | tf_op jit(solution)/shard_map/ppermute | solution.py:19
  416.9 2.2 copy-start
  426.7 26.2 %collective-permute-start.6 = (bf16[256,2048]{1,0:T(8,128)(2,1)}, bf16[256,2048]{1,0:T(8,128)(2,1)S(1)}, u32[]{:S(2)}, u32[]{:S(2)}) collective-permute-start(bf16[256,2048]{1,0:T(8,128)(2,1)} %dynamic-slice_convert_fusion.1), channel_id=1, source_target_pairs={{0,2},{1,3},{2,0},{3,1},{4,6},{5,7},{6,4},{7,5},{8,10},{9,11},{10,... | collective-permute-start | bytes 3145736 | tf_op jit(solution)/shard_map/ppermute | solution.py:19
  426.7 23.3 %collective-permute-start.5 = (bf16[256,8]{0,1:T(8,128)(2,1)S(1)}, bf16[256,8]{0,1:T(8,128)(2,1)S(1)}, u32[]{:S(2)}, u32[]{:S(2)}) collective-permute-start(bf16[256,8]{0,1:T(8,128)(2,1)S(1)} %dynamic-slice_convert_fusion.6), channel_id=1, source_target_pairs={{0,2},{1,3},{2,0},{3,1},{4,6},{5,7},{6,4},{7,5},{8,10},{9,11},{10,... | collective-permute-start | bytes 12296 | tf_op jit(solution)/shard_map/ppermute | solution.py:19
  428.8 21.4 %collective-permute-start.10 = (bf16[256,8]{0,1:T(8,128)(2,1)S(1)}, bf16[256,8]{0,1:T(8,128)(2,1)S(1)}, u32[]{:S(2)}, u32[]{:S(2)}) collective-permute-start(bf16[256,8]{0,1:T(8,128)(2,1)S(1)} %dynamic-slice_convert_fusion.5), channel_id=1, source_target_pairs={{0,2},{1,3},{2,0},{3,1},{4,6},{5,7},{6,4},{7,5},{8,10},{9,11},{10,... | collective-permute-start | bytes 12296 | tf_op jit(solution)/shard_map/ppermute | solution.py:19
  451.6 2.2 copy-start.2
  456.7 4.9 collective-permute-start.8
  456.7 1.5 collective-permute-start.7
  457.3 1.4 collective-permute-start.11
  459.0 2.7 copy-start.5
  464.2 12.0 %all-to-all-start = ((bf16[128,4,512]{2,0,1:T(8,128)(2,1)}), bf16[128,4,512]{2,0,1:T(8,128)(2,1)S(1)}, u32[]{:S(2)}, u32[]{:S(2)}) async-start(bf16[128,4,512]{2,0,1:T(8,128)(2,1)} %bitcast.56), calls=%async_computation | async-start | bytes 1048576 | tf_op jit(solution)/shard_map/all_to_all | solution.py:178
  467.7 48.1 %reduce-scatter.3.cloned.1.call-start = ((), (), s32[]{:S(2)}) async-start(), calls=%async_computation.4 | async-start | bytes 2621440 | tf_op jit(solution)/shard_map/reduce_scatter | solution.py:192
  480.5 73.7 %copy-start.3 = (bf16[128,2048]{1,0:T(8,128)(2,1)S(1)}, bf16[128,2048]{1,0:T(8,128)(2,1)}, u32[]{:S(2)}) copy-start(bf16[128,2048]{1,0:T(8,128)(2,1)} %param.11) | copy-start | bytes 1572868
  480.5 73.6 %reduce-scatter.5.cloned.1.call-start = ((), (), s32[]{:S(2)}) async-start(), calls=%async_computation.8 | async-start | bytes 2621440 | tf_op jit(solution)/shard_map/reduce_scatter | solution.py:194
  (2 other events, 3.3 us)
Sparse Core Ops, SparseCore 0:
  9.0 44.5 all-gather.4
  55.4 38.9 all-gather.6
  95.9 118.9 all-gather.10
  216.4 81.5 all-gather.8
  480.6 35.1 reduce-scatter.2
  518.9 35.1 reduce-scatter.4
where the time goes:
time: 567 us; the launch traced here: 563 us
  waiting for transfers between devices  341 us (60%)
  local copies, waits for them, and re-layouts  75 us (13%)
  matrix products  64.2 us (11%)
  other arithmetic  53 us (9%)
  starting transfers between devices  15.9 us (3%)
  between operations  14.1 us (2%)
    ppermute x12, waiting for transfers between devices, partner_2(): return lax.ppermute(value, axis, pairs)  280 us
    unnamed x30, local copies, waits for them, and re-layouts  38.7 us
    reduce_scatter x1, waiting for transfers between devices, on_device(): lax.psum_scatter(units.astype(jnp.bfloat16), 'req', scatter_dimension=0,...  38.3 us
    dot_general x1, matrix products, unit_adder(): return jnp.dot(hidden, pieces[1], preferred_element_type=jnp.float32)  22.7 us
    dynamic_update_slice x6, local copies, waits for them, and re-layouts, on_device(): partial_sums = lax.map(one_block, (query_blocks, block_starts))  20.4 us
    dot_general x2, matrix products, attend_block(): jnp.einsum('hqk,khd->qhd', weights.astype(jnp.bfloat16), value_rows, pref...  19.3 us
    dot_general x2, matrix products, attend_block(): jnp.einsum('qhd,khd->hqk', query_block, key_rows, preferred_element_type=...  18 us
    reduce_sum x2, other arithmetic, attend_block(): denominator = jnp.sum(weights, axis=-1)  17.2 us
  transfers between devices with their start and end apart: 19, of which 11 were waited for; matrix products, arithmetic and copies ran while one was open for 33% of the time, Pallas kernels for 0%

commit v1 on v0

v1 whole, which is shorter than its diff:
```python
import jax
import jax.numpy as jnp
from jax import lax
from jax.experimental import pallas as pl
from jax.experimental.pallas import tpu as pltpu
from jax.sharding import PartitionSpec as P

HD = 256
SPAN = 8
CORES = 2
CHIPS = SPAN // CORES
LOWEST = -1e29
NEG_FILL = -1e30
NORM_EPS = 1e-05
ROW_TILE = 256
F32 = jnp.float32
BF16 = jnp.bfloat16


def swap_cores(value):
    pairs = [(k, k ^ 1) for k in range(lax.axis_size("kv"))]
    return lax.ppermute(value, "kv", pairs)


def next_chip(value):
    pairs = [
        (k, k - k % SPAN + (k % SPAN + CORES) % SPAN) for k in range(lax.axis_size("kv"))
    ]
    return lax.ppermute(value, "kv", pairs)


def gather_chips(value):
    size = lax.axis_size("kv")
    groups = [
        [first + core + CORES * chip for chip in range(CHIPS)]
        for first in range(0, size, SPAN)
        for core in range(CORES)
    ]
    return lax.all_gather(value, "kv", axis=0, tiled=True, axis_index_groups=groups)


def gather_requests(value):
    size = lax.axis_size("kv")
    if size > SPAN:
        groups = [list(range(m, size, SPAN)) for m in range(SPAN)]
        value = lax.all_gather(value, "kv", axis=0, tiled=True, axis_index_groups=groups)
    return lax.all_gather(value, "req", axis=0, tiled=True)


def layer_norm(stream, norm_gain):
    values = stream.astype(F32)
    centred = values - jnp.mean(values, axis=-1, keepdims=True)
    spread = jnp.mean(centred * centred, axis=-1, keepdims=True)
    return (centred * lax.rsqrt(spread + NORM_EPS) * norm_gain).astype(BF16)


def attend_kernel(
    meta, q_mine, q_other, key, value, new_key, new_value, bias, out, lse, value_t, new_value_t
):
    slot = pl.program_id(0)
    core = meta[2]
    member = meta[3]
    half = q_mine.shape[0]
    token_count = new_key.shape[0]
    value_t[...] = value[...].T
    new_value_t[...] = new_value[...].T
    for first in (0, 1):
        source = q_mine if first == 0 else q_other
        source_core = core if first == 0 else 1 - core
        place = jnp.where(slot == 0, first, 1 - first) * half
        for tile in range(half // ROW_TILE):
            queries = source[pl.ds(tile * ROW_TILE, ROW_TILE), :] * BF16(1.0 / 16.0)
            scores = lax.dot_general(
                key[...], queries, (((1,), (1,)), ((), ())), preferred_element_type=F32
            )
            scores = scores + bias[...]
            fresh = lax.dot_general(
                new_key[...], queries, (((1,), (1,)), ((), ())), preferred_element_type=F32
            )
            row = tile * ROW_TILE + lax.broadcasted_iota(jnp.int32, (1, ROW_TILE), 1)
            chip = row // token_count
            token = row + chip * token_count + source_core * token_count
            position = member * token_count + lax.broadcasted_iota(
                jnp.int32, (token_count, 1), 0
            )
            fresh = jnp.where(position <= token, fresh, NEG_FILL)
            largest = jnp.maximum(
                jnp.max(scores, axis=0, keepdims=True), jnp.max(fresh, axis=0, keepdims=True)
            )
            largest = jnp.maximum(largest, LOWEST)
            weights = jnp.exp(scores - largest)
            fresh = jnp.exp(fresh - largest)
            total = jnp.sum(weights, axis=0, keepdims=True) + jnp.sum(
                fresh, axis=0, keepdims=True
            )
            total = jnp.maximum(total, 1.0)
            sums = jnp.dot(
                value_t[...], weights.astype(BF16), preferred_element_type=F32
            ) + jnp.dot(new_value_t[...], fresh.astype(BF16), preferred_element_type=F32)
            lanes = pl.ds(pl.multiple_of(place + tile * ROW_TILE, ROW_TILE), ROW_TILE)
            out[0, :, lanes] = (sums / total).astype(BF16)
            lse[0, :, lanes] = largest + jnp.log(total)


def attend(meta, q_mine, q_other, key_cache, value_cache, projections, bias):
    half = q_mine.shape[0]
    cache_rows = key_cache.shape[0]
    token_count = projections.shape[0]
    heads = key_cache.shape[1] // HD
    q_spec = pl.BlockSpec((half, HD), lambda i, meta: (0, meta[i]))
    cache_spec = pl.BlockSpec((cache_rows, HD), lambda i, meta: (0, meta[i]))
    flops = 2 * 2 * 2 * 2 * half * (cache_rows + token_count) * HD
    return pl.pallas_call(
        attend_kernel,
        grid_spec=pltpu.PrefetchScalarGridSpec(
            num_scalar_prefetch=1,
            grid=(CORES,),
            in_specs=[
                q_spec,
                q_spec,
                cache_spec,
                cache_spec,
                pl.BlockSpec((token_count, HD), lambda i, meta: (0, heads + meta[i])),
                pl.BlockSpec((token_count, HD), lambda i, meta: (0, 2 * heads + meta[i])),
                pl.BlockSpec((cache_rows, 1), lambda i, meta: (0, 0)),
            ],
            out_specs=[
                pl.BlockSpec((1, HD, 2 * half), lambda i, meta: (i, 0, 0)),
                pl.BlockSpec((1, 1, 2 * half), lambda i, meta: (i, 0, 0)),
            ],
            scratch_shapes=[
                pltpu.VMEM((HD, cache_rows), BF16),
                pltpu.VMEM((HD, token_count), BF16),
            ],
        ),
        out_shape=[
            jax.ShapeDtypeStruct((CORES, HD, 2 * half), BF16),
            jax.ShapeDtypeStruct((CORES, 1, 2 * half), F32),
        ],
        compiler_params=pltpu.CompilerParams(vmem_limit_bytes=40 * 2**20),
        cost_estimate=pl.CostEstimate(
            flops=flops, bytes_accessed=8 * 2**20, transcendentals=flops // (4 * HD)
        ),
    )(meta, q_mine, q_other, key_cache, value_cache, projections, projections, bias)


def merge(parts):
    largest = parts[0][1]
    for part in parts[1:]:
        largest = jnp.maximum(largest, part[1])
    shares = [jnp.exp(part[1] - largest) for part in parts]
    total = sum(shares)
    joined = sum(part[0].astype(F32) * (share / total) for part, share in zip(parts, shares))
    return joined.astype(BF16), largest + jnp.log(total)


def on_device(
    stream,
    projections,
    key_cache,
    value_cache,
    cache_range,
    norm_gain,
    out_weight,
    up_weight,
    down_weight,
):
    token_count, width = stream.shape
    cache_rows = key_cache.shape[0]
    kv_count = lax.axis_size("kv")
    device_count = kv_count * lax.axis_size("req")
    request_count = device_count // SPAN
    kv_place = lax.axis_index("kv")
    member = kv_place % SPAN
    core = member % CORES
    chip = member // CORES
    request = (lax.axis_index("req") * kv_count + kv_place) // SPAN

    q_mine = gather_chips(projections[:, :width])
    q_other = swap_cores(q_mine)
    up_rows = gather_requests(up_weight)
    down_rows = gather_requests(down_weight)
    head_pairs = [
        (d, (d % request_count) * SPAN + d // request_count) for d in range(device_count)
    ]
    out_rows = gather_requests(lax.ppermute(out_weight, ("req", "kv"), head_pairs))

    bounds = lax.dynamic_slice_in_dim(cache_range, request, 1, 0)[0]
    positions = member * cache_rows + jnp.arange(cache_rows, dtype=jnp.int32)[:, None]
    bias = jnp.where((positions >= bounds[0]) & (positions < bounds[1]), 0.0, NEG_FILL)
    bias = bias.astype(F32)

    normed, _ = lax.optimization_barrier((layer_norm(stream, norm_gain), q_mine))
    rows_mine = gather_chips(normed)
    rows_other = swap_cores(rows_mine)

    carried = None
    for phase in range(CHIPS):
        target = (chip + CHIPS - 1 - phase) % CHIPS
        kept = CORES * target + core
        given = CORES * target + 1 - core
        meta = jnp.stack([kept, given, core, member]).astype(jnp.int32)
        out, lse = attend(meta, q_mine, q_other, key_cache, value_cache, projections, bias)
        parts = [(out[0], lse[0]), swap_cores((out[1], lse[1]))]
        if carried is not None:
            parts.append(carried)
        carried = merge(parts)
        if phase < CHIPS - 1:
            carried = next_chip(carried)
    attention = carried[0]

    def hidden_of(rows):
        gates = lax.dot_general(
            rows, up_rows, (((1,), (1,)), ((), ())), preferred_element_type=F32
        )
        return jax.nn.gelu(gates, approximate=False).astype(BF16)

    hidden_mine = hidden_of(rows_mine)
    hidden_other = hidden_of(rows_other)
    half = CHIPS * token_count
    running = None
    for phase in range(CHIPS):
        first = ((chip + CHIPS - 1 - phase) % CHIPS) * token_count

        def share(hidden, offset):
            block = lax.dynamic_slice_in_dim(attention, offset + first, token_count, 1)
            branch = lax.dot_general(
                block, out_rows, (((0,), (0,)), ((), ())), preferred_element_type=F32
            )
            units = lax.dynamic_slice_in_dim(hidden, first, token_count, 0)
            return branch + jnp.dot(units, down_rows, preferred_element_type=F32)

        total = share(hidden_mine, 0)
        total = total + swap_cores(share(hidden_other, half).astype(BF16)).astype(F32)
        if running is not None:
            total = total + running.astype(F32)
        running = total
        if phase < CHIPS - 1:
            running = next_chip(total.astype(BF16))
    return (stream.astype(F32) + running).astype(BF16)


def solution(mesh):
    rows = P(("req", "kv"), None)
    in_specs = (rows, rows, rows, rows, P(), P(), rows, rows, rows)
    return jax.shard_map(
        on_device, mesh=mesh, in_specs=in_specs, out_specs=rows, check_vma=False
    )
```

time: 567 us -> 316 us (0.56)
  waiting for transfers between devices: 341 us -> 177 us
  local copies, waits for them, and re-layouts: 75 us -> 8.56 us
  other arithmetic: 53 us -> 8.77 us
  Pallas kernels: 0 us -> 28.2 us
  matrix products: 64.2 us -> 40 us
  starting transfers between devices: 15.9 us -> 38.7 us
    ppermute x12 -> x24, waiting for transfers between devices: 280 us -> 67.9 us  [the longest x9 66.7 us: next_chip(): return lax.ppermute(value, 'kv', pairs)]
    all_gather x4 -> x5, waiting for transfers between devices: 0.07 us -> 108 us  [the longest x3 61.6 us: gather_requests(): return lax.all_gather(value, 'req', axis=0, tiled=True)]
    reduce_scatter x2 -> x0, waiting for transfers between devices: 50.7 us -> none  [the longest x1 38.3 us: on_device(): lax.psum_scatter(units.astype(jnp.bfloat16), 'req', scatter_dimension=0,...]
    unnamed x30 -> x42, local copies, waits for them, and re-layouts: 38.7 us -> 5.8 us
    pallas_call x0 -> x4, Pallas kernels: none -> 28.2 us  [attend(): pl.pallas_call(attend_kernel, grid_spec=pltpu.PrefetchScalarGridSpec(num_...]
    ppermute x12 -> x24, starting transfers between devices: 12 us -> 38.5 us  [the longest x14 26.5 us: swap_cores(): return lax.ppermute(value, 'kv', pairs)]
    dot_general x6 -> x18, matrix products: 64.2 us -> 40 us  [the longest x2 18.2 us: hidden_of(): lax.dot_general(rows, up_rows, (((1,), (1,)), ((), ())), preferred_elemen...]
    dynamic_update_slice x6 -> x0, local copies, waits for them, and re-layouts: 20.4 us -> none  [on_device(): partial_sums = lax.map(one_block, (query_blocks, block_starts))]
  transfers between devices with their start and end apart: 19 -> 29, of which waited for: 11 -> 13; matrix products, arithmetic and copies ran while one was open for 33% -> 15% of each run, Pallas kernels for 0% -> 9%
where the time goes in v1:
time: 316 us; the launch traced here: 315 us
  waiting for transfers between devices  177 us (56%)
  matrix products  40 us (13%)
  starting transfers between devices  38.7 us (12%)
  Pallas kernels  28.2 us (9%)
  between operations  13.8 us (4%)
  other arithmetic  8.77 us (3%)
  local copies, waits for them, and re-layouts  8.56 us (3%)
    ppermute x9, waiting for transfers between devices, next_chip(): return lax.ppermute(value, 'kv', pairs)  66.7 us
    all_gather x3, waiting for transfers between devices, gather_requests(): return lax.all_gather(value, 'req', axis=0, tiled=True)  61.6 us
    all_gather x2, waiting for transfers between devices, gather_chips(): lax.all_gather(value, 'kv', axis=0, tiled=True, axis_index_groups=groups)  46.3 us
    pallas_call x4, Pallas kernels, attend(): pl.pallas_call(attend_kernel, grid_spec=pltpu.PrefetchScalarGridSpec(num_...  28.2 us
    ppermute x14, starting transfers between devices, swap_cores(): return lax.ppermute(value, 'kv', pairs)  26.5 us
    dot_general x2, matrix products, hidden_of(): lax.dot_general(rows, up_rows, (((1,), (1,)), ((), ())), preferred_elemen...  18.2 us
    dot_general x8, matrix products, share(): return branch + jnp.dot(units, down_rows, preferred_element_type=F32)  15.8 us
    ppermute x9, starting transfers between devices, next_chip(): return lax.ppermute(value, 'kv', pairs)  11.3 us
  transfers between devices with their start and end apart: 29, of which 13 were waited for; matrix products, arithmetic and copies ran while one was open for 15% of the time, Pallas kernels for 9%

profile of v1, /device:TPU:0, one launch (start us, length us, event | category | flops | bytes accessed | tf_op | source)
XLA Modules:
  0.0 315.0 jit_solution(2180611722975336001)
XLA Ops:
  6.5 2.0 slice.59
  11.3 46.3 %all-gather.6.cloned.1.call-done.q_mine = bf16[512,2048]{1,0:T(8,128)(2,1)} async-done(((bf16[128,2048]{1,0:T(8,128)(2,1)}), bf16[512,2048]{1,0:T(8,128)(2,1)}) %all-gather.6.cloned.1.call-update) | async-done | bytes 2097168 | tf_op jit(solution)/shard_map/all_gather | solution.py:39
  60.7 1.4 fusion.55.bias
  63.6 2.5 copy-done.2
  66.0 1.7 copy-done.4
  67.7 6.9 %shard_map.91 = (bf16[2,256,1024]{2,1,0:T(8,128)(2,1)S(1)}, f32[2,1,1024]{2,1,0:T(1,128)S(1)}) custom-call(s32[4]{0:T(128)S(1)} %get-tuple-element.44.meta, bf16[512,2048]{1,0:T(8,128)(2,1)S(1)} %copy-done.4, bf16[512,2048]{1,0:T(8,128)(2,1)} %collective-permute-done.q_other, bf16[1024,2048]{1,0:T(8,128)(2,1)S(1)} %copy-done.2, bf16[1024,2048]{1,0:T(8,128)(2,1)} %value.7, ...), custom_call_target="tpu_custom_call" | custom-call | flops 2415919104 | bytes 8388608 | tf_op jit(solution)/shard_map/pallas_call | solution.py:113
  74.6 24.1 %collective-permute-start.1 = (f32[1,1024]{1,0:T(1,128)S(1)}, f32[1,1024]{1,0:T(1,128)S(1)}, u32[]{:S(2)}, u32[]{:S(2)}) collective-permute-start(f32[1,1024]{1,0:T(1,128)S(1)} %slice_bitcast_fusion.7), channel_id=1, source_target_pairs={{0,1},{1,0},{2,3},{3,2},{4,5},{5,4},{6,7},{7,6},{8,9},{9,8},{10,11... | collective-permute-start | bytes 12296 | tf_op jit(solution)/shard_map/ppermute | solution.py:22
  98.7 6.9 %shard_map.92 = (bf16[2,256,1024]{2,1,0:T(8,128)(2,1)S(1)}, f32[2,1,1024]{2,1,0:T(1,128)S(1)}) custom-call(s32[4]{0:T(128)S(1)} %get-tuple-element.45.meta, bf16[512,2048]{1,0:T(8,128)(2,1)S(1)} %copy-done.4, bf16[512,2048]{1,0:T(8,128)(2,1)} %collective-permute-done.q_other, bf16[1024,2048]{1,0:T(8,128)(2,1)S(1)} %copy-done.2, bf16[1024,2048]{1,0:T(8,128)(2,1)} %value.7, ...), custom_call_target="tpu_custom_call" | custom-call | flops 2415919104 | bytes 8388608 | tf_op jit(solution)/shard_map/pallas_call | solution.py:113
  105.7 7.5 %shard_map.93 = (bf16[2,256,1024]{2,1,0:T(8,128)(2,1)S(1)}, f32[2,1,1024]{2,1,0:T(1,128)S(1)}) custom-call(s32[4]{0:T(128)S(1)} %get-tuple-element.46.meta, bf16[512,2048]{1,0:T(8,128)(2,1)S(1)} %copy-done.5, bf16[512,2048]{1,0:T(8,128)(2,1)} %collective-permute-done.q_other, bf16[1024,2048]{1,0:T(8,128)(2,1)S(1)} %copy-done.2, bf16[1024,2048]{1,0:T(8,128)(2,1)} %value.7, ...), custom_call_target="tpu_custom_call" | custom-call | flops 2415919104 | bytes 8388608 | tf_op jit(solution)/shard_map/pallas_call | solution.py:113
  113.5 6.9 %shard_map.94 = (bf16[2,256,1024]{2,1,0:T(8,128)(2,1)S(1)}, f32[2,1,1024]{2,1,0:T(1,128)S(1)}) custom-call(s32[4]{0:T(128)S(1)} %get-tuple-element.47.meta, bf16[512,2048]{1,0:T(8,128)(2,1)S(1)} %copy-done.5, bf16[512,2048]{1,0:T(8,128)(2,1)} %collective-permute-done.q_other, bf16[1024,2048]{1,0:T(8,128)(2,1)S(1)} %copy-done.3, bf16[1024,2048]{1,0:T(8,128)(2,1)} %value.7, ...), custom_call_target="tpu_custom_call" | custom-call | flops 2415919104 | bytes 8388608 | tf_op jit(solution)/shard_map/pallas_call | solution.py:113
  121.7 6.5 %collective-permute-start.5 = (f32[1,1024]{1,0:T(1,128)S(1)}, f32[1,1024]{1,0:T(1,128)S(1)}, u32[]{:S(2)}, u32[]{:S(2)}) collective-permute-start(f32[1,1024]{1,0:T(1,128)S(1)} %get-tuple-element.33), channel_id=1, source_target_pairs={{0,2},{1,3},{2,4},{3,5},{4,6},{5,7},{6,0},{7,1},{8,10},{9,11},{10,... | collective-permute-start | bytes 12296 | tf_op jit(solution)/shard_map/ppermute | solution.py:29
  129.5 2.3 collective-permute-start.6
  132.0 3.0 collective-permute-done.6
  136.2 4.4 %collective-permute-done.7 = f32[1,1024]{1,0:T(1,128)S(1)} collective-permute-done((f32[1,1024]{1,0:T(1,128)S(1)}, f32[1,1024]{1,0:T(1,128)S(1)}, u32[]{:S(2)}, u32[]{:S(2)}) %collective-permute-start.7) | collective-permute-done | bytes 4128 | tf_op jit(solution)/shard_map/ppermute | solution.py:29
  140.7 9.5 %collective-permute-done.12 = bf16[256,1024]{1,0:T(8,128)(2,1)S(1)} collective-permute-done((bf16[256,1024]{1,0:T(8,128)(2,1)S(1)}, bf16[256,1024]{1,0:T(8,128)(2,1)S(1)}, u32[]{:S(2)}, u32[]{:S(2)}) %collective-permute-start.12) | collective-permute-done | bytes 524320 | tf_op jit(solution)/shard_map/ppermute | solution.py:29
  151.4 16.9 %all-gather.12.cloned.1.call-done = bf16[1024,2048]{1,0:T(8,128)(2,1)} async-done(((bf16[256,2048]{1,0:T(8,128)(2,1)}), bf16[1024,2048]{1,0:T(8,128)(2,1)}) %all-gather.12.cloned.1.call-update) | async-done | bytes 4194320 | tf_op jit(solution)/shard_map/all_gather | solution.py:47
  168.3 9.8 %fusion.18 = bf16[512,1024]{1,0:T(8,128)(2,1)} fusion(bf16[512,2048]{1,0:T(8,128)(2,1)} %all-gather.10.cloned.1.call-done, bf16[1024,2048]{1,0:T(8,128)(2,1)} %all-gather.12.cloned.1.call-done), kind=kOutput, calls=%fused_computation.28 | convolution fusion | flops 2181562368 | bytes 7340032 | tf_op jit(solution)/shard_map/dot_general | solution.py:213
  178.2 44.6 %all-gather.14.cloned.1.call-done = bf16[1024,2048]{1,0:T(8,128)(2,1)} async-done(((bf16[256,2048]{1,0:T(8,128)(2,1)}), bf16[1024,2048]{1,0:T(8,128)(2,1)}) %all-gather.14.cloned.1.call-update) | async-done | bytes 4194320 | tf_op jit(solution)/shard_map/all_gather | solution.py:47
  222.8 4.1 %fusion.58 = f32[128,2048]{1,0:T(8,128)} fusion(bf16[1024,2048]{1,0:T(8,128)(2,1)} %all-gather.14.cloned.1.call-done, bf16[512,1024]{1,0:T(8,128)(2,1)} %fusion.18, s32[]{:T(128)S(6)} %select_n.109), kind=kOutput, calls=%fused_computation.95 | convolution fusion | flops 536870912 | bytes 5505028 | tf_op jit(solution)/shard_map/dot_general | solution.py:231
  226.9 1.6 fusion.48
  228.6 1.5 collective-permute-start.14
  230.1 1.7 fusion.62
  231.9 1.7 fusion.66
  233.6 10.5 %collective-permute-done.14 = bf16[256,1024]{1,0:T(8,128)(2,1)S(1)} collective-permute-done((bf16[256,1024]{1,0:T(8,128)(2,1)S(1)}, bf16[256,1024]{1,0:T(8,128)(2,1)S(1)}, u32[]{:S(2)}, u32[]{:S(2)}) %collective-permute-start.14) | collective-permute-done | bytes 524320 | tf_op jit(solution)/shard_map/ppermute | solution.py:29
  244.1 1.4 fusion.51
  245.5 8.4 %fusion.21 = bf16[512,1024]{1,0:T(8,128)(2,1)S(1)} fusion(bf16[512,2048]{1,0:T(8,128)(2,1)} %collective-permute-done.16, bf16[1024,2048]{1,0:T(8,128)(2,1)S(1)} %copy-done.19), kind=kOutput, calls=%fused_computation.31 | convolution fusion | flops 2181562368 | bytes 7340032 | tf_op jit(solution)/shard_map/dot_general | solution.py:213
  254.7 1.6 fusion.15
  256.4 3.0 fusion.60
  263.2 13.2 %collective-permute-done.21 = bf16[128,2048]{1,0:T(8,128)(2,1)S(1)} collective-permute-done((bf16[128,2048]{1,0:T(8,128)(2,1)S(1)}, bf16[128,2048]{1,0:T(8,128)(2,1)S(1)}, u32[]{:S(2)}, u32[]{:S(2)}) %collective-permute-start.21) | collective-permute-done | bytes 524320 | tf_op jit(solution)/shard_map/ppermute | solution.py:29
  278.1 13.7 %collective-permute-done.22 = bf16[128,2048]{1,0:T(8,128)(2,1)S(1)} collective-permute-done((bf16[128,2048]{1,0:T(8,128)(2,1)S(1)}, bf16[128,2048]{1,0:T(8,128)(2,1)S(1)}, u32[]{:S(2)}, u32[]{:S(2)}) %collective-permute-start.22) | collective-permute-done | bytes 524320 | tf_op jit(solution)/shard_map/ppermute | solution.py:29
  293.0 3.0 fusion.70
  296.1 11.1 %collective-permute-done.23 = bf16[128,2048]{1,0:T(8,128)(2,1)S(1)} collective-permute-done((bf16[128,2048]{1,0:T(8,128)(2,1)}, bf16[128,2048]{1,0:T(8,128)(2,1)S(1)}, u32[]{:S(2)}, u32[]{:S(2)}) %collective-permute-start.23) | collective-permute-done | bytes 524320 | tf_op jit(solution)/shard_map/ppermute | solution.py:29
  (125 shorter events, 21.3 us)
Async XLA Ops:
  6.5 53.4 %copy-start = (s32[4,2]{0,1:T(2,128)S(1)}, s32[4,2]{0,1:T(2,128)}, u32[]{:S(2)}) copy-start(s32[4,2]{0,1:T(2,128)} %param.13) | copy-start | bytes 100
  6.5 51.1 %all-gather.6.cloned.1.call-start = ((), (), s32[]{:S(2)}) async-start(), calls=%async_computation | async-start | bytes 2621440 | tf_op jit(solution)/shard_map/all_gather | solution.py:39
  8.5 142.8 %all-gather.10.cloned.1.call-start = ((), (), s32[]{:S(2)}) async-start(), calls=%async_computation.2 | async-start | bytes 2621440 | tf_op jit(solution)/shard_map/all_gather | solution.py:39
  9.8 49.3 %copy-start.20 = (bf16[64,2048]{1,0:T(8,128)(2,1)S(1)}, bf16[64,2048]{1,0:T(8,128)(2,1)}, u32[]{:S(2)}) copy-start(bf16[64,2048]{1,0:T(8,128)(2,1)} %param.15) | copy-start | bytes 786436
  11.3 52.3 %copy-start.1 = (bf16[128,6144]{1,0:T(8,128)(2,1)S(1)}, bf16[128,6144]{1,0:T(8,128)(2,1)}, u32[]{:S(2)}) copy-start(bf16[128,6144]{1,0:T(8,128)(2,1)} %new_value.7) | copy-start | bytes 4718596
  57.6 110.7 %all-gather.12.cloned.1.call-start = ((), (), s32[]{:S(2)}) async-start(), calls=%async_computation.3 | async-start | bytes 5242880 | tf_op jit(solution)/shard_map/all_gather | solution.py:47
  58.4 164.4 %all-gather.14.cloned.1.call-start = ((), (), s32[]{:S(2)}) async-start(), calls=%async_computation.4 | async-start | bytes 5242880 | tf_op jit(solution)/shard_map/all_gather | solution.py:47
  58.9 195.7 %all-gather.8.cloned.1.call-start = ((), (), s32[]{:S(2)}) async-start(), calls=%async_computation.1 | async-start | bytes 1310720 | tf_op jit(solution)/shard_map/all_gather | solution.py:47
  59.0 4.6 %collective-permute-start = (bf16[512,2048]{1,0:T(8,128)(2,1)}, bf16[512,2048]{1,0:T(8,128)(2,1)}, u32[]{:S(2)}, u32[]{:S(2)}) collective-permute-start(bf16[512,2048]{1,0:T(8,128)(2,1)} %all-gather.6.cloned.1.call-done.q_mine), channel_id=1, source_target_pairs={{0,1},{1,0},{2,3},{3,2},{4,5},{5,4},{6,7},{7,6},{8,9},{9,8},{10,11... | collective-permute-start | bytes 6291464 | tf_op jit(solution)/shard_map/ppermute | solution.py:22
  59.1 3.0 collective-permute-start.15
  74.6 61.5 %collective-permute-start.1 = (f32[1,1024]{1,0:T(1,128)S(1)}, f32[1,1024]{1,0:T(1,128)S(1)}, u32[]{:S(2)}, u32[]{:S(2)}) collective-permute-start(f32[1,1024]{1,0:T(1,128)S(1)} %slice_bitcast_fusion.7), channel_id=1, source_target_pairs={{0,1},{1,0},{2,3},{3,2},{4,5},{5,4},{6,7},{7,6},{8,9},{9,8},{10,11... | collective-permute-start | bytes 12296 | tf_op jit(solution)/shard_map/ppermute | solution.py:22
  105.6 26.3 %collective-permute-start.2 = (f32[1,1024]{1,0:T(1,128)S(1)}, f32[1,1024]{1,0:T(1,128)S(1)}, u32[]{:S(2)}, u32[]{:S(2)}) collective-permute-start(f32[1,1024]{1,0:T(1,128)S(1)} %slice_bitcast_fusion.6), channel_id=1, source_target_pairs={{0,1},{1,0},{2,3},{3,2},{4,5},{5,4},{6,7},{7,6},{8,9},{9,8},{10,11... | collective-permute-start | bytes 12296 | tf_op jit(solution)/shard_map/ppermute | solution.py:22
  113.2 15.0 %collective-permute-start.3 = (f32[1,1024]{1,0:T(1,128)S(1)}, f32[1,1024]{1,0:T(1,128)S(1)}, u32[]{:S(2)}, u32[]{:S(2)}) collective-permute-start(f32[1,1024]{1,0:T(1,128)S(1)} %slice_bitcast_fusion.5), channel_id=1, source_target_pairs={{0,1},{1,0},{2,3},{3,2},{4,5},{5,4},{6,7},{7,6},{8,9},{9,8},{10,11... | collective-permute-start | bytes 12296 | tf_op jit(solution)/shard_map/ppermute | solution.py:22
  120.4 1.2 collective-permute-start.4
  120.8 112.8 %collective-permute-start.8 = (bf16[256,1024]{1,0:T(8,128)(2,1)S(1)}, bf16[256,1024]{1,0:T(8,128)(2,1)}, u32[]{:S(2)}, u32[]{:S(2)}) collective-permute-start(bf16[256,1024]{1,0:T(8,128)(2,1)S(1)} %slice_bitcast_fusion.3), channel_id=1, source_target_pairs={{0,1},{1,0},{2,3},{3,2},{4,5},{5,4},{6,7},{7,6},{8,9},{9,8},{10,11... | collective-permute-start | bytes 1572872 | tf_op jit(solution)/shard_map/ppermute | solution.py:22
  121.7 7.9 %collective-permute-start.5 = (f32[1,1024]{1,0:T(1,128)S(1)}, f32[1,1024]{1,0:T(1,128)S(1)}, u32[]{:S(2)}, u32[]{:S(2)}) collective-permute-start(f32[1,1024]{1,0:T(1,128)S(1)} %get-tuple-element.33), channel_id=1, source_target_pairs={{0,2},{1,3},{2,4},{3,5},{4,6},{5,7},{6,0},{7,1},{8,10},{9,11},{10,... | collective-permute-start | bytes 12296 | tf_op jit(solution)/shard_map/ppermute | solution.py:29
  128.2 7.3 %collective-permute-start.11 = (bf16[256,1024]{1,0:T(8,128)(2,1)S(1)}, bf16[256,1024]{1,0:T(8,128)(2,1)S(1)}, u32[]{:S(2)}, u32[]{:S(2)}) collective-permute-start(bf16[256,1024]{1,0:T(8,128)(2,1)S(1)} %slice_bitcast_fusion), channel_id=1, source_target_pairs={{0,1},{1,0},{2,3},{3,2},{4,5},{5,4},{6,7},{7,6},{8,9},{9,8},{10,11... | collective-permute-start | bytes 1572872 | tf_op jit(solution)/shard_map/ppermute | solution.py:22
  129.5 5.5 %collective-permute-start.6 = (f32[1,1024]{1,0:T(1,128)S(1)}, f32[1,1024]{1,0:T(1,128)S(1)}, u32[]{:S(2)}, u32[]{:S(2)}) collective-permute-start(f32[1,1024]{1,0:T(1,128)S(1)} %get-tuple-element.28), channel_id=1, source_target_pairs={{0,2},{1,3},{2,4},{3,5},{4,6},{5,7},{6,0},{7,1},{8,10},{9,11},{10,... | collective-permute-start | bytes 12296 | tf_op jit(solution)/shard_map/ppermute | solution.py:29
  131.9 8.8 %collective-permute-start.10 = (bf16[256,1024]{1,0:T(8,128)(2,1)S(1)}, bf16[256,1024]{1,0:T(8,128)(2,1)S(1)}, u32[]{:S(2)}, u32[]{:S(2)}) collective-permute-start(bf16[256,1024]{1,0:T(8,128)(2,1)S(1)} %slice_bitcast_fusion.1), channel_id=1, source_target_pairs={{0,1},{1,0},{2,3},{3,2},{4,5},{5,4},{6,7},{7,6},{8,9},{9,8},{10,11... | collective-permute-start | bytes 1572872 | tf_op jit(solution)/shard_map/ppermute | solution.py:22
  135.0 5.6 %collective-permute-start.7 = (f32[1,1024]{1,0:T(1,128)S(1)}, f32[1,1024]{1,0:T(1,128)S(1)}, u32[]{:S(2)}, u32[]{:S(2)}) collective-permute-start(f32[1,1024]{1,0:T(1,128)S(1)} %get-tuple-element.25), channel_id=1, source_target_pairs={{0,2},{1,3},{2,4},{3,5},{4,6},{5,7},{6,0},{7,1},{8,10},{9,11},{10,... | collective-permute-start | bytes 12296 | tf_op jit(solution)/shard_map/ppermute | solution.py:29
  135.8 14.4 %collective-permute-start.12 = (bf16[256,1024]{1,0:T(8,128)(2,1)S(1)}, bf16[256,1024]{1,0:T(8,128)(2,1)S(1)}, u32[]{:S(2)}, u32[]{:S(2)}) collective-permute-start(bf16[256,1024]{1,0:T(8,128)(2,1)S(1)} %fusion.42), channel_id=1, source_target_pairs={{0,2},{1,3},{2,4},{3,5},{4,6},{5,7},{6,0},{7,1},{8,10},{9,11},{10,... | collective-permute-start | bytes 1572872 | tf_op jit(solution)/shard_map/ppermute | solution.py:29
  136.1 90.8 %collective-permute-start.9 = (bf16[256,1024]{1,0:T(8,128)(2,1)S(1)}, bf16[256,1024]{1,0:T(8,128)(2,1)}, u32[]{:S(2)}, u32[]{:S(2)}) collective-permute-start(bf16[256,1024]{1,0:T(8,128)(2,1)S(1)} %slice_bitcast_fusion.2), channel_id=1, source_target_pairs={{0,1},{1,0},{2,3},{3,2},{4,5},{5,4},{6,7},{7,6},{8,9},{9,8},{10,11... | collective-permute-start | bytes 1572872 | tf_op jit(solution)/shard_map/ppermute | solution.py:22
  151.4 75.6 %collective-permute-start.13 = (bf16[256,1024]{1,0:T(8,128)(2,1)}, bf16[256,1024]{1,0:T(8,128)(2,1)}, u32[]{:S(2)}, u32[]{:S(2)}) collective-permute-start(bf16[256,1024]{1,0:T(8,128)(2,1)} %fusion.45), channel_id=1, source_target_pairs={{0,2},{1,3},{2,4},{3,5},{4,6},{5,7},{6,0},{7,1},{8,10},{9,11},{10,... | collective-permute-start | bytes 1572872 | tf_op jit(solution)/shard_map/ppermute | solution.py:29
  151.4 94.1 %collective-permute-start.16 = (bf16[512,2048]{1,0:T(8,128)(2,1)}, bf16[512,2048]{1,0:T(8,128)(2,1)}, u32[]{:S(2)}, u32[]{:S(2)}) collective-permute-start(bf16[512,2048]{1,0:T(8,128)(2,1)} %all-gather.10.cloned.1.call-done), channel_id=1, source_target_pairs={{0,1},{1,0},{2,3},{3,2},{4,5},{5,4},{6,7},{7,6},{8,9},{9,8},{10,11... | collective-permute-start | bytes 6291464 | tf_op jit(solution)/shard_map/ppermute | solution.py:22
  228.6 15.5 %collective-permute-start.14 = (bf16[256,1024]{1,0:T(8,128)(2,1)S(1)}, bf16[256,1024]{1,0:T(8,128)(2,1)S(1)}, u32[]{:S(2)}, u32[]{:S(2)}) collective-permute-start(bf16[256,1024]{1,0:T(8,128)(2,1)S(1)} %fusion.48), channel_id=1, source_target_pairs={{0,2},{1,3},{2,4},{3,5},{4,6},{5,7},{6,0},{7,1},{8,10},{9,11},{10,... | collective-permute-start | bytes 1572872 | tf_op jit(solution)/shard_map/ppermute | solution.py:29
  256.3 4.0 %collective-permute-start.20 = (bf16[128,2048]{1,0:T(8,128)(2,1)S(1)}, bf16[128,2048]{1,0:T(8,128)(2,1)S(1)}, u32[]{:S(2)}, u32[]{:S(2)}) collective-permute-start(bf16[128,2048]{1,0:T(8,128)(2,1)S(1)} %fusion.15), channel_id=1, source_target_pairs={{0,1},{1,0},{2,3},{3,2},{4,5},{5,4},{6,7},{7,6},{8,9},{9,8},{10,11... | collective-permute-start | bytes 1572872 | tf_op jit(solution)/shard_map/ppermute | solution.py:22
  259.8 3.4 %collective-permute-start.19 = (bf16[128,2048]{1,0:T(8,128)(2,1)S(1)}, bf16[128,2048]{1,0:T(8,128)(2,1)S(1)}, u32[]{:S(2)}, u32[]{:S(2)}) collective-permute-start(bf16[128,2048]{1,0:T(8,128)(2,1)S(1)} %fusion.13), channel_id=1, source_target_pairs={{0,1},{1,0},{2,3},{3,2},{4,5},{5,4},{6,7},{7,6},{8,9},{9,8},{10,11... | collective-permute-start | bytes 1572872 | tf_op jit(solution)/shard_map/ppermute | solution.py:22
  260.7 15.8 %collective-permute-start.21 = (bf16[128,2048]{1,0:T(8,128)(2,1)S(1)}, bf16[128,2048]{1,0:T(8,128)(2,1)S(1)}, u32[]{:S(2)}, u32[]{:S(2)}) collective-permute-start(bf16[128,2048]{1,0:T(8,128)(2,1)S(1)} %fusion.14), channel_id=1, source_target_pairs={{0,2},{1,3},{2,4},{3,5},{4,6},{5,7},{6,0},{7,1},{8,10},{9,11},{10,... | collective-permute-start | bytes 1572872 | tf_op jit(solution)/shard_map/ppermute | solution.py:29
  262.7 15.4 %collective-permute-start.18 = (bf16[128,2048]{1,0:T(8,128)(2,1)S(1)}, bf16[128,2048]{1,0:T(8,128)(2,1)S(1)}, u32[]{:S(2)}, u32[]{:S(2)}) collective-permute-start(bf16[128,2048]{1,0:T(8,128)(2,1)S(1)} %fusion.11), channel_id=1, source_target_pairs={{0,1},{1,0},{2,3},{3,2},{4,5},{5,4},{6,7},{7,6},{8,9},{9,8},{10,11... | collective-permute-start | bytes 1572872 | tf_op jit(solution)/shard_map/ppermute | solution.py:22
  276.9 14.9 %collective-permute-start.22 = (bf16[128,2048]{1,0:T(8,128)(2,1)S(1)}, bf16[128,2048]{1,0:T(8,128)(2,1)S(1)}, u32[]{:S(2)}, u32[]{:S(2)}) collective-permute-start(bf16[128,2048]{1,0:T(8,128)(2,1)S(1)} %fusion.12), channel_id=1, source_target_pairs={{0,2},{1,3},{2,4},{3,5},{4,6},{5,7},{6,0},{7,1},{8,10},{9,11},{10,... | collective-permute-start | bytes 1572872 | tf_op jit(solution)/shard_map/ppermute | solution.py:29
  278.0 18.1 %collective-permute-start.17 = (bf16[128,2048]{1,0:T(8,128)(2,1)S(1)}, bf16[128,2048]{1,0:T(8,128)(2,1)S(1)}, u32[]{:S(2)}, u32[]{:S(2)}) collective-permute-start(bf16[128,2048]{1,0:T(8,128)(2,1)S(1)} %fusion.9), channel_id=1, source_target_pairs={{0,1},{1,0},{2,3},{3,2},{4,5},{5,4},{6,7},{7,6},{8,9},{9,8},{10,11... | collective-permute-start | bytes 1572872 | tf_op jit(solution)/shard_map/ppermute | solution.py:22
  293.0 14.2 %collective-permute-start.23 = (bf16[128,2048]{1,0:T(8,128)(2,1)}, bf16[128,2048]{1,0:T(8,128)(2,1)S(1)}, u32[]{:S(2)}, u32[]{:S(2)}) collective-permute-start(bf16[128,2048]{1,0:T(8,128)(2,1)} %fusion.10), channel_id=1, source_target_pairs={{0,2},{1,3},{2,4},{3,5},{4,6},{5,7},{6,0},{7,1},{8,10},{9,11},{10,... | collective-permute-start | bytes 1572872 | tf_op jit(solution)/shard_map/ppermute | solution.py:29
  (18 other events, 166.5 us)
Sparse Core Ops, SparseCore 0:
  8.9 48.6 all-gather.5
  59.2 57.1 all-gather.9
  118.2 50.0 all-gather.11
  170.0 52.7 all-gather.13
  224.5 26.6 all-gather.7

commit v2 on v1

v2 whole, which is shorter than its diff:
```python
import jax
import jax.numpy as jnp
from jax import lax
from jax.experimental import pallas as pl
from jax.experimental.pallas import tpu as pltpu
from jax.sharding import PartitionSpec as P

HD = 256
SPAN = 8
CORES = 2
CHIPS = SPAN // CORES
LOWEST = -1e29
NEG_FILL = -1e30
NORM_EPS = 1e-05
F32 = jnp.float32
BF16 = jnp.bfloat16


def swap_cores(value):
    pairs = [(k, k ^ 1) for k in range(lax.axis_size("kv"))]
    return lax.ppermute(value, "kv", pairs)


def next_chip(value):
    pairs = [
        (k, k - k % SPAN + (k % SPAN + CORES) % SPAN) for k in range(lax.axis_size("kv"))
    ]
    return lax.ppermute(value, "kv", pairs)


def gather_ring(value):
    pieces = [value]
    for _ in range(CHIPS - 1):
        pieces.append(next_chip(pieces[-1]))
    return pieces, [swap_cores(piece) for piece in pieces]


def gather_requests(value, low_first):
    device_count = lax.axis_size("kv") * lax.axis_size("req")
    bits = range((device_count // SPAN).bit_length() - 1)
    pieces = {0: value}
    for bit in bits if low_first else reversed(bits):
        pairs = [(d, d ^ (SPAN << bit)) for d in range(device_count)]
        for index in list(pieces):
            pieces[index | 1 << bit] = lax.ppermute(pieces[index], ("req", "kv"), pairs)
    return [pieces[index] for index in range(len(pieces))]


def gather_in_order(value):
    size = lax.axis_size("kv")
    if size > SPAN:
        groups = [list(range(m, size, SPAN)) for m in range(SPAN)]
        value = lax.all_gather(value, "kv", axis=0, tiled=True, axis_index_groups=groups)
    return lax.all_gather(value, "req", axis=0, tiled=True)


def layer_norm(stream, norm_gain):
    values = stream.astype(F32)
    centred = values - jnp.mean(values, axis=-1, keepdims=True)
    spread = jnp.mean(centred * centred, axis=-1, keepdims=True)
    return (centred * lax.rsqrt(spread + NORM_EPS) * norm_gain).astype(BF16)


def attend_kernel(meta, *refs):
    pieces = refs[: 2 * CHIPS]
    key, value, new_key, new_value, bias, out, lse, value_t, new_value_t = refs[2 * CHIPS :]
    slot = pl.program_id(0)
    core = meta[2]
    member = meta[3]
    chip = member // CORES
    token_count = new_key.shape[0]
    half = CHIPS * token_count
    value_t[...] = value[...].T
    new_value_t[...] = new_value[...].T
    position = member * token_count + lax.broadcasted_iota(jnp.int32, (token_count, 1), 0)
    lane = lax.broadcasted_iota(jnp.int32, (1, token_count), 1)
    for first in (0, 1):
        source_core = core if first == 0 else 1 - core
        place = jnp.where(slot == 0, first, 1 - first) * half
        for pair in range(0, CHIPS, 2):
            steps = (pair, pair + 1)
            chips = [lax.rem(chip - step + CHIPS, CHIPS) for step in steps]
            queries = jnp.concatenate(
                [pieces[first * CHIPS + step][...] for step in steps], 0
            ) * BF16(HD**-0.5)
            scores = lax.dot_general(
                key[...], queries, (((1,), (1,)), ((), ())), preferred_element_type=F32
            )
            scores = scores + bias[...]
            fresh = lax.dot_general(
                new_key[...], queries, (((1,), (1,)), ((), ())), preferred_element_type=F32
            )
            token = jnp.concatenate(
                [(CORES * place_z + source_core) * token_count + lane for place_z in chips], 1
            )
            fresh = jnp.where(position <= token, fresh, NEG_FILL)
            largest = jnp.maximum(
                jnp.max(scores, axis=0, keepdims=True), jnp.max(fresh, axis=0, keepdims=True)
            )
            largest = jnp.maximum(largest, LOWEST)
            weights = jnp.exp(scores - largest)
            fresh = jnp.exp(fresh - largest)
            total = jnp.sum(weights, axis=0, keepdims=True) + jnp.sum(
                fresh, axis=0, keepdims=True
            )
            total = jnp.maximum(total, 1.0)
            sums = jnp.dot(
                value_t[...], weights.astype(BF16), preferred_element_type=F32
            ) + jnp.dot(new_value_t[...], fresh.astype(BF16), preferred_element_type=F32)
            sums = (sums / total).astype(BF16)
            logs = largest + jnp.log(total)
            for step, place_z in enumerate(chips):
                lanes = pl.ds(
                    pl.multiple_of(place + place_z * token_count, token_count), token_count
                )
                held = slice(step * token_count, (step + 1) * token_count)
                out[0, :, lanes] = sums[:, held]
                lse[0, :, lanes] = logs[:, held]


def attend(meta, pieces, key_cache, value_cache, projections, bias):
    token_count = projections.shape[0]
    new_total = len(pieces) * token_count
    cache_rows = key_cache.shape[0]
    heads = key_cache.shape[1] // HD
    q_spec = pl.BlockSpec((token_count, HD), lambda i, meta: (0, meta[i]))
    cache_spec = pl.BlockSpec((cache_rows, HD), lambda i, meta: (0, meta[i]))
    flops = 2 * 2 * CORES * new_total * (cache_rows + token_count) * HD
    return pl.pallas_call(
        attend_kernel,
        grid_spec=pltpu.PrefetchScalarGridSpec(
            num_scalar_prefetch=1,
            grid=(CORES,),
            in_specs=[q_spec] * len(pieces)
            + [
                cache_spec,
                cache_spec,
                pl.BlockSpec((token_count, HD), lambda i, meta: (0, heads + meta[i])),
                pl.BlockSpec((token_count, HD), lambda i, meta: (0, 2 * heads + meta[i])),
                pl.BlockSpec((cache_rows, 1), lambda i, meta: (0, 0)),
            ],
            out_specs=[
                pl.BlockSpec((1, HD, new_total), lambda i, meta: (i, 0, 0)),
                pl.BlockSpec((1, 1, new_total), lambda i, meta: (i, 0, 0)),
            ],
            scratch_shapes=[
                pltpu.VMEM((HD, cache_rows), BF16),
                pltpu.VMEM((HD, token_count), BF16),
            ],
        ),
        out_shape=[
            jax.ShapeDtypeStruct((CORES, HD, new_total), BF16),
            jax.ShapeDtypeStruct((CORES, 1, new_total), F32),
        ],
        compiler_params=pltpu.CompilerParams(vmem_limit_bytes=40 * 2**20),
        cost_estimate=pl.CostEstimate(
            flops=flops, bytes_accessed=8 * 2**20, transcendentals=flops // (4 * HD)
        ),
    )(meta, *pieces, key_cache, value_cache, projections, projections, bias)


def merge(parts):
    largest = parts[0][1]
    for part in parts[1:]:
        largest = jnp.maximum(largest, part[1])
    shares = [jnp.exp(part[1] - largest) for part in parts]
    total = sum(shares)
    joined = sum(part[0].astype(F32) * (share / total) for part, share in zip(parts, shares))
    return joined.astype(BF16), largest + jnp.log(total)


def on_device(
    stream,
    projections,
    key_cache,
    value_cache,
    cache_range,
    norm_gain,
    out_weight,
    up_weight,
    down_weight,
):
    token_count, width = stream.shape
    cache_rows = key_cache.shape[0]
    kv_count = lax.axis_size("kv")
    device_count = kv_count * lax.axis_size("req")
    request_count = device_count // SPAN
    kv_place = lax.axis_index("kv")
    member = kv_place % SPAN
    core = member % CORES
    chip = member // CORES
    request = (lax.axis_index("req") * kv_count + kv_place) // SPAN

    q_mine, q_other = gather_ring(projections[:, :width])
    up_rows = jnp.concatenate(gather_requests(up_weight, True), 0)
    down_rows = jnp.concatenate(gather_requests(down_weight, False), 0)
    head_pairs = [
        (d, (d % request_count) * SPAN + d // request_count) for d in range(device_count)
    ]
    out_rows = gather_in_order(lax.ppermute(out_weight, ("req", "kv"), head_pairs))

    bounds = lax.dynamic_slice_in_dim(cache_range, request, 1, 0)[0]
    positions = member * cache_rows + jnp.arange(cache_rows, dtype=jnp.int32)[:, None]
    bias = jnp.where((positions >= bounds[0]) & (positions < bounds[1]), 0.0, NEG_FILL)
    bias = bias.astype(F32)

    normed, _ = lax.optimization_barrier((layer_norm(stream, norm_gain), q_mine[-1]))
    rows_mine, rows_other = gather_ring(normed)

    carried = None
    for phase in range(CHIPS):
        target = (chip + CHIPS - 1 - phase) % CHIPS
        kept = CORES * target + core
        given = CORES * target + 1 - core
        meta = jnp.stack([kept, given, core, member]).astype(jnp.int32)
        out, lse = attend(meta, q_mine + q_other, key_cache, value_cache, projections, bias)
        parts = [(out[0], lse[0]), swap_cores((out[1], lse[1]))]
        if carried is not None:
            parts.append(carried)
        carried = merge(parts)
        if phase < CHIPS - 1:
            carried = next_chip(carried)
    attention = carried[0]

    gates = lax.dot_general(
        jnp.concatenate(rows_mine + rows_other, 0),
        up_rows,
        (((1,), (1,)), ((), ())),
        preferred_element_type=F32,
    )
    hidden = jax.nn.gelu(gates, approximate=False).astype(BF16)
    units = jnp.dot(hidden, down_rows, preferred_element_type=F32)
    half = CHIPS * token_count
    running = None
    for phase in range(CHIPS):
        step = (phase + 1) % CHIPS
        first = ((chip + CHIPS - step) % CHIPS) * token_count

        def share(offset):
            block = lax.dynamic_slice_in_dim(attention, offset + first, token_count, 1)
            branch = lax.dot_general(
                block, out_rows, (((0,), (0,)), ((), ())), preferred_element_type=F32
            )
            held = offset + step * token_count
            return branch + units[held : held + token_count]

        total = share(0) + swap_cores(share(half).astype(BF16)).astype(F32)
        if running is not None:
            total = total + running.astype(F32)
        running = total
        if phase < CHIPS - 1:
            running = next_chip(total.astype(BF16))
    return (stream.astype(F32) + running).astype(BF16)


def solution(mesh):
    rows = P(("req", "kv"), None)
    in_specs = (rows, rows, rows, rows, P(), P(), rows, rows, rows)
    return jax.shard_map(
        on_device, mesh=mesh, in_specs=in_specs, out_specs=rows, check_vma=False
    )
```

time: 316 us -> 299 us (0.946)
  starting transfers between devices: 38.7 us -> 24.5 us
  waiting for transfers between devices: 177 us -> 170 us
  matrix products: 40 us -> 45.1 us
    all_gather x5 -> x1, waiting for transfers between devices: 108 us -> 0.02 us  [gather_in_order(): return lax.all_gather(value, 'req', axis=0, tiled=True)]
    ppermute x9 -> x15, waiting for transfers between devices: 66.7 us -> 141 us  [next_chip(): return lax.ppermute(value, 'kv', pairs)]
    ppermute x0 -> x6, waiting for transfers between devices: none -> 27.8 us  [gather_requests(): pieces[index | 1 << bit] = lax.ppermute(pieces[index], ('req', 'kv'), pairs)]
    ppermute x14 -> x20, starting transfers between devices: 26.5 us -> 2.68 us  [swap_cores(): return lax.ppermute(value, 'kv', pairs)]
    ppermute x0 -> x6, starting transfers between devices: none -> 16.2 us  [gather_requests(): pieces[index | 1 << bit] = lax.ppermute(pieces[index], ('req', 'kv'), pairs)]
    dot_general x8, matrix products: 5.98 us -> 19.5 us  [share(): lax.dot_general(block, out_rows, (((0,), (0,)), ((), ())), preferred_elem...]
    dot_general x10 -> x1, matrix products: 34.1 us -> 25.6 us  [on_device(): units = jnp.dot(hidden, down_rows, preferred_element_type=F32)]
    ppermute x9 -> x15, starting transfers between devices: 11.3 us -> 4.09 us  [next_chip(): return lax.ppermute(value, 'kv', pairs)]
  transfers between devices with their start and end apart: 29 -> 43, of which waited for: 13 -> 16; matrix products, arithmetic and copies ran while one was open for 15% -> 17% of each run, Pallas kernels for 9% -> 10%
where the time goes in v2:
time: 299 us; the launch traced here: 298 us
  waiting for transfers between devices  170 us (57%)
  matrix products  45.1 us (15%)
  Pallas kernels  29.8 us (10%)
  starting transfers between devices  24.5 us (8%)
  between operations  14 us (5%)
  other arithmetic  7.59 us (3%)
  local copies, waits for them, and re-layouts  7.22 us (2%)
    ppermute x15, waiting for transfers between devices, next_chip(): return lax.ppermute(value, 'kv', pairs)  141 us
    pallas_call x4, Pallas kernels, attend(): pl.pallas_call(attend_kernel, grid_spec=pltpu.PrefetchScalarGridSpec(num_...  29.8 us
    ppermute x6, waiting for transfers between devices, gather_requests(): pieces[index | 1 << bit] = lax.ppermute(pieces[index], ('req', 'kv'), pairs)  27.8 us
    dot_general x1, matrix products, on_device(): units = jnp.dot(hidden, down_rows, preferred_element_type=F32)  25.6 us
    dot_general x8, matrix products, share(): lax.dot_general(block, out_rows, (((0,), (0,)), ((), ())), preferred_elem...  19.5 us
    ppermute x6, starting transfers between devices, gather_requests(): pieces[index | 1 << bit] = lax.ppermute(pieces[index], ('req', 'kv'), pairs)  16.2 us
  transfers between devices with their start and end apart: 43, of which 16 were waited for; matrix products, arithmetic and copies ran while one was open for 17% of the time, Pallas kernels for 10%

profile of v2, /device:TPU:0, one launch (start us, length us, event | category | flops | bytes accessed | tf_op | source)
XLA Modules:
  0.0 298.1 jit_solution(5177215798155100075)
XLA Ops:
  7.7 3.1 %collective-permute-start = (bf16[128,2048]{1,0:T(8,128)(2,1)S(1)}, bf16[128,2048]{1,0:T(8,128)(2,1)S(1)}, u32[]{:S(2)}, u32[]{:S(2)}) collective-permute-start(bf16[128,2048]{1,0:T(8,128)(2,1)S(1)} %slice.83.refs_0_), channel_id=1, source_target_pairs={{0,2},{1,3},{2,4},{3,5},{4,6},{5,7},{6,0},{7,1},{8,10},{9,11},{10,... | collective-permute-start | bytes 1572872 | tf_op jit(solution)/shard_map/ppermute | solution.py:28
  13.6 12.2 %collective-permute-done.refs_1_ = bf16[128,2048]{1,0:T(8,128)(2,1)S(1)} collective-permute-done((bf16[128,2048]{1,0:T(8,128)(2,1)S(1)}, bf16[128,2048]{1,0:T(8,128)(2,1)S(1)}, u32[]{:S(2)}, u32[]{:S(2)}) %collective-permute-start) | collective-permute-done | bytes 524320 | tf_op jit(solution)/shard_map/ppermute | solution.py:28
  27.2 14.7 %collective-permute-done.1.refs_2_ = bf16[128,2048]{1,0:T(8,128)(2,1)} collective-permute-done((bf16[128,2048]{1,0:T(8,128)(2,1)S(1)}, bf16[128,2048]{1,0:T(8,128)(2,1)}, u32[]{:S(2)}, u32[]{:S(2)}) %collective-permute-start.1) | collective-permute-done | bytes 524320 | tf_op jit(solution)/shard_map/ppermute | solution.py:28
  42.0 2.2 fusion.39
  44.7 12.5 %collective-permute-done.2.refs_3_ = bf16[128,2048]{1,0:T(8,128)(2,1)} collective-permute-done((bf16[128,2048]{1,0:T(8,128)(2,1)}, bf16[128,2048]{1,0:T(8,128)(2,1)}, u32[]{:S(2)}, u32[]{:S(2)}) %collective-permute-start.2) | collective-permute-done | bytes 524320 | tf_op jit(solution)/shard_map/ppermute | solution.py:28
  61.5 10.8 %collective-permute-start.33 = (bf16[256,2048]{1,0:T(8,128)(2,1)}, bf16[256,2048]{1,0:T(8,128)(2,1)}, u32[]{:S(2)}, u32[]{:S(2)}) collective-permute-start(bf16[256,2048]{1,0:T(8,128)(2,1)} %param.17), channel_id=1, source_target_pairs={{0,16},{1,17},{2,18},{3,19},{4,20},{5,21},{6,22},{7,23},{8,24},{9,... | collective-permute-start | bytes 3145736 | tf_op jit(solution)/shard_map/ppermute | solution.py:45
  72.4 2.2 copy-done.2
  74.6 7.4 %shard_map.91 = (bf16[2,256,1024]{2,1,0:T(8,128)(2,1)S(1)}, f32[2,1,1024]{2,1,0:T(1,128)S(1)}) custom-call(s32[4]{0:T(128)S(1)} %get-tuple-element.44.meta, bf16[128,2048]{1,0:T(8,128)(2,1)S(1)} %slice.83.refs_0_, bf16[128,2048]{1,0:T(8,128)(2,1)S(1)} %collective-permute-done.refs_1_, bf16[128,2048]{1,0:T(8,128)(2,1)} %collective-permute-done.1.refs_2_, ...), custom_call_target="tpu_custom_call" | custom-call | flops 2415919104 | bytes 8388608 | tf_op jit(solution)/shard_map/pallas_call | solution.py:129
  82.0 7.4 %shard_map.92 = (bf16[2,256,1024]{2,1,0:T(8,128)(2,1)S(1)}, f32[2,1,1024]{2,1,0:T(1,128)S(1)}) custom-call(s32[4]{0:T(128)S(1)} %get-tuple-element.45.meta, bf16[128,2048]{1,0:T(8,128)(2,1)S(1)} %slice.83.refs_0_, bf16[128,2048]{1,0:T(8,128)(2,1)S(1)} %collective-permute-done.refs_1_, bf16[128,2048]{1,0:T(8,128)(2,1)} %collective-permute-done.1.refs_2_, ...), custom_call_target="tpu_custom_call" | custom-call | flops 2415919104 | bytes 8388608 | tf_op jit(solution)/shard_map/pallas_call | solution.py:129
  89.5 7.7 %shard_map.93 = (bf16[2,256,1024]{2,1,0:T(8,128)(2,1)S(1)}, f32[2,1,1024]{2,1,0:T(1,128)S(1)}) custom-call(s32[4]{0:T(128)S(1)} %get-tuple-element.46.meta, bf16[128,2048]{1,0:T(8,128)(2,1)S(1)} %slice.83.refs_0_, bf16[128,2048]{1,0:T(8,128)(2,1)S(1)} %collective-permute-done.refs_1_, bf16[128,2048]{1,0:T(8,128)(2,1)} %collective-permute-done.1.refs_2_, ...), custom_call_target="tpu_custom_call" | custom-call | flops 2415919104 | bytes 8388608 | tf_op jit(solution)/shard_map/pallas_call | solution.py:129
  97.7 7.4 %shard_map.94 = (bf16[2,256,1024]{2,1,0:T(8,128)(2,1)S(1)}, f32[2,1,1024]{2,1,0:T(1,128)S(1)}) custom-call(s32[4]{0:T(128)S(1)} %get-tuple-element.47.meta, bf16[128,2048]{1,0:T(8,128)(2,1)S(1)} %slice.83.refs_0_, bf16[128,2048]{1,0:T(8,128)(2,1)S(1)} %collective-permute-done.refs_1_, bf16[128,2048]{1,0:T(8,128)(2,1)} %collective-permute-done.1.refs_2_, ...), custom_call_target="tpu_custom_call" | custom-call | flops 2415919104 | bytes 8388608 | tf_op jit(solution)/shard_map/pallas_call | solution.py:129
  107.1 4.8 %collective-permute-done.11 = f32[1,1024]{1,0:T(1,128)S(1)} collective-permute-done((f32[1,1024]{1,0:T(1,128)S(1)}, f32[1,1024]{1,0:T(1,128)S(1)}, u32[]{:S(2)}, u32[]{:S(2)}) %collective-permute-start.11) | collective-permute-done | bytes 4128 | tf_op jit(solution)/shard_map/ppermute | solution.py:28
  112.1 5.3 %collective-permute-done.12 = f32[1,1024]{1,0:T(1,128)S(1)} collective-permute-done((f32[1,1024]{1,0:T(1,128)S(1)}, f32[1,1024]{1,0:T(1,128)S(1)}, u32[]{:S(2)}, u32[]{:S(2)}) %collective-permute-start.12) | collective-permute-done | bytes 4128 | tf_op jit(solution)/shard_map/ppermute | solution.py:28
  118.0 13.2 %collective-permute-done.13 = f32[1,1024]{1,0:T(1,128)S(1)} collective-permute-done((f32[1,1024]{1,0:T(1,128)S(1)}, f32[1,1024]{1,0:T(1,128)S(1)}, u32[]{:S(2)}, u32[]{:S(2)}) %collective-permute-start.13) | collective-permute-done | bytes 4128 | tf_op jit(solution)/shard_map/ppermute | solution.py:28
  132.1 15.8 %collective-permute-done.18 = bf16[256,1024]{1,0:T(8,128)(2,1)S(1)} collective-permute-done((bf16[256,1024]{1,0:T(8,128)(2,1)S(1)}, bf16[256,1024]{1,0:T(8,128)(2,1)S(1)}, u32[]{:S(2)}, u32[]{:S(2)}) %collective-permute-start.18) | collective-permute-done | bytes 524320 | tf_op jit(solution)/shard_map/ppermute | solution.py:28
  147.9 7.4 %collective-permute-done.24 = bf16[128,2048]{1,0:T(8,128)(2,1)S(1)} collective-permute-done((bf16[128,2048]{1,0:T(8,128)(2,1)S(1)}, bf16[128,2048]{1,0:T(8,128)(2,1)S(1)}, u32[]{:S(2)}, u32[]{:S(2)}) %collective-permute-start.24) | collective-permute-done | bytes 524320 | tf_op jit(solution)/shard_map/ppermute | solution.py:28
  156.7 1.9 collective-permute-start.31
  160.1 14.9 %collective-permute-done.19 = bf16[256,1024]{1,0:T(8,128)(2,1)S(1)} collective-permute-done((bf16[256,1024]{1,0:T(8,128)(2,1)S(1)}, bf16[256,1024]{1,0:T(8,128)(2,1)S(1)}, u32[]{:S(2)}, u32[]{:S(2)}) %collective-permute-start.19) | collective-permute-done | bytes 524320 | tf_op jit(solution)/shard_map/ppermute | solution.py:28
  175.3 6.4 %collective-permute-done.30 = bf16[256,2048]{1,0:T(8,128)(2,1)S(1)} collective-permute-done((bf16[256,2048]{1,0:T(8,128)(2,1)S(1)}, bf16[256,2048]{1,0:T(8,128)(2,1)S(1)}, u32[]{:S(2)}, u32[]{:S(2)}) %collective-permute-start.30) | collective-permute-done | bytes 1048608 | tf_op jit(solution)/shard_map/ppermute | solution.py:45
  182.7 21.1 %collective-permute-done.31 = bf16[256,2048]{1,0:T(8,128)(2,1)S(1)} collective-permute-done((bf16[256,2048]{1,0:T(8,128)(2,1)}, bf16[256,2048]{1,0:T(8,128)(2,1)S(1)}, u32[]{:S(2)}, u32[]{:S(2)}) %collective-permute-start.31) | collective-permute-done | bytes 1048608 | tf_op jit(solution)/shard_map/ppermute | solution.py:45
  204.8 25.6 %fusion.11 = f32[1024,2048]{1,0:T(8,128)} fusion(bf16[256,2048]{1,0:T(8,128)(2,1)} %collective-permute-done.34, bf16[256,2048]{1,0:T(8,128)(2,1)} %collective-permute-done.33, bf16[256,2048]{1,0:T(8,128)(2,1)} %copy-done.14, bf16[256,2048]{1,0:T(8,128)(2,1)} %param.17, bf16[1024,2048]{1,0:T(8,128)(2,1)} %copy-done.10, bf16[256,2048]{1,0:T(8,128)(2,1)} %copy-done.15, ...), kind=kOutput, calls=%fused_computation.12 | convolution fusion | flops 8691646464 | bytes 20971520 | tf_op jit(solution)/shard_map/dot_general | solution.py:232
  230.7 2.0 fusion.41
  232.8 2.7 fusion.44
  236.0 2.4 fusion.43
  238.3 2.3 fusion.48
  240.7 13.6 %collective-permute-done.39 = bf16[128,2048]{1,0:T(8,128)(2,1)} collective-permute-done((bf16[128,2048]{1,0:T(8,128)(2,1)}, bf16[128,2048]{1,0:T(8,128)(2,1)}, u32[]{:S(2)}, u32[]{:S(2)}) %collective-permute-start.39) | collective-permute-done | bytes 524320 | tf_op jit(solution)/shard_map/ppermute | solution.py:28
  254.3 2.6 fusion.47
  256.9 2.4 fusion.52
  259.3 12.7 %collective-permute-done.40 = bf16[128,2048]{1,0:T(8,128)(2,1)} collective-permute-done((bf16[128,2048]{1,0:T(8,128)(2,1)}, bf16[128,2048]{1,0:T(8,128)(2,1)}, u32[]{:S(2)}, u32[]{:S(2)}) %collective-permute-start.40) | collective-permute-done | bytes 524320 | tf_op jit(solution)/shard_map/ppermute | solution.py:28
  272.0 2.6 fusion.51
  274.6 14.1 %collective-permute-done.41 = bf16[128,2048]{1,0:T(8,128)(2,1)S(1)} collective-permute-done((bf16[128,2048]{1,0:T(8,128)(2,1)}, bf16[128,2048]{1,0:T(8,128)(2,1)S(1)}, u32[]{:S(2)}, u32[]{:S(2)}) %collective-permute-start.41) | collective-permute-done | bytes 524320 | tf_op jit(solution)/shard_map/ppermute | solution.py:28
  288.7 2.6 fusion.40
  (138 shorter events, 20.5 us)
Async XLA Ops:
  6.5 224.2 %all-gather.2.cloned.1.call-start = ((), (), s32[]{:S(2)}) async-start(), calls=%async_computation | async-start | bytes 1310720 | tf_op jit(solution)/shard_map/all_gather | solution.py:54
  7.7 18.1 %collective-permute-start = (bf16[128,2048]{1,0:T(8,128)(2,1)S(1)}, bf16[128,2048]{1,0:T(8,128)(2,1)S(1)}, u32[]{:S(2)}, u32[]{:S(2)}) collective-permute-start(bf16[128,2048]{1,0:T(8,128)(2,1)S(1)} %slice.83.refs_0_), channel_id=1, source_target_pairs={{0,2},{1,3},{2,4},{3,5},{4,6},{5,7},{6,0},{7,1},{8,10},{9,11},{10,... | collective-permute-start | bytes 1572872 | tf_op jit(solution)/shard_map/ppermute | solution.py:28
  10.8 50.7 %collective-permute-start.3 = (bf16[128,2048]{1,0:T(8,128)(2,1)S(1)}, bf16[128,2048]{1,0:T(8,128)(2,1)}, u32[]{:S(2)}, u32[]{:S(2)}) collective-permute-start(bf16[128,2048]{1,0:T(8,128)(2,1)S(1)} %slice.83.refs_0_), channel_id=1, source_target_pairs={{0,1},{1,0},{2,3},{3,2},{4,5},{5,4},{6,7},{7,6},{8,9},{9,8},{10,11... | collective-permute-start | bytes 1572872 | tf_op jit(solution)/shard_map/ppermute | solution.py:21
  10.8 48.3 %collective-permute-start.21 = (bf16[64,2048]{1,0:T(8,128)(2,1)}, bf16[64,2048]{1,0:T(8,128)(2,1)S(1)}, u32[]{:S(2)}, u32[]{:S(2)}) collective-permute-start(bf16[64,2048]{1,0:T(8,128)(2,1)} %param.15), channel_id=1, source_target_pairs={{0,0},{1,8},{2,16},{3,24},{4,1},{5,9},{6,17},{7,25},{8,2},{9,10},{... | collective-permute-start | bytes 786440 | tf_op jit(solution)/shard_map/ppermute | solution.py:200
  25.8 16.1 %collective-permute-start.1 = (bf16[128,2048]{1,0:T(8,128)(2,1)S(1)}, bf16[128,2048]{1,0:T(8,128)(2,1)}, u32[]{:S(2)}, u32[]{:S(2)}) collective-permute-start(bf16[128,2048]{1,0:T(8,128)(2,1)S(1)} %collective-permute-done.refs_1_), channel_id=1, source_target_pairs={{0,2},{1,3},{2,4},{3,5},{4,6},{5,7},{6,0},{7,1},{8,10},{9,11},{10,... | collective-permute-start | bytes 1572872 | tf_op jit(solution)/shard_map/ppermute | solution.py:28
  41.9 15.3 %collective-permute-start.2 = (bf16[128,2048]{1,0:T(8,128)(2,1)}, bf16[128,2048]{1,0:T(8,128)(2,1)}, u32[]{:S(2)}, u32[]{:S(2)}) collective-permute-start(bf16[128,2048]{1,0:T(8,128)(2,1)} %collective-permute-done.1.refs_2_), channel_id=1, source_target_pairs={{0,2},{1,3},{2,4},{3,5},{4,6},{5,7},{6,0},{7,1},{8,10},{9,11},{10,... | collective-permute-start | bytes 1572872 | tf_op jit(solution)/shard_map/ppermute | solution.py:28
  44.2 28.1 %collective-permute-start.4 = (bf16[128,2048]{1,0:T(8,128)(2,1)S(1)}, bf16[128,2048]{1,0:T(8,128)(2,1)}, u32[]{:S(2)}, u32[]{:S(2)}) collective-permute-start(bf16[128,2048]{1,0:T(8,128)(2,1)S(1)} %collective-permute-done.refs_1_), channel_id=1, source_target_pairs={{0,1},{1,0},{2,3},{3,2},{4,5},{5,4},{6,7},{7,6},{8,9},{9,8},{10,11... | collective-permute-start | bytes 1572872 | tf_op jit(solution)/shard_map/ppermute | solution.py:21
  44.2 28.1 %collective-permute-start.5 = (bf16[128,2048]{1,0:T(8,128)(2,1)}, bf16[128,2048]{1,0:T(8,128)(2,1)}, u32[]{:S(2)}, u32[]{:S(2)}) collective-permute-start(bf16[128,2048]{1,0:T(8,128)(2,1)} %collective-permute-done.1.refs_2_), channel_id=1, source_target_pairs={{0,1},{1,0},{2,3},{3,2},{4,5},{5,4},{6,7},{7,6},{8,9},{9,8},{10,11... | collective-permute-start | bytes 1572872 | tf_op jit(solution)/shard_map/ppermute | solution.py:21
  57.2 15.2 %collective-permute-start.6 = (bf16[128,2048]{1,0:T(8,128)(2,1)}, bf16[128,2048]{1,0:T(8,128)(2,1)}, u32[]{:S(2)}, u32[]{:S(2)}) collective-permute-start(bf16[128,2048]{1,0:T(8,128)(2,1)} %collective-permute-done.2.refs_3_), channel_id=1, source_target_pairs={{0,1},{1,0},{2,3},{3,2},{4,5},{5,4},{6,7},{7,6},{8,9},{9,8},{10,11... | collective-permute-start | bytes 1572872 | tf_op jit(solution)/shard_map/ppermute | solution.py:21
  59.2 72.2 %collective-permute-start.29 = (bf16[256,2048]{1,0:T(8,128)(2,1)}, bf16[256,2048]{1,0:T(8,128)(2,1)}, u32[]{:S(2)}, u32[]{:S(2)}) collective-permute-start(bf16[256,2048]{1,0:T(8,128)(2,1)} %param.16), channel_id=1, source_target_pairs={{0,8},{1,9},{2,10},{3,11},{4,12},{5,13},{6,14},{7,15},{8,0},{9,1},... | collective-permute-start | bytes 3145736 | tf_op jit(solution)/shard_map/ppermute | solution.py:45
  61.5 70.0 %collective-permute-start.33 = (bf16[256,2048]{1,0:T(8,128)(2,1)}, bf16[256,2048]{1,0:T(8,128)(2,1)}, u32[]{:S(2)}, u32[]{:S(2)}) collective-permute-start(bf16[256,2048]{1,0:T(8,128)(2,1)} %param.17), channel_id=1, source_target_pairs={{0,16},{1,17},{2,18},{3,19},{4,20},{5,21},{6,22},{7,23},{8,24},{9,... | collective-permute-start | bytes 3145736 | tf_op jit(solution)/shard_map/ppermute | solution.py:45
  72.3 32.8 %collective-permute-start.22 = (bf16[128,2048]{1,0:T(8,128)(2,1)}, bf16[128,2048]{1,0:T(8,128)(2,1)S(1)}, u32[]{:S(2)}, u32[]{:S(2)}) collective-permute-start(bf16[128,2048]{1,0:T(8,128)(2,1)} %fusion.39), channel_id=1, source_target_pairs={{0,2},{1,3},{2,4},{3,5},{4,6},{5,7},{6,0},{7,1},{8,10},{9,11},{10,... | collective-permute-start | bytes 1572872 | tf_op jit(solution)/shard_map/ppermute | solution.py:28
  89.4 22.7 %collective-permute-start.8 = (f32[1,1024]{1,0:T(1,128)S(1)}, f32[1,1024]{1,0:T(1,128)S(1)}, u32[]{:S(2)}, u32[]{:S(2)}) collective-permute-start(f32[1,1024]{1,0:T(1,128)S(1)} %slice_bitcast_fusion.6), channel_id=1, source_target_pairs={{0,1},{1,0},{2,3},{3,2},{4,5},{5,4},{6,7},{7,6},{8,9},{9,8},{10,11... | collective-permute-start | bytes 12296 | tf_op jit(solution)/shard_map/ppermute | solution.py:21
  117.4 13.9 %collective-permute-start.23 = (bf16[128,2048]{1,0:T(8,128)(2,1)S(1)}, bf16[128,2048]{1,0:T(8,128)(2,1)S(1)}, u32[]{:S(2)}, u32[]{:S(2)}) collective-permute-start(bf16[128,2048]{1,0:T(8,128)(2,1)S(1)} %collective-permute-done.22), channel_id=1, source_target_pairs={{0,2},{1,3},{2,4},{3,5},{4,6},{5,7},{6,0},{7,1},{8,10},{9,11},{10,... | collective-permute-start | bytes 1572872 | tf_op jit(solution)/shard_map/ppermute | solution.py:28
  117.9 14.1 %collective-permute-start.16 = (bf16[256,1024]{1,0:T(8,128)(2,1)S(1)}, bf16[256,1024]{1,0:T(8,128)(2,1)S(1)}, u32[]{:S(2)}, u32[]{:S(2)}) collective-permute-start(bf16[256,1024]{1,0:T(8,128)(2,1)S(1)} %slice_bitcast_fusion.1), channel_id=1, source_target_pairs={{0,1},{1,0},{2,3},{3,2},{4,5},{5,4},{6,7},{7,6},{8,9},{9,8},{10,11... | collective-permute-start | bytes 1572872 | tf_op jit(solution)/shard_map/ppermute | solution.py:21
  131.2 16.7 %collective-permute-start.18 = (bf16[256,1024]{1,0:T(8,128)(2,1)S(1)}, bf16[256,1024]{1,0:T(8,128)(2,1)S(1)}, u32[]{:S(2)}, u32[]{:S(2)}) collective-permute-start(bf16[256,1024]{1,0:T(8,128)(2,1)S(1)} %fusion.56), channel_id=1, source_target_pairs={{0,2},{1,3},{2,4},{3,5},{4,6},{5,7},{6,0},{7,1},{8,10},{9,11},{10,... | collective-permute-start | bytes 1572872 | tf_op jit(solution)/shard_map/ppermute | solution.py:28
  131.3 24.0 %collective-permute-start.24 = (bf16[128,2048]{1,0:T(8,128)(2,1)S(1)}, bf16[128,2048]{1,0:T(8,128)(2,1)S(1)}, u32[]{:S(2)}, u32[]{:S(2)}) collective-permute-start(bf16[128,2048]{1,0:T(8,128)(2,1)S(1)} %collective-permute-done.23), channel_id=1, source_target_pairs={{0,2},{1,3},{2,4},{3,5},{4,6},{5,7},{6,0},{7,1},{8,10},{9,11},{10,... | collective-permute-start | bytes 1572872 | tf_op jit(solution)/shard_map/ppermute | solution.py:28
  131.4 24.2 %collective-permute-start.25 = (bf16[128,2048]{1,0:T(8,128)(2,1)S(1)}, bf16[128,2048]{1,0:T(8,128)(2,1)S(1)}, u32[]{:S(2)}, u32[]{:S(2)}) collective-permute-start(bf16[128,2048]{1,0:T(8,128)(2,1)S(1)} %copy-done.8), channel_id=1, source_target_pairs={{0,1},{1,0},{2,3},{3,2},{4,5},{5,4},{6,7},{7,6},{8,9},{9,8},{10,11... | collective-permute-start | bytes 1572872 | tf_op jit(solution)/shard_map/ppermute | solution.py:21
  131.5 24.5 %collective-permute-start.15 = (bf16[256,1024]{1,0:T(8,128)(2,1)S(1)}, bf16[256,1024]{1,0:T(8,128)(2,1)S(1)}, u32[]{:S(2)}, u32[]{:S(2)}) collective-permute-start(bf16[256,1024]{1,0:T(8,128)(2,1)S(1)} %slice_bitcast_fusion.2), channel_id=1, source_target_pairs={{0,1},{1,0},{2,3},{3,2},{4,5},{5,4},{6,7},{7,6},{8,9},{9,8},{10,11... | collective-permute-start | bytes 1572872 | tf_op jit(solution)/shard_map/ppermute | solution.py:21
  132.0 24.6 %collective-permute-start.26 = (bf16[128,2048]{1,0:T(8,128)(2,1)S(1)}, bf16[128,2048]{1,0:T(8,128)(2,1)S(1)}, u32[]{:S(2)}, u32[]{:S(2)}) collective-permute-start(bf16[128,2048]{1,0:T(8,128)(2,1)S(1)} %collective-permute-done.22), channel_id=1, source_target_pairs={{0,1},{1,0},{2,3},{3,2},{4,5},{5,4},{6,7},{7,6},{8,9},{9,8},{10,11... | collective-permute-start | bytes 1572872 | tf_op jit(solution)/shard_map/ppermute | solution.py:21
  155.7 26.0 %collective-permute-start.30 = (bf16[256,2048]{1,0:T(8,128)(2,1)S(1)}, bf16[256,2048]{1,0:T(8,128)(2,1)S(1)}, u32[]{:S(2)}, u32[]{:S(2)}) collective-permute-start(bf16[256,2048]{1,0:T(8,128)(2,1)S(1)} %copy-done.12), channel_id=1, source_target_pairs={{0,16},{1,17},{2,18},{3,19},{4,20},{5,21},{6,22},{7,23},{8,24},{9,... | collective-permute-start | bytes 3145736 | tf_op jit(solution)/shard_map/ppermute | solution.py:45
  156.0 26.0 %collective-permute-start.32 = (bf16[256,2048]{1,0:T(8,128)(2,1)S(1)}, bf16[256,2048]{1,0:T(8,128)(2,1)S(1)}, u32[]{:S(2)}, u32[]{:S(2)}) collective-permute-start(bf16[256,2048]{1,0:T(8,128)(2,1)S(1)} %copy-done.11), channel_id=1, source_target_pairs={{0,8},{1,9},{2,10},{3,11},{4,12},{5,13},{6,14},{7,15},{8,0},{9,1},... | collective-permute-start | bytes 3145736 | tf_op jit(solution)/shard_map/ppermute | solution.py:45
  156.7 47.1 %collective-permute-start.31 = (bf16[256,2048]{1,0:T(8,128)(2,1)}, bf16[256,2048]{1,0:T(8,128)(2,1)S(1)}, u32[]{:S(2)}, u32[]{:S(2)}) collective-permute-start(bf16[256,2048]{1,0:T(8,128)(2,1)} %collective-permute-done.29), channel_id=1, source_target_pairs={{0,16},{1,17},{2,18},{3,19},{4,20},{5,21},{6,22},{7,23},{8,24},{9,... | collective-permute-start | bytes 3145736 | tf_op jit(solution)/shard_map/ppermute | solution.py:45
  158.6 46.2 %collective-permute-start.34 = (bf16[256,2048]{1,0:T(8,128)(2,1)}, bf16[256,2048]{1,0:T(8,128)(2,1)}, u32[]{:S(2)}, u32[]{:S(2)}) collective-permute-start(bf16[256,2048]{1,0:T(8,128)(2,1)} %collective-permute-done.33), channel_id=1, source_target_pairs={{0,8},{1,9},{2,10},{3,11},{4,12},{5,13},{6,14},{7,15},{8,0},{9,1},... | collective-permute-start | bytes 3145736 | tf_op jit(solution)/shard_map/ppermute | solution.py:45
  159.9 15.1 %collective-permute-start.19 = (bf16[256,1024]{1,0:T(8,128)(2,1)S(1)}, bf16[256,1024]{1,0:T(8,128)(2,1)S(1)}, u32[]{:S(2)}, u32[]{:S(2)}) collective-permute-start(bf16[256,1024]{1,0:T(8,128)(2,1)S(1)} %fusion.59), channel_id=1, source_target_pairs={{0,2},{1,3},{2,4},{3,5},{4,6},{5,7},{6,0},{7,1},{8,10},{9,11},{10,... | collective-permute-start | bytes 1572872 | tf_op jit(solution)/shard_map/ppermute | solution.py:28
  174.9 55.4 %collective-permute-start.14 = (bf16[256,1024]{1,0:T(8,128)(2,1)S(1)}, bf16[256,1024]{1,0:T(8,128)(2,1)S(1)}, u32[]{:S(2)}, u32[]{:S(2)}) collective-permute-start(bf16[256,1024]{1,0:T(8,128)(2,1)S(1)} %slice_bitcast_fusion.3), channel_id=1, source_target_pairs={{0,1},{1,0},{2,3},{3,2},{4,5},{5,4},{6,7},{7,6},{8,9},{9,8},{10,11... | collective-permute-start | bytes 1572872 | tf_op jit(solution)/shard_map/ppermute | solution.py:21
  181.7 48.7 %collective-permute-start.20 = (bf16[256,1024]{1,0:T(8,128)(2,1)S(1)}, bf16[256,1024]{1,0:T(8,128)(2,1)S(1)}, u32[]{:S(2)}, u32[]{:S(2)}) collective-permute-start(bf16[256,1024]{1,0:T(8,128)(2,1)S(1)} %fusion.62), channel_id=1, source_target_pairs={{0,2},{1,3},{2,4},{3,5},{4,6},{5,7},{6,0},{7,1},{8,10},{9,11},{10,... | collective-permute-start | bytes 1572872 | tf_op jit(solution)/shard_map/ppermute | solution.py:28
  238.3 16.0 %collective-permute-start.39 = (bf16[128,2048]{1,0:T(8,128)(2,1)}, bf16[128,2048]{1,0:T(8,128)(2,1)}, u32[]{:S(2)}, u32[]{:S(2)}) collective-permute-start(bf16[128,2048]{1,0:T(8,128)(2,1)} %fusion.43), channel_id=1, source_target_pairs={{0,2},{1,3},{2,4},{3,5},{4,6},{5,7},{6,0},{7,1},{8,10},{9,11},{10,... | collective-permute-start | bytes 1572872 | tf_op jit(solution)/shard_map/ppermute | solution.py:28
  240.7 18.6 %collective-permute-start.36 = (bf16[128,2048]{1,0:T(8,128)(2,1)}, bf16[128,2048]{1,0:T(8,128)(2,1)S(1)}, u32[]{:S(2)}, u32[]{:S(2)}) collective-permute-start(bf16[128,2048]{1,0:T(8,128)(2,1)} %fusion.48), channel_id=1, source_target_pairs={{0,1},{1,0},{2,3},{3,2},{4,5},{5,4},{6,7},{7,6},{8,9},{9,8},{10,11... | collective-permute-start | bytes 1572872 | tf_op jit(solution)/shard_map/ppermute | solution.py:21
  256.9 15.1 %collective-permute-start.40 = (bf16[128,2048]{1,0:T(8,128)(2,1)}, bf16[128,2048]{1,0:T(8,128)(2,1)}, u32[]{:S(2)}, u32[]{:S(2)}) collective-permute-start(bf16[128,2048]{1,0:T(8,128)(2,1)} %fusion.47), channel_id=1, source_target_pairs={{0,2},{1,3},{2,4},{3,5},{4,6},{5,7},{6,0},{7,1},{8,10},{9,11},{10,... | collective-permute-start | bytes 1572872 | tf_op jit(solution)/shard_map/ppermute | solution.py:28
  259.3 15.3 %collective-permute-start.35 = (bf16[128,2048]{1,0:T(8,128)(2,1)}, bf16[128,2048]{1,0:T(8,128)(2,1)S(1)}, u32[]{:S(2)}, u32[]{:S(2)}) collective-permute-start(bf16[128,2048]{1,0:T(8,128)(2,1)} %fusion.52), channel_id=1, source_target_pairs={{0,1},{1,0},{2,3},{3,2},{4,5},{5,4},{6,7},{7,6},{8,9},{9,8},{10,11... | collective-permute-start | bytes 1572872 | tf_op jit(solution)/shard_map/ppermute | solution.py:21
  274.6 14.1 %collective-permute-start.41 = (bf16[128,2048]{1,0:T(8,128)(2,1)}, bf16[128,2048]{1,0:T(8,128)(2,1)S(1)}, u32[]{:S(2)}, u32[]{:S(2)}) collective-permute-start(bf16[128,2048]{1,0:T(8,128)(2,1)} %fusion.51), channel_id=1, source_target_pairs={{0,2},{1,3},{2,4},{3,5},{4,6},{5,7},{6,0},{7,1},{8,10},{9,11},{10,... | collective-permute-start | bytes 1572872 | tf_op jit(solution)/shard_map/ppermute | solution.py:28
  (27 other events, 476.4 us)
Sparse Core Ops, SparseCore 0:
  60.5 43.1 all-gather.1

commit v3 on v2

--- a/solution.py
+++ b/solution.py
@@ -32,18 +32,16 @@
     pieces = [value]
     for _ in range(CHIPS - 1):
         pieces.append(next_chip(pieces[-1]))
-    return pieces, [swap_cores(piece) for piece in pieces]
-
-
-def gather_requests(value, low_first):
+    return pieces
+
+
+def widen(pieces, bit):
     device_count = lax.axis_size("kv") * lax.axis_size("req")
-    bits = range((device_count // SPAN).bit_length() - 1)
-    pieces = {0: value}
-    for bit in bits if low_first else reversed(bits):
-        pairs = [(d, d ^ (SPAN << bit)) for d in range(device_count)]
-        for index in list(pieces):
-            pieces[index | 1 << bit] = lax.ppermute(pieces[index], ("req", "kv"), pairs)
-    return [pieces[index] for index in range(len(pieces))]
+    pairs = [(d, d ^ (SPAN << bit)) for d in range(device_count)]
+    found = dict(pieces)
+    for index, piece in pieces.items():
+        found[index | 1 << bit] = lax.ppermute(piece, ("req", "kv"), pairs)
+    return found
 
 
 def gather_in_order(value):
@@ -191,9 +189,22 @@
     chip = member // CORES
     request = (lax.axis_index("req") * kv_count + kv_place) // SPAN
 
-    q_mine, q_other = gather_ring(projections[:, :width])
-    up_rows = jnp.concatenate(gather_requests(up_weight, True), 0)
-    down_rows = jnp.concatenate(gather_requests(down_weight, False), 0)
+    bits = list(range(request_count.bit_length() - 1))
+    q_mine = [projections[:, :width]]
+    up_pieces, down_pieces = {0: up_weight}, {0: down_weight}
+    for step in range(CHIPS - 2):
+        q_mine.append(next_chip(q_mine[-1]))
+    up_pieces = widen(up_pieces, bits[0])
+    down_pieces = widen(down_pieces, bits[-1])
+    q_mine[-1], up_pieces, down_pieces = lax.optimization_barrier(
+        (q_mine[-1], up_pieces, down_pieces)
+    )
+    q_mine.append(next_chip(q_mine[-1]))
+    q_other = [swap_cores(piece) for piece in q_mine]
+    for bit in bits[1:]:
+        up_pieces = widen(up_pieces, bit)
+    for bit in reversed(bits[:-1]):
+        down_pieces = widen(down_pieces, bit)
     head_pairs = [
         (d, (d % request_count) * SPAN + d // request_count) for d in range(device_count)
     ]
@@ -205,7 +216,8 @@
     bias = bias.astype(F32)
 
     normed, _ = lax.optimization_barrier((layer_norm(stream, norm_gain), q_mine[-1]))
-    rows_mine, rows_other = gather_ring(normed)
+    rows_mine = gather_ring(normed)
+    rows_other = [swap_cores(piece) for piece in rows_mine]
 
     carried = None
     for phase in range(CHIPS):
@@ -213,6 +225,10 @@
         kept = CORES * target + core
         given = CORES * target + 1 - core
         meta = jnp.stack([kept, given, core, member]).astype(jnp.int32)
+        if phase == CHIPS - 1:
+            meta, up_pieces, down_pieces = lax.optimization_barrier(
+                (meta, up_pieces, down_pieces)
+            )
         out, lse = attend(meta, q_mine + q_other, key_cache, value_cache, projections, bias)
         parts = [(out[0], lse[0]), swap_cores((out[1], lse[1]))]
         if carried is not None:
@@ -220,31 +236,45 @@
         carried = merge(parts)
         if phase < CHIPS - 1:
             carried = next_chip(carried)
-    attention = carried[0]
-
-    gates = lax.dot_general(
-        jnp.concatenate(rows_mine + rows_other, 0),
-        up_rows,
-        (((1,), (1,)), ((), ())),
-        preferred_element_type=F32,
-    )
-    hidden = jax.nn.gelu(gates, approximate=False).astype(BF16)
-    units = jnp.dot(hidden, down_rows, preferred_element_type=F32)
+    up_rows = jnp.concatenate([up_pieces[i] for i in range(request_count)], 0)
+    down_rows = jnp.concatenate([down_pieces[i] for i in range(request_count)], 0)
+    units = []
+    for step in range(CHIPS):
+        gates = lax.dot_general(
+            jnp.concatenate([rows_mine[step], rows_other[step]], 0),
+            up_rows,
+            (((1,), (1,)), ((), ())),
+            preferred_element_type=F32,
+        )
+        hidden = jax.nn.gelu(gates, approximate=False).astype(BF16)
+        units.append(jnp.dot(hidden, down_rows, preferred_element_type=F32))
+    attention, units = lax.optimization_barrier((carried[0], units))
+
     half = CHIPS * token_count
+    order = [(step + 1) % CHIPS for step in range(CHIPS)]
+    firsts = [((chip + CHIPS - step) % CHIPS) * token_count for step in order]
+
+    def branch(offset):
+        block = jnp.concatenate(
+            [
+                lax.dynamic_slice_in_dim(attention, offset + first, token_count, 1)
+                for first in firsts
+            ],
+            1,
+        )
+        return lax.dot_general(
+            block, out_rows, (((0,), (0,)), ((), ())), preferred_element_type=F32
+        )
+
+    given, kept = branch(half), branch(0)
+    received = []
+    for phase, step in enumerate(order):
+        rows = slice(phase * token_count, (phase + 1) * token_count)
+        received.append(swap_cores((given[rows] + units[step][token_count:]).astype(BF16)))
     running = None
-    for phase in range(CHIPS):
-        step = (phase + 1) % CHIPS
-        first = ((chip + CHIPS - step) % CHIPS) * token_count
-
-        def share(offset):
-            block = lax.dynamic_slice_in_dim(attention, offset + first, token_count, 1)
-            branch = lax.dot_general(
-                block, out_rows, (((0,), (0,)), ((), ())), preferred_element_type=F32
-            )
-            held = offset + step * token_count
-            return branch + units[held : held + token_count]
-
-        total = share(0) + swap_cores(share(half).astype(BF16)).astype(F32)
+    for phase, step in enumerate(order):
+        rows = slice(phase * token_count, (phase + 1) * token_count)
+        total = kept[rows] + units[step][:token_count] + received[phase].astype(F32)
         if running is not None:
             total = total + running.astype(F32)
         running = total

time: 299 us -> 305 us (1.020)
  waiting for transfers between devices: 170 us -> 145 us
  local copies, waits for them, and re-layouts: 7.22 us -> 24.4 us
  starting transfers between devices: 24.5 us -> 32.3 us
  other arithmetic: 7.59 us -> 13.4 us
  matrix products: 45.1 us -> 41.7 us
    ppermute x15, waiting for transfers between devices: 141 us -> 122 us  [next_chip(): return lax.ppermute(value, 'kv', pairs)]
    ppermute x15, starting transfers between devices: 4.09 us -> 16.4 us  [next_chip(): return lax.ppermute(value, 'kv', pairs)]
    unnamed x39 -> x60, local copies, waits for them, and re-layouts: 5.22 us -> 17 us
    ppermute x6, waiting for transfers between devices: 27.8 us -> 21.6 us  [widen(): found[index | 1 << bit] = lax.ppermute(piece, ('req', 'kv'), pairs)]
    ppermute x6, starting transfers between devices: 16.2 us -> 10.4 us  [widen(): found[index | 1 << bit] = lax.ppermute(piece, ('req', 'kv'), pairs)]
    convert_element_type x0 -> x5, other arithmetic: none -> 3.74 us  [the longest x1 1.88 us: on_device(): (given[rows] + units[step][token_count:]).astype(BF16)]
    dot_general x9 -> x6, matrix products: 45.1 us -> 41.7 us  [the longest x4 38.9 us: on_device(): units.append(jnp.dot(hidden, down_rows, preferred_element_type=F32))]
  transfers between devices with their start and end apart: 43 -> 43, of which waited for: 16 -> 18; matrix products, arithmetic and copies ran while one was open for 17% -> 22% of each run, Pallas kernels for 10% -> 10%
where the time goes in v3:
time: 305 us; the launch traced here: 302 us
  waiting for transfers between devices  145 us (48%)
  matrix products  41.7 us (14%)
  starting transfers between devices  32.3 us (11%)
  Pallas kernels  30.1 us (10%)
  local copies, waits for them, and re-layouts  24.4 us (8%)
  between operations  14.5 us (5%)
  other arithmetic  13.4 us (4%)
    ppermute x15, waiting for transfers between devices, next_chip(): return lax.ppermute(value, 'kv', pairs)  122 us
    dot_general x4, matrix products, on_device(): units.append(jnp.dot(hidden, down_rows, preferred_element_type=F32))  38.9 us
    pallas_call x4, Pallas kernels, attend(): pl.pallas_call(attend_kernel, grid_spec=pltpu.PrefetchScalarGridSpec(num_...  30.1 us
    ppermute x6, waiting for transfers between devices, widen(): found[index | 1 << bit] = lax.ppermute(piece, ('req', 'kv'), pairs)  21.6 us
    unnamed x60, local copies, waits for them, and re-layouts  17 us
    ppermute x15, starting transfers between devices, next_chip(): return lax.ppermute(value, 'kv', pairs)  16.4 us
    ppermute x6, starting transfers between devices, widen(): found[index | 1 << bit] = lax.ppermute(piece, ('req', 'kv'), pairs)  10.4 us
  transfers between devices with their start and end apart: 43, of which 18 were waited for; matrix products, arithmetic and copies ran while one was open for 22% of the time, Pallas kernels for 10%

profile of v3, /device:TPU:0, one launch (start us, length us, event | category | flops | bytes accessed | tf_op | source)
XLA Modules:
  0.0 301.5 jit_solution(17398166110449842981)
XLA Ops:
  7.7 3.1 %collective-permute-start = (bf16[128,2048]{1,0:T(8,128)(2,1)S(1)}, bf16[128,2048]{1,0:T(8,128)(2,1)S(1)}, u32[]{:S(2)}, u32[]{:S(2)}) collective-permute-start(bf16[128,2048]{1,0:T(8,128)(2,1)S(1)} %slice.107.refs_0_), channel_id=1, source_target_pairs={{0,2},{1,3},{2,4},{3,5},{4,6},{5,7},{6,0},{7,1},{8,10},{9,11},{10,... | collective-permute-start | bytes 1572872 | tf_op jit(solution)/shard_map/ppermute | solution.py:28
  15.5 10.3 %collective-permute-done.refs_1_ = bf16[128,2048]{1,0:T(8,128)(2,1)S(1)} collective-permute-done((bf16[128,2048]{1,0:T(8,128)(2,1)S(1)}, bf16[128,2048]{1,0:T(8,128)(2,1)S(1)}, u32[]{:S(2)}, u32[]{:S(2)}) %collective-permute-start) | collective-permute-done | bytes 524320 | tf_op jit(solution)/shard_map/ppermute | solution.py:28
  28.9 13.0 %collective-permute-done.1.refs_2_ = bf16[128,2048]{1,0:T(8,128)(2,1)S(1)} collective-permute-done((bf16[128,2048]{1,0:T(8,128)(2,1)S(1)}, bf16[128,2048]{1,0:T(8,128)(2,1)S(1)}, u32[]{:S(2)}, u32[]{:S(2)}) %collective-permute-start.1) | collective-permute-done | bytes 524320 | tf_op jit(solution)/shard_map/ppermute | solution.py:28
  43.9 5.3 %collective-permute-start.6 = (bf16[256,2048]{1,0:T(8,128)(2,1)}, bf16[256,2048]{1,0:T(8,128)(2,1)}, u32[]{:S(2)}, u32[]{:S(2)}) collective-permute-start(bf16[256,2048]{1,0:T(8,128)(2,1)} %param.17), channel_id=1, source_target_pairs={{0,8},{1,9},{2,10},{3,11},{4,12},{5,13},{6,14},{7,15},{8,0},{9,1},... | collective-permute-start | bytes 3145736 | tf_op jit(solution)/shard_map/ppermute | solution.py:43
  52.6 2.2 fusion.4
  54.8 15.3 %collective-permute-done.8.refs_3_ = bf16[128,2048]{1,0:T(8,128)(2,1)} collective-permute-done((bf16[128,2048]{1,0:T(8,128)(2,1)}, bf16[128,2048]{1,0:T(8,128)(2,1)}, u32[]{:S(2)}, u32[]{:S(2)}) %collective-permute-start.8) | collective-permute-done | bytes 524320 | tf_op jit(solution)/shard_map/ppermute | solution.py:28
  70.7 19.8 %collective-permute-done.5 = bf16[256,2048]{1,0:T(8,128)(2,1)} collective-permute-done((bf16[256,2048]{1,0:T(8,128)(2,1)}, bf16[256,2048]{1,0:T(8,128)(2,1)}, u32[]{:S(2)}, u32[]{:S(2)}) %collective-permute-start.5) | collective-permute-done | bytes 1048608 | tf_op jit(solution)/shard_map/ppermute | solution.py:43
  94.4 2.3 constant_dynamic-update-slice_fusion.7
  98.2 2.2 copy-done.3
  100.4 7.3 %shard_map.91 = (bf16[2,256,1024]{2,1,0:T(8,128)(2,1)S(1)}, f32[2,1,1024]{2,1,0:T(1,128)S(1)}) custom-call(s32[4]{0:T(128)S(1)} %add_add_fusion.3.meta, bf16[128,2048]{1,0:T(8,128)(2,1)S(1)} %slice.107.refs_0_, bf16[128,2048]{1,0:T(8,128)(2,1)S(1)} %collective-permute-done.refs_1_, bf16[128,2048]{1,0:T(8,128)(2,1)S(1)} %copy-done.6, ...), custom_call_target="tpu_custom_call" | custom-call | flops 2415919104 | bytes 8388608 | tf_op jit(solution)/shard_map/pallas_call | solution.py:127
  108.3 7.3 %shard_map.92 = (bf16[2,256,1024]{2,1,0:T(8,128)(2,1)S(1)}, f32[2,1,1024]{2,1,0:T(1,128)S(1)}) custom-call(s32[4]{0:T(128)S(1)} %get-tuple-element.94.meta, bf16[128,2048]{1,0:T(8,128)(2,1)S(1)} %slice.107.refs_0_, bf16[128,2048]{1,0:T(8,128)(2,1)S(1)} %collective-permute-done.refs_1_, bf16[128,2048]{1,0:T(8,128)(2,1)S(1)} %copy-done.6, ...), custom_call_target="tpu_custom_call" | custom-call | flops 2415919104 | bytes 8388608 | tf_op jit(solution)/shard_map/pallas_call | solution.py:127
  115.8 7.9 %shard_map.93 = (bf16[2,256,1024]{2,1,0:T(8,128)(2,1)S(1)}, f32[2,1,1024]{2,1,0:T(1,128)S(1)}) custom-call(s32[4]{0:T(128)S(1)} %get-tuple-element.95.meta, bf16[128,2048]{1,0:T(8,128)(2,1)S(1)} %slice.107.refs_0_, bf16[128,2048]{1,0:T(8,128)(2,1)S(1)} %collective-permute-done.refs_1_, bf16[128,2048]{1,0:T(8,128)(2,1)S(1)} %copy-done.6, ...), custom_call_target="tpu_custom_call" | custom-call | flops 2415919104 | bytes 8388608 | tf_op jit(solution)/shard_map/pallas_call | solution.py:127
  124.9 7.5 %shard_map.94 = (bf16[2,256,1024]{2,1,0:T(8,128)(2,1)S(1)}, f32[2,1,1024]{2,1,0:T(1,128)S(1)}) custom-call(s32[4]{0:T(128)S(1)} %add_add_fusion.6.meta, bf16[128,2048]{1,0:T(8,128)(2,1)S(1)} %slice.107.refs_0_, bf16[128,2048]{1,0:T(8,128)(2,1)S(1)} %collective-permute-done.refs_1_, bf16[128,2048]{1,0:T(8,128)(2,1)S(1)} %copy-done.6, ...), custom_call_target="tpu_custom_call" | custom-call | flops 2415919104 | bytes 8388608 | tf_op jit(solution)/shard_map/pallas_call | solution.py:127
  134.2 2.3 constant_dynamic-update-slice_fusion.6
  136.5 2.4 constant_dynamic-update-slice_fusion.5
  141.6 2.8 constant_dynamic-update-slice_fusion
  146.6 9.7 %fusion.105 = f32[256,2048]{1,0:T(8,128)} fusion(bf16[1024,2048]{1,0:T(8,128)(2,1)} %get-tuple-element.97, bf16[1024,2048]{1,0:T(8,128)(2,1)} %copy-done.24, bf16[128,2048]{1,0:T(8,128)(2,1)} %copy-done.26, bf16[128,2048]{1,0:T(8,128)(2,1)S(1)} %copy-done.22), kind=kOutput, calls=%fused_computation.141 | convolution fusion | flops 2166620160 | bytes 11534336 | tf_op jit(solution)/shard_map/dot_general | solution.py:250
  157.2 7.0 %collective-permute-start.17 = (f32[1,1024]{1,0:T(1,128)S(1)}, f32[1,1024]{1,0:T(1,128)S(1)}, u32[]{:S(2)}, u32[]{:S(2)}) collective-permute-start(f32[1,1024]{1,0:T(1,128)S(1)} %get-tuple-element.83), channel_id=1, source_target_pairs={{0,2},{1,3},{2,4},{3,5},{4,6},{5,7},{6,0},{7,1},{8,10},{9,11},{10,... | collective-permute-start | bytes 12296 | tf_op jit(solution)/shard_map/ppermute | solution.py:28
  164.3 2.8 collective-permute-done.17
  168.3 4.4 %collective-permute-done.18 = f32[1,1024]{1,0:T(1,128)S(1)} collective-permute-done((f32[1,1024]{1,0:T(1,128)S(1)}, f32[1,1024]{1,0:T(1,128)S(1)}, u32[]{:S(2)}, u32[]{:S(2)}) %collective-permute-start.18) | collective-permute-done | bytes 4128 | tf_op jit(solution)/shard_map/ppermute | solution.py:28
  174.3 3.8 %collective-permute-done.19 = f32[1,1024]{1,0:T(1,128)S(1)} collective-permute-done((f32[1,1024]{1,0:T(1,128)S(1)}, f32[1,1024]{1,0:T(1,128)S(1)}, u32[]{:S(2)}, u32[]{:S(2)}) %collective-permute-start.19) | collective-permute-done | bytes 4128 | tf_op jit(solution)/shard_map/ppermute | solution.py:28
  178.5 11.3 %collective-permute-done.30 = bf16[128,2048]{1,0:T(8,128)(2,1)} collective-permute-done((bf16[128,2048]{1,0:T(8,128)(2,1)}, bf16[128,2048]{1,0:T(8,128)(2,1)}, u32[]{:S(2)}, u32[]{:S(2)}) %collective-permute-start.30) | collective-permute-done | bytes 524320 | tf_op jit(solution)/shard_map/ppermute | solution.py:28
  189.9 9.8 %fusion.100 = f32[256,2048]{1,0:T(8,128)} fusion(bf16[1024,2048]{1,0:T(8,128)(2,1)} %get-tuple-element.97, bf16[1024,2048]{1,0:T(8,128)(2,1)} %copy-done.24, bf16[128,2048]{1,0:T(8,128)(2,1)} %collective-permute-done.29, bf16[128,2048]{1,0:T(8,128)(2,1)} %collective-permute-done.28), kind=kOutput, calls=%fused_computation.140 | convolution fusion | flops 2166620160 | bytes 11534336 | tf_op jit(solution)/shard_map/dot_general | solution.py:250
  202.7 9.7 %collective-permute-done.32 = bf16[128,2048]{1,0:T(8,128)(2,1)} collective-permute-done((bf16[128,2048]{1,0:T(8,128)(2,1)}, bf16[128,2048]{1,0:T(8,128)(2,1)}, u32[]{:S(2)}, u32[]{:S(2)}) %collective-permute-start.32) | collective-permute-done | bytes 524320 | tf_op jit(solution)/shard_map/ppermute | solution.py:28
  212.3 9.7 %fusion.95 = f32[256,2048]{1,0:T(8,128)} fusion(bf16[1024,2048]{1,0:T(8,128)(2,1)} %get-tuple-element.97, bf16[1024,2048]{1,0:T(8,128)(2,1)} %copy-done.24, bf16[128,2048]{1,0:T(8,128)(2,1)} %collective-permute-done.31, bf16[128,2048]{1,0:T(8,128)(2,1)} %collective-permute-done.30), kind=kOutput, calls=%fused_computation.139 | convolution fusion | flops 2166620160 | bytes 11534336 | tf_op jit(solution)/shard_map/dot_general | solution.py:250
  223.6 9.7 %fusion.90 = f32[256,2048]{1,0:T(8,128)} fusion(bf16[1024,2048]{1,0:T(8,128)(2,1)} %get-tuple-element.97, bf16[1024,2048]{1,0:T(8,128)(2,1)} %copy-done.24, bf16[128,2048]{1,0:T(8,128)(2,1)} %collective-permute-done.33, bf16[128,2048]{1,0:T(8,128)(2,1)} %collective-permute-done.32), kind=kOutput, calls=%fused_computation.138 | convolution fusion | flops 2166620160 | bytes 11534336 | tf_op jit(solution)/shard_map/dot_general | solution.py:250
  233.3 5.7 %collective-permute-done.26 = bf16[256,1024]{1,0:T(8,128)(2,1)S(1)} collective-permute-done((bf16[256,1024]{1,0:T(8,128)(2,1)S(1)}, bf16[256,1024]{1,0:T(8,128)(2,1)S(1)}, u32[]{:S(2)}, u32[]{:S(2)}) %collective-permute-start.26) | collective-permute-done | bytes 524320 | tf_op jit(solution)/shard_map/ppermute | solution.py:28
  240.6 2.1 fusion.239
  243.6 1.9 fusion.29
  248.2 15.2 %collective-permute-done.39 = bf16[128,2048]{1,0:T(8,128)(2,1)S(1)} collective-permute-done((bf16[128,2048]{1,0:T(8,128)(2,1)S(1)}, bf16[128,2048]{1,0:T(8,128)(2,1)S(1)}, u32[]{:S(2)}, u32[]{:S(2)}) %collective-permute-start.39) | collective-permute-done | bytes 524320 | tf_op jit(solution)/shard_map/ppermute | solution.py:28
  263.9 14.8 %collective-permute-done.40 = bf16[128,2048]{1,0:T(8,128)(2,1)S(1)} collective-permute-done((bf16[128,2048]{1,0:T(8,128)(2,1)S(1)}, bf16[128,2048]{1,0:T(8,128)(2,1)S(1)}, u32[]{:S(2)}, u32[]{:S(2)}) %collective-permute-start.40) | collective-permute-done | bytes 524320 | tf_op jit(solution)/shard_map/ppermute | solution.py:28
  279.1 14.0 %collective-permute-done.41 = bf16[128,2048]{1,0:T(8,128)(2,1)S(1)} collective-permute-done((bf16[128,2048]{1,0:T(8,128)(2,1)S(1)}, bf16[128,2048]{1,0:T(8,128)(2,1)S(1)}, u32[]{:S(2)}, u32[]{:S(2)}) %collective-permute-start.41) | collective-permute-done | bytes 524320 | tf_op jit(solution)/shard_map/ppermute | solution.py:28
  (163 shorter events, 44.3 us)
Async XLA Ops:
  6.5 234.0 %all-gather.2.cloned.1.call-start = ((), (), s32[]{:S(2)}) async-start(), calls=%async_computation | async-start | bytes 1310720 | tf_op jit(solution)/shard_map/all_gather | solution.py:52
  7.7 18.1 %collective-permute-start = (bf16[128,2048]{1,0:T(8,128)(2,1)S(1)}, bf16[128,2048]{1,0:T(8,128)(2,1)S(1)}, u32[]{:S(2)}, u32[]{:S(2)}) collective-permute-start(bf16[128,2048]{1,0:T(8,128)(2,1)S(1)} %slice.107.refs_0_), channel_id=1, source_target_pairs={{0,2},{1,3},{2,4},{3,5},{4,6},{5,7},{6,0},{7,1},{8,10},{9,11},{10,... | collective-permute-start | bytes 1572872 | tf_op jit(solution)/shard_map/ppermute | solution.py:28
  10.8 31.0 %collective-permute-start.2 = (bf16[256,2048]{1,0:T(8,128)(2,1)}, bf16[256,2048]{1,0:T(8,128)(2,1)}, u32[]{:S(2)}, u32[]{:S(2)}) collective-permute-start(bf16[256,2048]{1,0:T(8,128)(2,1)} %param.16), channel_id=1, source_target_pairs={{0,8},{1,9},{2,10},{3,11},{4,12},{5,13},{6,14},{7,15},{8,0},{9,1},... | collective-permute-start | bytes 3145736 | tf_op jit(solution)/shard_map/ppermute | solution.py:43
  12.3 29.5 %collective-permute-start.3 = (bf16[256,2048]{1,0:T(8,128)(2,1)}, bf16[256,2048]{1,0:T(8,128)(2,1)}, u32[]{:S(2)}, u32[]{:S(2)}) collective-permute-start(bf16[256,2048]{1,0:T(8,128)(2,1)} %param.17), channel_id=1, source_target_pairs={{0,16},{1,17},{2,18},{3,19},{4,20},{5,21},{6,22},{7,23},{8,24},{9,... | collective-permute-start | bytes 3145736 | tf_op jit(solution)/shard_map/ppermute | solution.py:43
  13.8 36.9 %collective-permute-start.34 = (bf16[64,2048]{1,0:T(8,128)(2,1)}, bf16[64,2048]{1,0:T(8,128)(2,1)S(1)}, u32[]{:S(2)}, u32[]{:S(2)}) collective-permute-start(bf16[64,2048]{1,0:T(8,128)(2,1)} %param.15), channel_id=1, source_target_pairs={{0,0},{1,8},{2,16},{3,24},{4,1},{5,9},{6,17},{7,25},{8,2},{9,10},{... | collective-permute-start | bytes 786440 | tf_op jit(solution)/shard_map/ppermute | solution.py:211
  25.8 16.0 %collective-permute-start.1 = (bf16[128,2048]{1,0:T(8,128)(2,1)S(1)}, bf16[128,2048]{1,0:T(8,128)(2,1)S(1)}, u32[]{:S(2)}, u32[]{:S(2)}) collective-permute-start(bf16[128,2048]{1,0:T(8,128)(2,1)S(1)} %collective-permute-done.refs_1_), channel_id=1, source_target_pairs={{0,2},{1,3},{2,4},{3,5},{4,6},{5,7},{6,0},{7,1},{8,10},{9,11},{10,... | collective-permute-start | bytes 1572872 | tf_op jit(solution)/shard_map/ppermute | solution.py:28
  41.8 28.3 %collective-permute-start.4 = (bf16[256,2048]{1,0:T(8,128)(2,1)}, bf16[256,2048]{1,0:T(8,128)(2,1)}, u32[]{:S(2)}, u32[]{:S(2)}) collective-permute-start(bf16[256,2048]{1,0:T(8,128)(2,1)} %param.16), channel_id=1, source_target_pairs={{0,16},{1,17},{2,18},{3,19},{4,20},{5,21},{6,22},{7,23},{8,24},{9,... | collective-permute-start | bytes 3145736 | tf_op jit(solution)/shard_map/ppermute | solution.py:43
  43.2 47.2 %collective-permute-start.5 = (bf16[256,2048]{1,0:T(8,128)(2,1)}, bf16[256,2048]{1,0:T(8,128)(2,1)}, u32[]{:S(2)}, u32[]{:S(2)}) collective-permute-start(bf16[256,2048]{1,0:T(8,128)(2,1)} %collective-permute-done.2), channel_id=1, source_target_pairs={{0,16},{1,17},{2,18},{3,19},{4,20},{5,21},{6,22},{7,23},{8,24},{9,... | collective-permute-start | bytes 3145736 | tf_op jit(solution)/shard_map/ppermute | solution.py:43
  43.9 46.5 %collective-permute-start.6 = (bf16[256,2048]{1,0:T(8,128)(2,1)}, bf16[256,2048]{1,0:T(8,128)(2,1)}, u32[]{:S(2)}, u32[]{:S(2)}) collective-permute-start(bf16[256,2048]{1,0:T(8,128)(2,1)} %param.17), channel_id=1, source_target_pairs={{0,8},{1,9},{2,10},{3,11},{4,12},{5,13},{6,14},{7,15},{8,0},{9,1},... | collective-permute-start | bytes 3145736 | tf_op jit(solution)/shard_map/ppermute | solution.py:43
  49.2 43.7 %collective-permute-start.7 = (bf16[256,2048]{1,0:T(8,128)(2,1)}, bf16[256,2048]{1,0:T(8,128)(2,1)}, u32[]{:S(2)}, u32[]{:S(2)}) collective-permute-start(bf16[256,2048]{1,0:T(8,128)(2,1)} %collective-permute-done.3), channel_id=1, source_target_pairs={{0,8},{1,9},{2,10},{3,11},{4,12},{5,13},{6,14},{7,15},{8,0},{9,1},... | collective-permute-start | bytes 3145736 | tf_op jit(solution)/shard_map/ppermute | solution.py:43
  50.7 19.4 %collective-permute-start.8 = (bf16[128,2048]{1,0:T(8,128)(2,1)}, bf16[128,2048]{1,0:T(8,128)(2,1)}, u32[]{:S(2)}, u32[]{:S(2)}) collective-permute-start(bf16[128,2048]{1,0:T(8,128)(2,1)} %copy-done.5), channel_id=1, source_target_pairs={{0,2},{1,3},{2,4},{3,5},{4,6},{5,7},{6,0},{7,1},{8,10},{9,11},{10,... | collective-permute-start | bytes 1572872 | tf_op jit(solution)/shard_map/ppermute | solution.py:28
  70.1 28.0 %collective-permute-start.9 = (bf16[128,2048]{1,0:T(8,128)(2,1)S(1)}, bf16[128,2048]{1,0:T(8,128)(2,1)}, u32[]{:S(2)}, u32[]{:S(2)}) collective-permute-start(bf16[128,2048]{1,0:T(8,128)(2,1)S(1)} %slice.107.refs_0_), channel_id=1, source_target_pairs={{0,1},{1,0},{2,3},{3,2},{4,5},{5,4},{6,7},{7,6},{8,9},{9,8},{10,11... | collective-permute-start | bytes 1572872 | tf_op jit(solution)/shard_map/ppermute | solution.py:21
  70.1 28.0 %collective-permute-start.10 = (bf16[128,2048]{1,0:T(8,128)(2,1)S(1)}, bf16[128,2048]{1,0:T(8,128)(2,1)}, u32[]{:S(2)}, u32[]{:S(2)}) collective-permute-start(bf16[128,2048]{1,0:T(8,128)(2,1)S(1)} %collective-permute-done.refs_1_), channel_id=1, source_target_pairs={{0,1},{1,0},{2,3},{3,2},{4,5},{5,4},{6,7},{7,6},{8,9},{9,8},{10,11... | collective-permute-start | bytes 1572872 | tf_op jit(solution)/shard_map/ppermute | solution.py:21
  92.9 79.9 %collective-permute-start.28 = (bf16[128,2048]{1,0:T(8,128)(2,1)}, bf16[128,2048]{1,0:T(8,128)(2,1)}, u32[]{:S(2)}, u32[]{:S(2)}) collective-permute-start(bf16[128,2048]{1,0:T(8,128)(2,1)} %fusion.4), channel_id=1, source_target_pairs={{0,2},{1,3},{2,4},{3,5},{4,6},{5,7},{6,0},{7,1},{8,10},{9,11},{10,... | collective-permute-start | bytes 1572872 | tf_op jit(solution)/shard_map/ppermute | solution.py:28
  98.1 46.4 %collective-permute-start.27 = (bf16[128,2048]{1,0:T(8,128)(2,1)}, bf16[128,2048]{1,0:T(8,128)(2,1)S(1)}, u32[]{:S(2)}, u32[]{:S(2)}) collective-permute-start(bf16[128,2048]{1,0:T(8,128)(2,1)} %fusion.4), channel_id=1, source_target_pairs={{0,1},{1,0},{2,3},{3,2},{4,5},{5,4},{6,7},{7,6},{8,9},{9,8},{10,11... | collective-permute-start | bytes 1572872 | tf_op jit(solution)/shard_map/ppermute | solution.py:21
  107.8 65.1 %collective-permute-start.13 = (f32[1,1024]{1,0:T(1,128)S(1)}, f32[1,1024]{1,0:T(1,128)S(1)}, u32[]{:S(2)}, u32[]{:S(2)}) collective-permute-start(f32[1,1024]{1,0:T(1,128)S(1)} %slice_bitcast_fusion.7), channel_id=1, source_target_pairs={{0,1},{1,0},{2,3},{3,2},{4,5},{5,4},{6,7},{7,6},{8,9},{9,8},{10,11... | collective-permute-start | bytes 12296 | tf_op jit(solution)/shard_map/ppermute | solution.py:21
  115.7 52.5 %collective-permute-start.14 = (f32[1,1024]{1,0:T(1,128)S(1)}, f32[1,1024]{1,0:T(1,128)S(1)}, u32[]{:S(2)}, u32[]{:S(2)}) collective-permute-start(f32[1,1024]{1,0:T(1,128)S(1)} %slice_bitcast_fusion.6), channel_id=1, source_target_pairs={{0,1},{1,0},{2,3},{3,2},{4,5},{5,4},{6,7},{7,6},{8,9},{9,8},{10,11... | collective-permute-start | bytes 12296 | tf_op jit(solution)/shard_map/ppermute | solution.py:21
  124.6 39.6 %collective-permute-start.15 = (f32[1,1024]{1,0:T(1,128)S(1)}, f32[1,1024]{1,0:T(1,128)S(1)}, u32[]{:S(2)}, u32[]{:S(2)}) collective-permute-start(f32[1,1024]{1,0:T(1,128)S(1)} %slice_bitcast_fusion.5), channel_id=1, source_target_pairs={{0,1},{1,0},{2,3},{3,2},{4,5},{5,4},{6,7},{7,6},{8,9},{9,8},{10,11... | collective-permute-start | bytes 12296 | tf_op jit(solution)/shard_map/ppermute | solution.py:21
  164.2 69.1 %collective-permute-start.20 = (bf16[256,1024]{1,0:T(8,128)(2,1)}, bf16[256,1024]{1,0:T(8,128)(2,1)}, u32[]{:S(2)}, u32[]{:S(2)}) collective-permute-start(bf16[256,1024]{1,0:T(8,128)(2,1)} %slice_bitcast_fusion.3), channel_id=1, source_target_pairs={{0,1},{1,0},{2,3},{3,2},{4,5},{5,4},{6,7},{7,6},{8,9},{9,8},{10,11... | collective-permute-start | bytes 1572872 | tf_op jit(solution)/shard_map/ppermute | solution.py:21
  172.8 26.9 %collective-permute-start.22 = (bf16[256,1024]{1,0:T(8,128)(2,1)}, bf16[256,1024]{1,0:T(8,128)(2,1)}, u32[]{:S(2)}, u32[]{:S(2)}) collective-permute-start(bf16[256,1024]{1,0:T(8,128)(2,1)} %slice_bitcast_fusion.1), channel_id=1, source_target_pairs={{0,1},{1,0},{2,3},{3,2},{4,5},{5,4},{6,7},{7,6},{8,9},{9,8},{10,11... | collective-permute-start | bytes 1572872 | tf_op jit(solution)/shard_map/ppermute | solution.py:21
  172.9 17.0 %collective-permute-start.30 = (bf16[128,2048]{1,0:T(8,128)(2,1)}, bf16[128,2048]{1,0:T(8,128)(2,1)}, u32[]{:S(2)}, u32[]{:S(2)}) collective-permute-start(bf16[128,2048]{1,0:T(8,128)(2,1)} %collective-permute-done.28), channel_id=1, source_target_pairs={{0,2},{1,3},{2,4},{3,5},{4,6},{5,7},{6,0},{7,1},{8,10},{9,11},{10,... | collective-permute-start | bytes 1572872 | tf_op jit(solution)/shard_map/ppermute | solution.py:28
  178.5 22.5 %collective-permute-start.24 = (bf16[256,1024]{1,0:T(8,128)(2,1)S(1)}, bf16[256,1024]{1,0:T(8,128)(2,1)S(1)}, u32[]{:S(2)}, u32[]{:S(2)}) collective-permute-start(bf16[256,1024]{1,0:T(8,128)(2,1)S(1)} %fusion.49), channel_id=1, source_target_pairs={{0,2},{1,3},{2,4},{3,5},{4,6},{5,7},{6,0},{7,1},{8,10},{9,11},{10,... | collective-permute-start | bytes 1572872 | tf_op jit(solution)/shard_map/ppermute | solution.py:28
  189.9 22.5 %collective-permute-start.32 = (bf16[128,2048]{1,0:T(8,128)(2,1)}, bf16[128,2048]{1,0:T(8,128)(2,1)}, u32[]{:S(2)}, u32[]{:S(2)}) collective-permute-start(bf16[128,2048]{1,0:T(8,128)(2,1)} %collective-permute-done.30), channel_id=1, source_target_pairs={{0,2},{1,3},{2,4},{3,5},{4,6},{5,7},{6,0},{7,1},{8,10},{9,11},{10,... | collective-permute-start | bytes 1572872 | tf_op jit(solution)/shard_map/ppermute | solution.py:28
  189.9 22.5 %collective-permute-start.31 = (bf16[128,2048]{1,0:T(8,128)(2,1)}, bf16[128,2048]{1,0:T(8,128)(2,1)}, u32[]{:S(2)}, u32[]{:S(2)}) collective-permute-start(bf16[128,2048]{1,0:T(8,128)(2,1)} %collective-permute-done.30), channel_id=1, source_target_pairs={{0,1},{1,0},{2,3},{3,2},{4,5},{5,4},{6,7},{7,6},{8,9},{9,8},{10,11... | collective-permute-start | bytes 1572872 | tf_op jit(solution)/shard_map/ppermute | solution.py:21
  199.7 22.3 %collective-permute-start.21 = (bf16[256,1024]{1,0:T(8,128)(2,1)S(1)}, bf16[256,1024]{1,0:T(8,128)(2,1)S(1)}, u32[]{:S(2)}, u32[]{:S(2)}) collective-permute-start(bf16[256,1024]{1,0:T(8,128)(2,1)S(1)} %copy-done.23), channel_id=1, source_target_pairs={{0,1},{1,0},{2,3},{3,2},{4,5},{5,4},{6,7},{7,6},{8,9},{9,8},{10,11... | collective-permute-start | bytes 1572872 | tf_op jit(solution)/shard_map/ppermute | solution.py:21
  202.3 20.9 %collective-permute-start.25 = (bf16[256,1024]{1,0:T(8,128)(2,1)S(1)}, bf16[256,1024]{1,0:T(8,128)(2,1)S(1)}, u32[]{:S(2)}, u32[]{:S(2)}) collective-permute-start(bf16[256,1024]{1,0:T(8,128)(2,1)S(1)} %fusion.52), channel_id=1, source_target_pairs={{0,2},{1,3},{2,4},{3,5},{4,6},{5,7},{6,0},{7,1},{8,10},{9,11},{10,... | collective-permute-start | bytes 1572872 | tf_op jit(solution)/shard_map/ppermute | solution.py:28
  223.5 15.5 %collective-permute-start.26 = (bf16[256,1024]{1,0:T(8,128)(2,1)S(1)}, bf16[256,1024]{1,0:T(8,128)(2,1)S(1)}, u32[]{:S(2)}, u32[]{:S(2)}) collective-permute-start(bf16[256,1024]{1,0:T(8,128)(2,1)S(1)} %fusion.55), channel_id=1, source_target_pairs={{0,2},{1,3},{2,4},{3,5},{4,6},{5,7},{6,0},{7,1},{8,10},{9,11},{10,... | collective-permute-start | bytes 1572872 | tf_op jit(solution)/shard_map/ppermute | solution.py:28
  247.7 15.8 %collective-permute-start.39 = (bf16[128,2048]{1,0:T(8,128)(2,1)S(1)}, bf16[128,2048]{1,0:T(8,128)(2,1)S(1)}, u32[]{:S(2)}, u32[]{:S(2)}) collective-permute-start(bf16[128,2048]{1,0:T(8,128)(2,1)S(1)} %fusion.20), channel_id=1, source_target_pairs={{0,2},{1,3},{2,4},{3,5},{4,6},{5,7},{6,0},{7,1},{8,10},{9,11},{10,... | collective-permute-start | bytes 1572872 | tf_op jit(solution)/shard_map/ppermute | solution.py:28
  247.7 16.2 %collective-permute-start.36 = (bf16[128,2048]{1,0:T(8,128)(2,1)S(1)}, bf16[128,2048]{1,0:T(8,128)(2,1)S(1)}, u32[]{:S(2)}, u32[]{:S(2)}) collective-permute-start(bf16[128,2048]{1,0:T(8,128)(2,1)S(1)} %get-tuple-element.72), channel_id=1, source_target_pairs={{0,1},{1,0},{2,3},{3,2},{4,5},{5,4},{6,7},{7,6},{8,9},{9,8},{10,11... | collective-permute-start | bytes 1572872 | tf_op jit(solution)/shard_map/ppermute | solution.py:21
  263.8 15.0 %collective-permute-start.40 = (bf16[128,2048]{1,0:T(8,128)(2,1)S(1)}, bf16[128,2048]{1,0:T(8,128)(2,1)S(1)}, u32[]{:S(2)}, u32[]{:S(2)}) collective-permute-start(bf16[128,2048]{1,0:T(8,128)(2,1)S(1)} %fusion.24), channel_id=1, source_target_pairs={{0,2},{1,3},{2,4},{3,5},{4,6},{5,7},{6,0},{7,1},{8,10},{9,11},{10,... | collective-permute-start | bytes 1572872 | tf_op jit(solution)/shard_map/ppermute | solution.py:28
  263.8 15.3 %collective-permute-start.35 = (bf16[128,2048]{1,0:T(8,128)(2,1)S(1)}, bf16[128,2048]{1,0:T(8,128)(2,1)S(1)}, u32[]{:S(2)}, u32[]{:S(2)}) collective-permute-start(bf16[128,2048]{1,0:T(8,128)(2,1)S(1)} %get-tuple-element.69), channel_id=1, source_target_pairs={{0,1},{1,0},{2,3},{3,2},{4,5},{5,4},{6,7},{7,6},{8,9},{9,8},{10,11... | collective-permute-start | bytes 1572872 | tf_op jit(solution)/shard_map/ppermute | solution.py:21
  279.0 14.1 %collective-permute-start.41 = (bf16[128,2048]{1,0:T(8,128)(2,1)S(1)}, bf16[128,2048]{1,0:T(8,128)(2,1)S(1)}, u32[]{:S(2)}, u32[]{:S(2)}) collective-permute-start(bf16[128,2048]{1,0:T(8,128)(2,1)S(1)} %fusion.28), channel_id=1, source_target_pairs={{0,2},{1,3},{2,4},{3,5},{4,6},{5,7},{6,0},{7,1},{8,10},{9,11},{10,... | collective-permute-start | bytes 1572872 | tf_op jit(solution)/shard_map/ppermute | solution.py:28
  (38 other events, 507.4 us)
Sparse Core Ops, SparseCore 0:
  91.2 35.3 all-gather.1

commit v4 on v3

--- a/solution.py
+++ b/solution.py
@@ -26,13 +26,6 @@
         (k, k - k % SPAN + (k % SPAN + CORES) % SPAN) for k in range(lax.axis_size("kv"))
     ]
     return lax.ppermute(value, "kv", pairs)
-
-
-def gather_ring(value):
-    pieces = [value]
-    for _ in range(CHIPS - 1):
-        pieces.append(next_chip(pieces[-1]))
-    return pieces
 
 
 def widen(pieces, bit):
@@ -157,6 +150,45 @@
     )(meta, *pieces, key_cache, value_cache, projections, projections, bias)
 
 
+def units_kernel(rows, up, down, out):
+    unit_count = up.shape[0]
+    block = min(256, unit_count)
+    total = jnp.zeros(out.shape, F32)
+    for first in range(0, unit_count, block):
+        gates = lax.dot_general(
+            rows[...],
+            up[first : first + block, :],
+            (((1,), (1,)), ((), ())),
+            preferred_element_type=F32,
+        )
+        hidden = (gates * 0.5 * (1.0 + lax.erf(gates * (0.5**0.5)))).astype(BF16)
+        total = total + jnp.dot(
+            hidden, down[first : first + block, :], preferred_element_type=F32
+        )
+    out[...] = total
+
+
+def all_units(rows, up_rows, down_rows):
+    row_count, width = rows.shape
+    unit_count = up_rows.shape[0]
+    block = min(256, row_count)
+    weights = pl.BlockSpec((unit_count, width), lambda i: (0, 0), pipeline_mode=pl.Buffered(1))
+    rows_spec = pl.BlockSpec((block, width), lambda i: (i, 0))
+    return pl.pallas_call(
+        units_kernel,
+        grid=(row_count // block,),
+        in_specs=[rows_spec, weights, weights],
+        out_specs=rows_spec,
+        out_shape=jax.ShapeDtypeStruct((row_count, width), F32),
+        compiler_params=pltpu.CompilerParams(vmem_limit_bytes=40 * 2**20),
+        cost_estimate=pl.CostEstimate(
+            flops=4 * row_count * width * unit_count,
+            bytes_accessed=20 * 2**20,
+            transcendentals=row_count * unit_count,
+        ),
+    )(rows, up_rows, down_rows)
+
+
 def merge(parts):
     largest = parts[0][1]
     for part in parts[1:]:
@@ -196,11 +228,12 @@
         q_mine.append(next_chip(q_mine[-1]))
     up_pieces = widen(up_pieces, bits[0])
     down_pieces = widen(down_pieces, bits[-1])
-    q_mine[-1], up_pieces, down_pieces = lax.optimization_barrier(
-        (q_mine[-1], up_pieces, down_pieces)
+    q_other = [swap_cores(piece) for piece in q_mine[:-1]]
+    q_mine[-1], q_other, up_pieces, down_pieces = lax.optimization_barrier(
+        (q_mine[-1], q_other, up_pieces, down_pieces)
     )
     q_mine.append(next_chip(q_mine[-1]))
-    q_other = [swap_cores(piece) for piece in q_mine]
+    q_other += [swap_cores(piece) for piece in q_mine[-2:]]
     for bit in bits[1:]:
         up_pieces = widen(up_pieces, bit)
     for bit in reversed(bits[:-1]):
@@ -216,8 +249,8 @@
     bias = bias.astype(F32)
 
     normed, _ = lax.optimization_barrier((layer_norm(stream, norm_gain), q_mine[-1]))
-    rows_mine = gather_ring(normed)
-    rows_other = [swap_cores(piece) for piece in rows_mine]
+    rows_mine = [normed, next_chip(normed)]
+    rows_other = [swap_cores(normed)]
 
     carried = None
     for phase in range(CHIPS):
@@ -225,11 +258,13 @@
         kept = CORES * target + core
         given = CORES * target + 1 - core
         meta = jnp.stack([kept, given, core, member]).astype(jnp.int32)
-        if phase == CHIPS - 1:
-            meta, up_pieces, down_pieces = lax.optimization_barrier(
-                (meta, up_pieces, down_pieces)
-            )
+        if phase % 2 == 1:
+            meta, rows_mine, rows_other = lax.optimization_barrier((meta, rows_mine, rows_other))
+            rows_mine.append(next_chip(rows_mine[-1]))
+            rows_other.append(swap_cores(rows_mine[-2]))
         out, lse = attend(meta, q_mine + q_other, key_cache, value_cache, projections, bias)
+        if phase == CHIPS - 2:
+            out, up_pieces, down_pieces = lax.optimization_barrier((out, up_pieces, down_pieces))
         parts = [(out[0], lse[0]), swap_cores((out[1], lse[1]))]
         if carried is not None:
             parts.append(carried)
@@ -238,16 +273,9 @@
             carried = next_chip(carried)
     up_rows = jnp.concatenate([up_pieces[i] for i in range(request_count)], 0)
     down_rows = jnp.concatenate([down_pieces[i] for i in range(request_count)], 0)
-    units = []
-    for step in range(CHIPS):
-        gates = lax.dot_general(
-            jnp.concatenate([rows_mine[step], rows_other[step]], 0),
-            up_rows,
-            (((1,), (1,)), ((), ())),
-            preferred_element_type=F32,
-        )
-        hidden = jax.nn.gelu(gates, approximate=False).astype(BF16)
-        units.append(jnp.dot(hidden, down_rows, preferred_element_type=F32))
+    rows_other += [swap_cores(piece) for piece in rows_mine[len(rows_other) :]]
+    rows = jnp.concatenate(rows_mine + rows_other, 0)
+    units = all_units(rows, up_rows, down_rows)
     attention, units = lax.optimization_barrier((carried[0], units))
 
     half = CHIPS * token_count
@@ -266,15 +294,19 @@
             block, out_rows, (((0,), (0,)), ((), ())), preferred_element_type=F32
         )
 
+    def units_of(offset, step):
+        first = offset + step * token_count
+        return units[first : first + token_count]
+
     given, kept = branch(half), branch(0)
     received = []
     for phase, step in enumerate(order):
         rows = slice(phase * token_count, (phase + 1) * token_count)
-        received.append(swap_cores((given[rows] + units[step][token_count:]).astype(BF16)))
+        received.append(swap_cores((given[rows] + units_of(half, step)).astype(BF16)))
     running = None
     for phase, step in enumerate(order):
         rows = slice(phase * token_count, (phase + 1) * token_count)
-        total = kept[rows] + units[step][:token_count] + received[phase].astype(F32)
+        total = kept[rows] + units_of(0, step) + received[phase].astype(F32)
         if running is not None:
             total = total + running.astype(F32)
         running = total

time: 305 us -> 269 us (0.88); the launches traced: 302 us -> 269 us
  matrix products: 41.7 us -> 2.85 us
  waiting for transfers between devices: 145 us -> 122 us
  starting transfers between devices: 32.3 us -> 51.5 us
  Pallas kernels: 30.1 us -> 43.4 us
  local copies, waits for them, and re-layouts: 24.4 us -> 14.4 us
  other arithmetic: 13.4 us -> 19.9 us
    dot_general x4 -> x0, matrix products: 38.9 us -> none  [on_device(): units.append(jnp.dot(hidden, down_rows, preferred_element_type=F32))]
    ppermute x6, starting transfers between devices: 10.4 us -> 25.9 us  [widen(): found[index | 1 << bit] = lax.ppermute(piece, ('req', 'kv'), pairs)]
    pallas_call x0 -> x1, Pallas kernels: none -> 14.3 us  [all_units(): pl.pallas_call(units_kernel, grid=(row_count // block,), in_specs=[rows_s...]
    ppermute x15, waiting for transfers between devices: 122 us -> 109 us  [next_chip(): return lax.ppermute(value, 'kv', pairs)]
    ppermute x6, waiting for transfers between devices: 21.6 us -> 12.8 us  [widen(): found[index | 1 << bit] = lax.ppermute(piece, ('req', 'kv'), pairs)]
    concatenate x0 -> x2, other arithmetic: none -> 7.5 us  [the longest x1 5.68 us: on_device(): jnp.concatenate([down_pieces[i] for i in range(request_count)], 0)]
    unnamed x60 -> x53, local copies, waits for them, and re-layouts: 17 us -> 11.4 us
    ppermute x15, starting transfers between devices: 16.4 us -> 21.3 us  [next_chip(): return lax.ppermute(value, 'kv', pairs)]
  transfers between devices with their start and end apart: 43 -> 43, of which waited for: 18 -> 15; matrix products, arithmetic and copies ran while one was open for 22% -> 9% of each run, Pallas kernels for 10% -> 16%
where the time goes in v4:
time: 269 us
  waiting for transfers between devices  122 us (45%)
  starting transfers between devices  51.5 us (19%)
  Pallas kernels  43.4 us (16%)
  other arithmetic  19.9 us (7%)
  local copies, waits for them, and re-layouts  14.4 us (5%)
  between operations  14.1 us (5%)
  matrix products  2.85 us (1%)
    ppermute x15, waiting for transfers between devices, next_chip(): return lax.ppermute(value, 'kv', pairs)  109 us
    pallas_call x4, Pallas kernels, attend(): pl.pallas_call(attend_kernel, grid_spec=pltpu.PrefetchScalarGridSpec(num_...  29.1 us
    ppermute x6, starting transfers between devices, widen(): found[index | 1 << bit] = lax.ppermute(piece, ('req', 'kv'), pairs)  25.9 us
    ppermute x15, starting transfers between devices, next_chip(): return lax.ppermute(value, 'kv', pairs)  21.3 us
    pallas_call x1, Pallas kernels, all_units(): pl.pallas_call(units_kernel, grid=(row_count // block,), in_specs=[rows_s...  14.3 us
    ppermute x6, waiting for transfers between devices, widen(): found[index | 1 << bit] = lax.ppermute(piece, ('req', 'kv'), pairs)  12.8 us
    unnamed x53, local copies, waits for them, and re-layouts  11.4 us
    concatenate x1, other arithmetic, on_device(): jnp.concatenate([down_pieces[i] for i in range(request_count)], 0)  5.68 us
  transfers between devices with their start and end apart: 43, of which 15 were waited for; matrix products, arithmetic and copies ran while one was open for 9% of the time, Pallas kernels for 16%

profile of v4, /device:TPU:0, one launch (start us, length us, event | category | flops | bytes accessed | tf_op | source)
XLA Modules:
  0.0 268.7 jit_solution(16315270235413414557)
XLA Ops:
  7.7 3.1 %collective-permute-start = (bf16[128,2048]{1,0:T(8,128)(2,1)S(1)}, bf16[128,2048]{1,0:T(8,128)(2,1)S(1)}, u32[]{:S(2)}, u32[]{:S(2)}) collective-permute-start(bf16[128,2048]{1,0:T(8,128)(2,1)S(1)} %slice.107.refs_0_), channel_id=1, source_target_pairs={{0,2},{1,3},{2,4},{3,5},{4,6},{5,7},{6,0},{7,1},{8,10},{9,11},{10,... | collective-permute-start | bytes 1572872 | tf_op jit(solution)/shard_map/ppermute | solution.py:28
  10.8 1.5 collective-permute-start.4
  12.3 1.5 collective-permute-start.5
  15.0 9.7 %collective-permute-done.refs_1_ = bf16[128,2048]{1,0:T(8,128)(2,1)S(1)} collective-permute-done((bf16[128,2048]{1,0:T(8,128)(2,1)S(1)}, bf16[128,2048]{1,0:T(8,128)(2,1)S(1)}, u32[]{:S(2)}, u32[]{:S(2)}) %collective-permute-start) | collective-permute-done | bytes 524320 | tf_op jit(solution)/shard_map/ppermute | solution.py:28
  26.1 1.6 collective-permute-start.34
  27.8 14.0 %collective-permute-done.1.refs_2_ = bf16[128,2048]{1,0:T(8,128)(2,1)} collective-permute-done((bf16[128,2048]{1,0:T(8,128)(2,1)S(1)}, bf16[128,2048]{1,0:T(8,128)(2,1)}, u32[]{:S(2)}, u32[]{:S(2)}) %collective-permute-start.1) | collective-permute-done | bytes 524320 | tf_op jit(solution)/shard_map/ppermute | solution.py:28
  42.7 2.2 fusion.4
  44.9 11.9 %collective-permute-done.6.refs_3_ = bf16[128,2048]{1,0:T(8,128)(2,1)} collective-permute-done((bf16[128,2048]{1,0:T(8,128)(2,1)}, bf16[128,2048]{1,0:T(8,128)(2,1)}, u32[]{:S(2)}, u32[]{:S(2)}) %collective-permute-start.6) | collective-permute-done | bytes 524320 | tf_op jit(solution)/shard_map/ppermute | solution.py:28
  57.6 1.4 fusion.34.refs_12_
  60.5 20.7 %collective-permute-start.21 = (bf16[256,2048]{1,0:T(8,128)(2,1)}, bf16[256,2048]{1,0:T(8,128)(2,1)S(1)}, u32[]{:S(2)}, u32[]{:S(2)}) collective-permute-start(bf16[256,2048]{1,0:T(8,128)(2,1)} %param.16), channel_id=1, source_target_pairs={{0,16},{1,17},{2,18},{3,19},{4,20},{5,21},{6,22},{7,23},{8,24},{9,... | collective-permute-start | bytes 3145736 | tf_op jit(solution)/shard_map/ppermute | solution.py:36
  81.3 1.6 collective-permute-start.23
  82.9 2.3 copy-done.3
  87.3 7.3 %shard_map.94 = (bf16[2,256,1024]{2,1,0:T(8,128)(2,1)S(1)}, f32[2,1,1024]{2,1,0:T(1,128)S(1)}) custom-call(s32[4]{0:T(128)S(1)} %get-tuple-element.113.meta, bf16[128,2048]{1,0:T(8,128)(2,1)S(1)} %slice.107.refs_0_, bf16[128,2048]{1,0:T(8,128)(2,1)S(1)} %collective-permute-done.refs_1_, bf16[128,2048]{1,0:T(8,128)(2,1)} %collective-permute-done.1.refs_2_, ...), custom_call_target="tpu_custom_call" | custom-call | flops 2415919104 | bytes 8388608 | tf_op jit(solution)/shard_map/pallas_call | solution.py:120
  95.1 7.3 %shard_map.93 = (bf16[2,256,1024]{2,1,0:T(8,128)(2,1)S(1)}, f32[2,1,1024]{2,1,0:T(1,128)S(1)}) custom-call(s32[4]{0:T(128)S(1)} %add_add_fusion.4.meta, bf16[128,2048]{1,0:T(8,128)(2,1)S(1)} %slice.107.refs_0_, bf16[128,2048]{1,0:T(8,128)(2,1)S(1)} %collective-permute-done.refs_1_, bf16[128,2048]{1,0:T(8,128)(2,1)} %collective-permute-done.1.refs_2_, ...), custom_call_target="tpu_custom_call" | custom-call | flops 2415919104 | bytes 8388608 | tf_op jit(solution)/shard_map/pallas_call | solution.py:120
  102.4 7.3 %shard_map.92 = (bf16[2,256,1024]{2,1,0:T(8,128)(2,1)S(1)}, f32[2,1,1024]{2,1,0:T(1,128)S(1)}) custom-call(s32[4]{0:T(128)S(1)} %get-tuple-element.112.meta, bf16[128,2048]{1,0:T(8,128)(2,1)S(1)} %slice.107.refs_0_, bf16[128,2048]{1,0:T(8,128)(2,1)S(1)} %collective-permute-done.refs_1_, bf16[128,2048]{1,0:T(8,128)(2,1)} %collective-permute-done.1.refs_2_, ...), custom_call_target="tpu_custom_call" | custom-call | flops 2415919104 | bytes 8388608 | tf_op jit(solution)/shard_map/pallas_call | solution.py:120
  110.6 9.1 %collective-permute-done.22 = bf16[256,2048]{1,0:T(8,128)(2,1)S(1)} collective-permute-done((bf16[256,2048]{1,0:T(8,128)(2,1)}, bf16[256,2048]{1,0:T(8,128)(2,1)S(1)}, u32[]{:S(2)}, u32[]{:S(2)}) %collective-permute-start.22) | collective-permute-done | bytes 1048608 | tf_op jit(solution)/shard_map/ppermute | solution.py:36
  120.3 3.7 %collective-permute-done.24 = bf16[256,2048]{1,0:T(8,128)(2,1)S(1)} collective-permute-done((bf16[256,2048]{1,0:T(8,128)(2,1)}, bf16[256,2048]{1,0:T(8,128)(2,1)S(1)}, u32[]{:S(2)}, u32[]{:S(2)}) %collective-permute-start.24) | collective-permute-done | bytes 1048608 | tf_op jit(solution)/shard_map/ppermute | solution.py:36
  124.9 1.8 pad_maximum_fusion.up
  126.8 5.7 %pad_maximum_fusion.1.down = bf16[1024,2048]{1,0:T(8,128)(2,1)S(1)} fusion(bf16[256,2048]{1,0:T(8,128)(2,1)} %copy-done.19, bf16[256,2048]{1,0:T(8,128)(2,1)} %collective-permute-done.5, bf16[256,2048]{1,0:T(8,128)(2,1)S(1)} %copy-done.18, bf16[256,2048]{1,0:T(8,128)(2,1)S(1)} %copy-done.16), kind=kLoop, calls=%fused_computation.1 | loop fusion | flops 16777216 | bytes 8388608 | tf_op jit(solution)/shard_map/concatenate | solution.py:275
  132.6 13.4 %collective-permute-start.17 = (f32[1,1024]{1,0:T(1,128)S(1)}, f32[1,1024]{1,0:T(1,128)S(1)}, u32[]{:S(2)}, u32[]{:S(2)}) collective-permute-start(f32[1,1024]{1,0:T(1,128)S(1)} %get-tuple-element.101), channel_id=1, source_target_pairs={{0,2},{1,3},{2,4},{3,5},{4,6},{5,7},{6,0},{7,1},{8,10},{9,11},{10,... | collective-permute-start | bytes 12296 | tf_op jit(solution)/shard_map/ppermute | solution.py:28
  147.3 2.3 collective-permute-start.18
  149.7 3.0 %collective-permute-done.18 = f32[1,1024]{1,0:T(1,128)S(1)} collective-permute-done((f32[1,1024]{1,0:T(1,128)S(1)}, f32[1,1024]{1,0:T(1,128)S(1)}, u32[]{:S(2)}, u32[]{:S(2)}) %collective-permute-start.18) | collective-permute-done | bytes 4128 | tf_op jit(solution)/shard_map/ppermute | solution.py:28
  153.9 7.3 %shard_map.91 = (bf16[2,256,1024]{2,1,0:T(8,128)(2,1)S(1)}, f32[2,1,1024]{2,1,0:T(1,128)S(1)}) custom-call(s32[4]{0:T(128)S(1)} %add_add_fusion.3.meta, bf16[128,2048]{1,0:T(8,128)(2,1)S(1)} %slice.107.refs_0_, bf16[128,2048]{1,0:T(8,128)(2,1)S(1)} %collective-permute-done.refs_1_, bf16[128,2048]{1,0:T(8,128)(2,1)} %collective-permute-done.1.refs_2_, ...), custom_call_target="tpu_custom_call" | custom-call | flops 2415919104 | bytes 8388608 | tf_op jit(solution)/shard_map/pallas_call | solution.py:120
  164.8 5.6 %collective-permute-done.28 = bf16[256,1024]{1,0:T(8,128)(2,1)S(1)} collective-permute-done((bf16[256,1024]{1,0:T(8,128)(2,1)S(1)}, bf16[256,1024]{1,0:T(8,128)(2,1)S(1)}, u32[]{:S(2)}, u32[]{:S(2)}) %collective-permute-start.28) | collective-permute-done | bytes 524320 | tf_op jit(solution)/shard_map/ppermute | solution.py:28
  170.8 10.8 %collective-permute-done.31 = bf16[128,2048]{1,0:T(8,128)(2,1)S(1)} collective-permute-done((bf16[128,2048]{1,0:T(8,128)(2,1)}, bf16[128,2048]{1,0:T(8,128)(2,1)S(1)}, u32[]{:S(2)}, u32[]{:S(2)}) %collective-permute-start.31) | collective-permute-done | bytes 524320 | tf_op jit(solution)/shard_map/ppermute | solution.py:28
  184.0 8.2 %collective-permute-done.29 = bf16[256,1024]{1,0:T(8,128)(2,1)S(1)} collective-permute-done((bf16[256,1024]{1,0:T(8,128)(2,1)S(1)}, bf16[256,1024]{1,0:T(8,128)(2,1)S(1)}, u32[]{:S(2)}, u32[]{:S(2)}) %collective-permute-start.29) | collective-permute-done | bytes 524320 | tf_op jit(solution)/shard_map/ppermute | solution.py:28
  192.6 14.3 %shard_map.95 = f32[1024,2048]{1,0:T(8,128)} custom-call(bf16[1024,2048]{1,0:T(8,128)(2,1)S(1)} %constant_dynamic-update-slice_fusion.rows, bf16[1024,2048]{1,0:T(8,128)(2,1)S(1)} %pad_maximum_fusion.up, bf16[1024,2048]{1,0:T(8,128)(2,1)S(1)} %pad_maximum_fusion.1.down), custom_call_target="tpu_custom_call" | custom-call | flops 8589934592 | bytes 20971520 | tf_op jit(solution)/shard_map/pallas_call | solution.py:177
  208.1 2.1 fusion.43
  210.3 2.9 %fusion.17 = (bf16[128,2048]{1,0:T(8,128)(2,1)S(1)}, bf16[128,2048]{1,0:T(8,128)(2,1)S(1)}, bf16[128,2048]{1,0:T(8,128)(2,1)S(1)}, bf16[128,2048]{1,0:T(8,128)(2,1)S(1)}) fusion(f32[512,2048]{1,0:T(8,128)S(1)} %fusion.43, f32[1024,2048]{1,0:T(8,128)} %shard_map.95), kind=kLoop, calls=%fused_computation.29 | loop fusion | flops 2097152 | bytes 10485760 | tf_op jit(solution)/shard_map/convert_element_type | solution.py:305
  216.3 14.8 %collective-permute-done.39 = bf16[128,2048]{1,0:T(8,128)(2,1)S(1)} collective-permute-done((bf16[128,2048]{1,0:T(8,128)(2,1)S(1)}, bf16[128,2048]{1,0:T(8,128)(2,1)S(1)}, u32[]{:S(2)}, u32[]{:S(2)}) %collective-permute-start.39) | collective-permute-done | bytes 524320 | tf_op jit(solution)/shard_map/ppermute | solution.py:28
  231.5 14.8 %collective-permute-done.40 = bf16[128,2048]{1,0:T(8,128)(2,1)S(1)} collective-permute-done((bf16[128,2048]{1,0:T(8,128)(2,1)S(1)}, bf16[128,2048]{1,0:T(8,128)(2,1)S(1)}, u32[]{:S(2)}, u32[]{:S(2)}) %collective-permute-start.40) | collective-permute-done | bytes 524320 | tf_op jit(solution)/shard_map/ppermute | solution.py:28
  246.7 14.0 %collective-permute-done.41 = bf16[128,2048]{1,0:T(8,128)(2,1)S(1)} collective-permute-done((bf16[128,2048]{1,0:T(8,128)(2,1)S(1)}, bf16[128,2048]{1,0:T(8,128)(2,1)S(1)}, u32[]{:S(2)}, u32[]{:S(2)}) %collective-permute-start.41) | collective-permute-done | bytes 524320 | tf_op jit(solution)/shard_map/ppermute | solution.py:28
  (156 shorter events, 27.4 us)
Async XLA Ops:
  6.5 201.6 %all-gather.2.cloned.1.call-start = ((), (), s32[]{:S(2)}) async-start(), calls=%async_computation | async-start | bytes 1310720 | tf_op jit(solution)/shard_map/all_gather | solution.py:45
  7.7 17.0 %collective-permute-start = (bf16[128,2048]{1,0:T(8,128)(2,1)S(1)}, bf16[128,2048]{1,0:T(8,128)(2,1)S(1)}, u32[]{:S(2)}, u32[]{:S(2)}) collective-permute-start(bf16[128,2048]{1,0:T(8,128)(2,1)S(1)} %slice.107.refs_0_), channel_id=1, source_target_pairs={{0,2},{1,3},{2,4},{3,5},{4,6},{5,7},{6,0},{7,1},{8,10},{9,11},{10,... | collective-permute-start | bytes 1572872 | tf_op jit(solution)/shard_map/ppermute | solution.py:28
  10.8 31.8 %collective-permute-start.4 = (bf16[256,2048]{1,0:T(8,128)(2,1)}, bf16[256,2048]{1,0:T(8,128)(2,1)}, u32[]{:S(2)}, u32[]{:S(2)}) collective-permute-start(bf16[256,2048]{1,0:T(8,128)(2,1)} %param.16), channel_id=1, source_target_pairs={{0,8},{1,9},{2,10},{3,11},{4,12},{5,13},{6,14},{7,15},{8,0},{9,1},... | collective-permute-start | bytes 3145736 | tf_op jit(solution)/shard_map/ppermute | solution.py:36
  12.3 30.3 %collective-permute-start.5 = (bf16[256,2048]{1,0:T(8,128)(2,1)}, bf16[256,2048]{1,0:T(8,128)(2,1)}, u32[]{:S(2)}, u32[]{:S(2)}) collective-permute-start(bf16[256,2048]{1,0:T(8,128)(2,1)} %param.17), channel_id=1, source_target_pairs={{0,16},{1,17},{2,18},{3,19},{4,20},{5,21},{6,22},{7,23},{8,24},{9,... | collective-permute-start | bytes 3145736 | tf_op jit(solution)/shard_map/ppermute | solution.py:36
  24.8 17.0 %collective-permute-start.1 = (bf16[128,2048]{1,0:T(8,128)(2,1)S(1)}, bf16[128,2048]{1,0:T(8,128)(2,1)}, u32[]{:S(2)}, u32[]{:S(2)}) collective-permute-start(bf16[128,2048]{1,0:T(8,128)(2,1)S(1)} %collective-permute-done.refs_1_), channel_id=1, source_target_pairs={{0,2},{1,3},{2,4},{3,5},{4,6},{5,7},{6,0},{7,1},{8,10},{9,11},{10,... | collective-permute-start | bytes 1572872 | tf_op jit(solution)/shard_map/ppermute | solution.py:28
  24.8 17.0 %collective-permute-start.3 = (bf16[128,2048]{1,0:T(8,128)(2,1)S(1)}, bf16[128,2048]{1,0:T(8,128)(2,1)S(1)}, u32[]{:S(2)}, u32[]{:S(2)}) collective-permute-start(bf16[128,2048]{1,0:T(8,128)(2,1)S(1)} %collective-permute-done.refs_1_), channel_id=1, source_target_pairs={{0,1},{1,0},{2,3},{3,2},{4,5},{5,4},{6,7},{7,6},{8,9},{9,8},{10,11... | collective-permute-start | bytes 1572872 | tf_op jit(solution)/shard_map/ppermute | solution.py:21
  26.1 33.6 %collective-permute-start.34 = (bf16[64,2048]{1,0:T(8,128)(2,1)}, bf16[64,2048]{1,0:T(8,128)(2,1)S(1)}, u32[]{:S(2)}, u32[]{:S(2)}) collective-permute-start(bf16[64,2048]{1,0:T(8,128)(2,1)} %param.15), channel_id=1, source_target_pairs={{0,0},{1,8},{2,16},{3,24},{4,1},{5,9},{6,17},{7,25},{8,2},{9,10},{... | collective-permute-start | bytes 786440 | tf_op jit(solution)/shard_map/ppermute | solution.py:244
  44.9 36.3 %collective-permute-start.11 = (bf16[128,2048]{1,0:T(8,128)(2,1)}, bf16[128,2048]{1,0:T(8,128)(2,1)}, u32[]{:S(2)}, u32[]{:S(2)}) collective-permute-start(bf16[128,2048]{1,0:T(8,128)(2,1)} %collective-permute-done.1.refs_2_), channel_id=1, source_target_pairs={{0,1},{1,0},{2,3},{3,2},{4,5},{5,4},{6,7},{7,6},{8,9},{9,8},{10,11... | collective-permute-start | bytes 1572872 | tf_op jit(solution)/shard_map/ppermute | solution.py:21
  56.8 24.5 %collective-permute-start.12 = (bf16[128,2048]{1,0:T(8,128)(2,1)}, bf16[128,2048]{1,0:T(8,128)(2,1)}, u32[]{:S(2)}, u32[]{:S(2)}) collective-permute-start(bf16[128,2048]{1,0:T(8,128)(2,1)} %collective-permute-done.6.refs_3_), channel_id=1, source_target_pairs={{0,1},{1,0},{2,3},{3,2},{4,5},{5,4},{6,7},{7,6},{8,9},{9,8},{10,11... | collective-permute-start | bytes 1572872 | tf_op jit(solution)/shard_map/ppermute | solution.py:21
  59.1 35.5 %collective-permute-start.7 = (bf16[128,2048]{1,0:T(8,128)(2,1)}, bf16[128,2048]{1,0:T(8,128)(2,1)}, u32[]{:S(2)}, u32[]{:S(2)}) collective-permute-start(bf16[128,2048]{1,0:T(8,128)(2,1)} %fusion.4), channel_id=1, source_target_pairs={{0,2},{1,3},{2,4},{3,5},{4,6},{5,7},{6,0},{7,1},{8,10},{9,11},{10,... | collective-permute-start | bytes 1572872 | tf_op jit(solution)/shard_map/ppermute | solution.py:28
  59.1 35.9 %collective-permute-start.8 = (bf16[128,2048]{1,0:T(8,128)(2,1)}, bf16[128,2048]{1,0:T(8,128)(2,1)}, u32[]{:S(2)}, u32[]{:S(2)}) collective-permute-start(bf16[128,2048]{1,0:T(8,128)(2,1)} %fusion.4), channel_id=1, source_target_pairs={{0,1},{1,0},{2,3},{3,2},{4,5},{5,4},{6,7},{7,6},{8,9},{9,8},{10,11... | collective-permute-start | bytes 1572872 | tf_op jit(solution)/shard_map/ppermute | solution.py:21
  60.5 50.1 %collective-permute-start.21 = (bf16[256,2048]{1,0:T(8,128)(2,1)}, bf16[256,2048]{1,0:T(8,128)(2,1)S(1)}, u32[]{:S(2)}, u32[]{:S(2)}) collective-permute-start(bf16[256,2048]{1,0:T(8,128)(2,1)} %param.16), channel_id=1, source_target_pairs={{0,16},{1,17},{2,18},{3,19},{4,20},{5,21},{6,22},{7,23},{8,24},{9,... | collective-permute-start | bytes 3145736 | tf_op jit(solution)/shard_map/ppermute | solution.py:36
  81.2 38.5 %collective-permute-start.22 = (bf16[256,2048]{1,0:T(8,128)(2,1)}, bf16[256,2048]{1,0:T(8,128)(2,1)S(1)}, u32[]{:S(2)}, u32[]{:S(2)}) collective-permute-start(bf16[256,2048]{1,0:T(8,128)(2,1)} %collective-permute-done.4), channel_id=1, source_target_pairs={{0,16},{1,17},{2,18},{3,19},{4,20},{5,21},{6,22},{7,23},{8,24},{9,... | collective-permute-start | bytes 3145736 | tf_op jit(solution)/shard_map/ppermute | solution.py:36
  81.3 38.4 %collective-permute-start.23 = (bf16[256,2048]{1,0:T(8,128)(2,1)}, bf16[256,2048]{1,0:T(8,128)(2,1)S(1)}, u32[]{:S(2)}, u32[]{:S(2)}) collective-permute-start(bf16[256,2048]{1,0:T(8,128)(2,1)} %param.17), channel_id=1, source_target_pairs={{0,8},{1,9},{2,10},{3,11},{4,12},{5,13},{6,14},{7,15},{8,0},{9,1},... | collective-permute-start | bytes 3145736 | tf_op jit(solution)/shard_map/ppermute | solution.py:36
  94.6 29.4 %collective-permute-start.24 = (bf16[256,2048]{1,0:T(8,128)(2,1)}, bf16[256,2048]{1,0:T(8,128)(2,1)S(1)}, u32[]{:S(2)}, u32[]{:S(2)}) collective-permute-start(bf16[256,2048]{1,0:T(8,128)(2,1)} %collective-permute-done.5), channel_id=1, source_target_pairs={{0,8},{1,9},{2,10},{3,11},{4,12},{5,13},{6,14},{7,15},{8,0},{9,1},... | collective-permute-start | bytes 3145736 | tf_op jit(solution)/shard_map/ppermute | solution.py:36
  95.0 58.5 %collective-permute-start.9 = (bf16[128,2048]{1,0:T(8,128)(2,1)}, bf16[128,2048]{1,0:T(8,128)(2,1)}, u32[]{:S(2)}, u32[]{:S(2)}) collective-permute-start(bf16[128,2048]{1,0:T(8,128)(2,1)} %collective-permute-done.7), channel_id=1, source_target_pairs={{0,2},{1,3},{2,4},{3,5},{4,6},{5,7},{6,0},{7,1},{8,10},{9,11},{10,... | collective-permute-start | bytes 1572872 | tf_op jit(solution)/shard_map/ppermute | solution.py:28
  110.6 43.3 %collective-permute-start.10 = (bf16[128,2048]{1,0:T(8,128)(2,1)}, bf16[128,2048]{1,0:T(8,128)(2,1)}, u32[]{:S(2)}, u32[]{:S(2)}) collective-permute-start(bf16[128,2048]{1,0:T(8,128)(2,1)} %collective-permute-done.7), channel_id=1, source_target_pairs={{0,1},{1,0},{2,3},{3,2},{4,5},{5,4},{6,7},{7,6},{8,9},{9,8},{10,11... | collective-permute-start | bytes 1572872 | tf_op jit(solution)/shard_map/ppermute | solution.py:21
  119.8 33.1 %collective-permute-start.27 = (bf16[256,1024]{1,0:T(8,128)(2,1)S(1)}, bf16[256,1024]{1,0:T(8,128)(2,1)S(1)}, u32[]{:S(2)}, u32[]{:S(2)}) collective-permute-start(bf16[256,1024]{1,0:T(8,128)(2,1)S(1)} %slice_bitcast_fusion), channel_id=1, source_target_pairs={{0,1},{1,0},{2,3},{3,2},{4,5},{5,4},{6,7},{7,6},{8,9},{9,8},{10,11... | collective-permute-start | bytes 1572872 | tf_op jit(solution)/shard_map/ppermute | solution.py:21
  123.9 22.0 %collective-permute-start.15 = (f32[1,1024]{1,0:T(1,128)S(1)}, f32[1,1024]{1,0:T(1,128)S(1)}, u32[]{:S(2)}, u32[]{:S(2)}) collective-permute-start(f32[1,1024]{1,0:T(1,128)S(1)} %slice_bitcast_fusion.5), channel_id=1, source_target_pairs={{0,1},{1,0},{2,3},{3,2},{4,5},{5,4},{6,7},{7,6},{8,9},{9,8},{10,11... | collective-permute-start | bytes 12296 | tf_op jit(solution)/shard_map/ppermute | solution.py:21
  132.6 14.7 %collective-permute-start.17 = (f32[1,1024]{1,0:T(1,128)S(1)}, f32[1,1024]{1,0:T(1,128)S(1)}, u32[]{:S(2)}, u32[]{:S(2)}) collective-permute-start(f32[1,1024]{1,0:T(1,128)S(1)} %get-tuple-element.101), channel_id=1, source_target_pairs={{0,2},{1,3},{2,4},{3,5},{4,6},{5,7},{6,0},{7,1},{8,10},{9,11},{10,... | collective-permute-start | bytes 12296 | tf_op jit(solution)/shard_map/ppermute | solution.py:28
  149.7 14.6 %collective-permute-start.26 = (bf16[256,1024]{1,0:T(8,128)(2,1)}, bf16[256,1024]{1,0:T(8,128)(2,1)S(1)}, u32[]{:S(2)}, u32[]{:S(2)}) collective-permute-start(bf16[256,1024]{1,0:T(8,128)(2,1)} %slice_bitcast_fusion.1), channel_id=1, source_target_pairs={{0,1},{1,0},{2,3},{3,2},{4,5},{5,4},{6,7},{7,6},{8,9},{9,8},{10,11... | collective-permute-start | bytes 1572872 | tf_op jit(solution)/shard_map/ppermute | solution.py:21
  152.7 31.3 %collective-permute-start.25 = (bf16[256,1024]{1,0:T(8,128)(2,1)S(1)}, bf16[256,1024]{1,0:T(8,128)(2,1)S(1)}, u32[]{:S(2)}, u32[]{:S(2)}) collective-permute-start(bf16[256,1024]{1,0:T(8,128)(2,1)S(1)} %slice_bitcast_fusion.2), channel_id=1, source_target_pairs={{0,1},{1,0},{2,3},{3,2},{4,5},{5,4},{6,7},{7,6},{8,9},{9,8},{10,11... | collective-permute-start | bytes 1572872 | tf_op jit(solution)/shard_map/ppermute | solution.py:21
  153.6 16.8 %collective-permute-start.28 = (bf16[256,1024]{1,0:T(8,128)(2,1)S(1)}, bf16[256,1024]{1,0:T(8,128)(2,1)S(1)}, u32[]{:S(2)}, u32[]{:S(2)}) collective-permute-start(bf16[256,1024]{1,0:T(8,128)(2,1)S(1)} %fusion.21), channel_id=1, source_target_pairs={{0,2},{1,3},{2,4},{3,5},{4,6},{5,7},{6,0},{7,1},{8,10},{9,11},{10,... | collective-permute-start | bytes 1572872 | tf_op jit(solution)/shard_map/ppermute | solution.py:28
  163.8 17.9 %collective-permute-start.31 = (bf16[128,2048]{1,0:T(8,128)(2,1)}, bf16[128,2048]{1,0:T(8,128)(2,1)S(1)}, u32[]{:S(2)}, u32[]{:S(2)}) collective-permute-start(bf16[128,2048]{1,0:T(8,128)(2,1)} %collective-permute-done.9), channel_id=1, source_target_pairs={{0,2},{1,3},{2,4},{3,5},{4,6},{5,7},{6,0},{7,1},{8,10},{9,11},{10,... | collective-permute-start | bytes 1572872 | tf_op jit(solution)/shard_map/ppermute | solution.py:28
  164.1 19.9 %collective-permute-start.32 = (bf16[128,2048]{1,0:T(8,128)(2,1)}, bf16[128,2048]{1,0:T(8,128)(2,1)S(1)}, u32[]{:S(2)}, u32[]{:S(2)}) collective-permute-start(bf16[128,2048]{1,0:T(8,128)(2,1)} %collective-permute-done.9), channel_id=1, source_target_pairs={{0,1},{1,0},{2,3},{3,2},{4,5},{5,4},{6,7},{7,6},{8,9},{9,8},{10,11... | collective-permute-start | bytes 1572872 | tf_op jit(solution)/shard_map/ppermute | solution.py:21
  164.3 42.6 %collective-permute-start.20 = (bf16[256,1024]{1,0:T(8,128)(2,1)S(1)}, bf16[256,1024]{1,0:T(8,128)(2,1)S(1)}, u32[]{:S(2)}, u32[]{:S(2)}) collective-permute-start(bf16[256,1024]{1,0:T(8,128)(2,1)S(1)} %slice_bitcast_fusion.3), channel_id=1, source_target_pairs={{0,1},{1,0},{2,3},{3,2},{4,5},{5,4},{6,7},{7,6},{8,9},{9,8},{10,11... | collective-permute-start | bytes 1572872 | tf_op jit(solution)/shard_map/ppermute | solution.py:21
  170.7 21.4 %collective-permute-start.29 = (bf16[256,1024]{1,0:T(8,128)(2,1)S(1)}, bf16[256,1024]{1,0:T(8,128)(2,1)S(1)}, u32[]{:S(2)}, u32[]{:S(2)}) collective-permute-start(bf16[256,1024]{1,0:T(8,128)(2,1)S(1)} %fusion.24), channel_id=1, source_target_pairs={{0,2},{1,3},{2,4},{3,5},{4,6},{5,7},{6,0},{7,1},{8,10},{9,11},{10,... | collective-permute-start | bytes 1572872 | tf_op jit(solution)/shard_map/ppermute | solution.py:28
  192.5 15.1 %collective-permute-start.30 = (bf16[256,1024]{1,0:T(8,128)(2,1)S(1)}, bf16[256,1024]{1,0:T(8,128)(2,1)S(1)}, u32[]{:S(2)}, u32[]{:S(2)}) collective-permute-start(bf16[256,1024]{1,0:T(8,128)(2,1)S(1)} %fusion.27), channel_id=1, source_target_pairs={{0,2},{1,3},{2,4},{3,5},{4,6},{5,7},{6,0},{7,1},{8,10},{9,11},{10,... | collective-permute-start | bytes 1572872 | tf_op jit(solution)/shard_map/ppermute | solution.py:28
  215.3 15.8 %collective-permute-start.39 = (bf16[128,2048]{1,0:T(8,128)(2,1)S(1)}, bf16[128,2048]{1,0:T(8,128)(2,1)S(1)}, u32[]{:S(2)}, u32[]{:S(2)}) collective-permute-start(bf16[128,2048]{1,0:T(8,128)(2,1)S(1)} %fusion.8), channel_id=1, source_target_pairs={{0,2},{1,3},{2,4},{3,5},{4,6},{5,7},{6,0},{7,1},{8,10},{9,11},{10,... | collective-permute-start | bytes 1572872 | tf_op jit(solution)/shard_map/ppermute | solution.py:28
  216.3 15.3 %collective-permute-start.36 = (bf16[128,2048]{1,0:T(8,128)(2,1)S(1)}, bf16[128,2048]{1,0:T(8,128)(2,1)S(1)}, u32[]{:S(2)}, u32[]{:S(2)}) collective-permute-start(bf16[128,2048]{1,0:T(8,128)(2,1)S(1)} %get-tuple-element.90), channel_id=1, source_target_pairs={{0,1},{1,0},{2,3},{3,2},{4,5},{5,4},{6,7},{7,6},{8,9},{9,8},{10,11... | collective-permute-start | bytes 1572872 | tf_op jit(solution)/shard_map/ppermute | solution.py:21
  231.4 15.0 %collective-permute-start.40 = (bf16[128,2048]{1,0:T(8,128)(2,1)S(1)}, bf16[128,2048]{1,0:T(8,128)(2,1)S(1)}, u32[]{:S(2)}, u32[]{:S(2)}) collective-permute-start(bf16[128,2048]{1,0:T(8,128)(2,1)S(1)} %fusion.12), channel_id=1, source_target_pairs={{0,2},{1,3},{2,4},{3,5},{4,6},{5,7},{6,0},{7,1},{8,10},{9,11},{10,... | collective-permute-start | bytes 1572872 | tf_op jit(solution)/shard_map/ppermute | solution.py:28
  231.4 15.2 %collective-permute-start.35 = (bf16[128,2048]{1,0:T(8,128)(2,1)S(1)}, bf16[128,2048]{1,0:T(8,128)(2,1)S(1)}, u32[]{:S(2)}, u32[]{:S(2)}) collective-permute-start(bf16[128,2048]{1,0:T(8,128)(2,1)S(1)} %get-tuple-element.87), channel_id=1, source_target_pairs={{0,1},{1,0},{2,3},{3,2},{4,5},{5,4},{6,7},{7,6},{8,9},{9,8},{10,11... | collective-permute-start | bytes 1572872 | tf_op jit(solution)/shard_map/ppermute | solution.py:21
  (34 other events, 404.1 us)
Sparse Core Ops, SparseCore 0:
  60.7 50.8 all-gather.1

commit v5 on v4

--- a/solution.py
+++ b/solution.py
@@ -28,13 +28,10 @@
     return lax.ppermute(value, "kv", pairs)
 
 
-def widen(pieces, bit):
+def widen(rows, bit):
     device_count = lax.axis_size("kv") * lax.axis_size("req")
     pairs = [(d, d ^ (SPAN << bit)) for d in range(device_count)]
-    found = dict(pieces)
-    for index, piece in pieces.items():
-        found[index | 1 << bit] = lax.ppermute(piece, ("req", "kv"), pairs)
-    return found
+    return jnp.concatenate([rows, lax.ppermute(rows, ("req", "kv"), pairs)], 0)
 
 
 def gather_in_order(value):
@@ -223,21 +220,20 @@
 
     bits = list(range(request_count.bit_length() - 1))
     q_mine = [projections[:, :width]]
-    up_pieces, down_pieces = {0: up_weight}, {0: down_weight}
     for step in range(CHIPS - 2):
         q_mine.append(next_chip(q_mine[-1]))
-    up_pieces = widen(up_pieces, bits[0])
-    down_pieces = widen(down_pieces, bits[-1])
+    up_rows = widen(up_weight, bits[0])
+    down_rows = widen(down_weight, bits[-1])
     q_other = [swap_cores(piece) for piece in q_mine[:-1]]
-    q_mine[-1], q_other, up_pieces, down_pieces = lax.optimization_barrier(
-        (q_mine[-1], q_other, up_pieces, down_pieces)
+    q_mine[-1], q_other, up_rows, down_rows = lax.optimization_barrier(
+        (q_mine[-1], q_other, up_rows, down_rows)
     )
     q_mine.append(next_chip(q_mine[-1]))
     q_other += [swap_cores(piece) for piece in q_mine[-2:]]
     for bit in bits[1:]:
-        up_pieces = widen(up_pieces, bit)
+        up_rows = widen(up_rows, bit)
     for bit in reversed(bits[:-1]):
-        down_pieces = widen(down_pieces, bit)
+        down_rows = widen(down_rows, bit)
     head_pairs = [
         (d, (d % request_count) * SPAN + d // request_count) for d in range(device_count)
     ]
@@ -253,6 +249,7 @@
     rows_other = [swap_cores(normed)]
 
     carried = None
+    shares = []
     for phase in range(CHIPS):
         target = (chip + CHIPS - 1 - phase) % CHIPS
         kept = CORES * target + core
@@ -262,17 +259,26 @@
             meta, rows_mine, rows_other = lax.optimization_barrier((meta, rows_mine, rows_other))
             rows_mine.append(next_chip(rows_mine[-1]))
             rows_other.append(swap_cores(rows_mine[-2]))
+        if phase == 2:
+            meta, first = lax.optimization_barrier((meta, merge(shares[0])))
+            carried = next_chip(first)
+        if phase == 3:
+            meta, shares[1] = lax.optimization_barrier((meta, shares[1]))
         out, lse = attend(meta, q_mine + q_other, key_cache, value_cache, projections, bias)
-        if phase == CHIPS - 2:
-            out, up_pieces, down_pieces = lax.optimization_barrier((out, up_pieces, down_pieces))
-        parts = [(out[0], lse[0]), swap_cores((out[1], lse[1]))]
-        if carried is not None:
-            parts.append(carried)
-        carried = merge(parts)
+        shares.append([(out[0], lse[0]), swap_cores((out[1], lse[1]))])
+    for phase in range(1, CHIPS):
+        carried = merge(shares[phase] + [carried])
         if phase < CHIPS - 1:
             carried = next_chip(carried)
-    up_rows = jnp.concatenate([up_pieces[i] for i in range(request_count)], 0)
-    down_rows = jnp.concatenate([down_pieces[i] for i in range(request_count)], 0)
+        if phase == 1:
+            carried, up_rows, down_rows = lax.optimization_barrier(
+                (carried, up_rows, down_rows)
+            )
+    unit_rows = down_weight.shape[0]
+    down_rows = down_rows.reshape([2] * len(bits) + [unit_rows, width]).transpose(
+        list(reversed(range(len(bits)))) + [len(bits), len(bits) + 1]
+    )
+    down_rows = down_rows.reshape(request_count * unit_rows, width)
     rows_other += [swap_cores(piece) for piece in rows_mine[len(rows_other) :]]
     rows = jnp.concatenate(rows_mine + rows_other, 0)
     units = all_units(rows, up_rows, down_rows)

time: 269 us -> 251 us (0.933)
  starting transfers between devices: 51.5 us -> 29.9 us
  other arithmetic: 19.9 us -> 23.8 us
    ppermute x15, waiting for transfers between devices: 109 us -> 85.2 us  [next_chip(): return lax.ppermute(value, 'kv', pairs)]
    ppermute x6 -> x4, waiting for transfers between devices: 12.8 us -> 34.4 us  [widen(): return jnp.concatenate([rows, lax.ppermute(rows, ('req', 'kv'), pairs)], 0)]
    ppermute x6 -> x4, starting transfers between devices: 25.9 us -> 11 us  [widen(): return jnp.concatenate([rows, lax.ppermute(rows, ('req', 'kv'), pairs)], 0)]
    ppermute x15, starting transfers between devices: 21.3 us -> 13.9 us  [next_chip(): return lax.ppermute(value, 'kv', pairs)]
    concatenate x2 -> x4, other arithmetic: 7.5 us -> 10.2 us  [widen(): return jnp.concatenate([rows, lax.ppermute(rows, ('req', 'kv'), pairs)], 0)]
    unnamed x53 -> x55, local copies, waits for them, and re-layouts: 11.4 us -> 11.4 us
  transfers between devices with their start and end apart: 43 -> 41, of which waited for: 15 -> 14; matrix products, arithmetic and copies ran while one was open for 9% -> 12% of each run, Pallas kernels for 16% -> 17%
where the time goes in v5:
time: 251 us; the launch traced here: 250 us
  waiting for transfers between devices  121 us (48%)
  Pallas kernels  43.6 us (17%)
  starting transfers between devices  29.9 us (12%)
  other arithmetic  23.8 us (9%)
  local copies, waits for them, and re-layouts  14.9 us (6%)
  between operations  14.1 us (6%)
  matrix products  2.85 us (1%)
    ppermute x15, waiting for transfers between devices, next_chip(): return lax.ppermute(value, 'kv', pairs)  85.2 us
    ppermute x4, waiting for transfers between devices, widen(): return jnp.concatenate([rows, lax.ppermute(rows, ('req', 'kv'), pairs)], 0)  34.4 us
    pallas_call x4, Pallas kernels, attend(): pl.pallas_call(attend_kernel, grid_spec=pltpu.PrefetchScalarGridSpec(num_...  29.3 us
    pallas_call x1, Pallas kernels, all_units(): pl.pallas_call(units_kernel, grid=(row_count // block,), in_specs=[rows_s...  14.2 us
    ppermute x15, starting transfers between devices, next_chip(): return lax.ppermute(value, 'kv', pairs)  13.9 us
    unnamed x55, local copies, waits for them, and re-layouts  11.4 us
    ppermute x4, starting transfers between devices, widen(): return jnp.concatenate([rows, lax.ppermute(rows, ('req', 'kv'), pairs)], 0)  11 us
    concatenate x4, other arithmetic, widen(): return jnp.concatenate([rows, lax.ppermute(rows, ('req', 'kv'), pairs)], 0)  10.2 us
  transfers between devices with their start and end apart: 41, of which 14 were waited for; matrix products, arithmetic and copies ran while one was open for 12% of the time, Pallas kernels for 17%

profile of v5, /device:TPU:0, one launch (start us, length us, event | category | flops | bytes accessed | tf_op | source)
XLA Modules:
  0.0 249.7 jit_solution(14032263355468073113)
XLA Ops:
  6.5 2.9 %collective-permute-start.4 = (bf16[256,2048]{1,0:T(8,128)(2,1)}, bf16[256,2048]{1,0:T(8,128)(2,1)}, u32[]{:S(2)}, u32[]{:S(2)}) collective-permute-start(bf16[256,2048]{1,0:T(8,128)(2,1)} %param.16), channel_id=1, source_target_pairs={{0,8},{1,9},{2,10},{3,11},{4,12},{5,13},{6,14},{7,15},{8,0},{9,1},... | collective-permute-start | bytes 3145736 | tf_op jit(solution)/shard_map/ppermute | solution.py:34
  10.6 1.6 collective-permute-start
  12.2 1.6 collective-permute-start.32
  13.8 4.4 %collective-permute-start.5 = (bf16[256,2048]{1,0:T(8,128)(2,1)}, bf16[256,2048]{1,0:T(8,128)(2,1)}, u32[]{:S(2)}, u32[]{:S(2)}) collective-permute-start(bf16[256,2048]{1,0:T(8,128)(2,1)} %param.17), channel_id=1, source_target_pairs={{0,16},{1,17},{2,18},{3,19},{4,20},{5,21},{6,22},{7,23},{8,24},{9,... | collective-permute-start | bytes 3145736 | tf_op jit(solution)/shard_map/ppermute | solution.py:34
  21.0 6.4 %collective-permute-done.refs_1_ = bf16[128,2048]{1,0:T(8,128)(2,1)S(1)} collective-permute-done((bf16[128,2048]{1,0:T(8,128)(2,1)S(1)}, bf16[128,2048]{1,0:T(8,128)(2,1)S(1)}, u32[]{:S(2)}, u32[]{:S(2)}) %collective-permute-start) | collective-permute-done | bytes 524320 | tf_op jit(solution)/shard_map/ppermute | solution.py:28
  27.5 8.9 %collective-permute-done.4 = bf16[256,2048]{1,0:T(8,128)(2,1)} collective-permute-done((bf16[256,2048]{1,0:T(8,128)(2,1)}, bf16[256,2048]{1,0:T(8,128)(2,1)}, u32[]{:S(2)}, u32[]{:S(2)}) %collective-permute-start.4) | collective-permute-done | bytes 1048608 | tf_op jit(solution)/shard_map/ppermute | solution.py:34
  36.3 3.1 %pad_maximum_fusion.2 = bf16[512,2048]{1,0:T(8,128)(2,1)} fusion(bf16[256,2048]{1,0:T(8,128)(2,1)} %collective-permute-done.4, bf16[256,2048]{1,0:T(8,128)(2,1)} %param.16), kind=kLoop, calls=%fused_computation.2 | loop fusion | flops 4194304 | bytes 4194304 | tf_op jit(solution)/shard_map/concatenate | solution.py:34
  39.4 4.6 %collective-permute-done.5 = bf16[256,2048]{1,0:T(8,128)(2,1)} collective-permute-done((bf16[256,2048]{1,0:T(8,128)(2,1)}, bf16[256,2048]{1,0:T(8,128)(2,1)}, u32[]{:S(2)}, u32[]{:S(2)}) %collective-permute-start.5) | collective-permute-done | bytes 1048608 | tf_op jit(solution)/shard_map/ppermute | solution.py:34
  44.0 2.8 %pad_maximum_fusion.3 = bf16[512,2048]{1,0:T(8,128)(2,1)} fusion(bf16[256,2048]{1,0:T(8,128)(2,1)} %collective-permute-done.5, bf16[256,2048]{1,0:T(8,128)(2,1)S(1)} %copy-done.15), kind=kLoop, calls=%fused_computation.3 | loop fusion | flops 4194304 | bytes 4194304 | tf_op jit(solution)/shard_map/concatenate | solution.py:34
  47.7 3.4 %collective-permute-start.6 = (bf16[128,2048]{1,0:T(8,128)(2,1)}, bf16[128,2048]{1,0:T(8,128)(2,1)}, u32[]{:S(2)}, u32[]{:S(2)}) collective-permute-start(bf16[128,2048]{1,0:T(8,128)(2,1)} %collective-permute-done.1.refs_2_), channel_id=1, source_target_pairs={{0,2},{1,3},{2,4},{3,5},{4,6},{5,7},{6,0},{7,1},{8,10},{9,11},{10,... | collective-permute-start | bytes 1572872 | tf_op jit(solution)/shard_map/ppermute | solution.py:28
  51.3 2.2 fusion.4
  53.5 12.0 %collective-permute-done.6.refs_3_ = bf16[128,2048]{1,0:T(8,128)(2,1)} collective-permute-done((bf16[128,2048]{1,0:T(8,128)(2,1)}, bf16[128,2048]{1,0:T(8,128)(2,1)}, u32[]{:S(2)}, u32[]{:S(2)}) %collective-permute-start.6) | collective-permute-done | bytes 524320 | tf_op jit(solution)/shard_map/ppermute | solution.py:28
  66.9 1.4 fusion.31.refs_12_
  69.0 11.0 %collective-permute-done.7 = bf16[128,2048]{1,0:T(8,128)(2,1)} collective-permute-done((bf16[128,2048]{1,0:T(8,128)(2,1)}, bf16[128,2048]{1,0:T(8,128)(2,1)}, u32[]{:S(2)}, u32[]{:S(2)}) %collective-permute-start.7) | collective-permute-done | bytes 524320 | tf_op jit(solution)/shard_map/ppermute | solution.py:28
  80.1 2.2 copy-done.3
  84.4 7.2 %shard_map.93 = (bf16[2,256,1024]{2,1,0:T(8,128)(2,1)S(1)}, f32[2,1,1024]{2,1,0:T(1,128)S(1)}) custom-call(s32[4]{0:T(128)S(1)} %add_add_fusion.6.meta, bf16[128,2048]{1,0:T(8,128)(2,1)S(1)} %slice.107.refs_0_, bf16[128,2048]{1,0:T(8,128)(2,1)S(1)} %collective-permute-done.refs_1_, bf16[128,2048]{1,0:T(8,128)(2,1)} %collective-permute-done.1.refs_2_, ...), custom_call_target="tpu_custom_call" | custom-call | flops 2415919104 | bytes 8388608 | tf_op jit(solution)/shard_map/pallas_call | solution.py:117
  92.3 7.6 %shard_map.91 = (bf16[2,256,1024]{2,1,0:T(8,128)(2,1)S(1)}, f32[2,1,1024]{2,1,0:T(1,128)S(1)}) custom-call(s32[4]{0:T(128)S(1)} %add_add_fusion.4.meta, bf16[128,2048]{1,0:T(8,128)(2,1)S(1)} %slice.107.refs_0_, bf16[128,2048]{1,0:T(8,128)(2,1)S(1)} %collective-permute-done.refs_1_, bf16[128,2048]{1,0:T(8,128)(2,1)} %collective-permute-done.1.refs_2_, ...), custom_call_target="tpu_custom_call" | custom-call | flops 2415919104 | bytes 8388608 | tf_op jit(solution)/shard_map/pallas_call | solution.py:117
  102.6 3.2 %collective-permute-start.24 = (bf16[512,2048]{1,0:T(8,128)(2,1)S(1)}, bf16[512,2048]{1,0:T(8,128)(2,1)}, u32[]{:S(2)}, u32[]{:S(2)}) collective-permute-start(bf16[512,2048]{1,0:T(8,128)(2,1)S(1)} %copy-done.10), channel_id=1, source_target_pairs={{0,8},{1,9},{2,10},{3,11},{4,12},{5,13},{6,14},{7,15},{8,0},{9,1},... | collective-permute-start | bytes 6291464 | tf_op jit(solution)/shard_map/ppermute | solution.py:34
  108.2 7.2 %shard_map.94 = (bf16[2,256,1024]{2,1,0:T(8,128)(2,1)S(1)}, f32[2,1,1024]{2,1,0:T(1,128)S(1)}) custom-call(s32[4]{0:T(128)S(1)} %add_add_fusion.5.meta, bf16[128,2048]{1,0:T(8,128)(2,1)S(1)} %slice.107.refs_0_, bf16[128,2048]{1,0:T(8,128)(2,1)S(1)} %collective-permute-done.refs_1_, bf16[128,2048]{1,0:T(8,128)(2,1)} %collective-permute-done.1.refs_2_, ...), custom_call_target="tpu_custom_call" | custom-call | flops 2415919104 | bytes 8388608 | tf_op jit(solution)/shard_map/pallas_call | solution.py:117
  115.4 7.2 %shard_map.92 = (bf16[2,256,1024]{2,1,0:T(8,128)(2,1)S(1)}, f32[2,1,1024]{2,1,0:T(1,128)S(1)}) custom-call(s32[4]{0:T(128)S(1)} %add_add_fusion.3.meta, bf16[128,2048]{1,0:T(8,128)(2,1)S(1)} %slice.107.refs_0_, bf16[128,2048]{1,0:T(8,128)(2,1)S(1)} %collective-permute-done.refs_1_, bf16[128,2048]{1,0:T(8,128)(2,1)} %collective-permute-done.1.refs_2_, ...), custom_call_target="tpu_custom_call" | custom-call | flops 2415919104 | bytes 8388608 | tf_op jit(solution)/shard_map/pallas_call | solution.py:117
  125.0 4.0 %collective-permute-start.20 = (bf16[256,1024]{1,0:T(8,128)(2,1)}, bf16[256,1024]{1,0:T(8,128)(2,1)S(1)}, u32[]{:S(2)}, u32[]{:S(2)}) collective-permute-start(bf16[256,1024]{1,0:T(8,128)(2,1)} %fusion.24), channel_id=1, source_target_pairs={{0,2},{1,3},{2,4},{3,5},{4,6},{5,7},{6,0},{7,1},{8,10},{9,11},{10,... | collective-permute-start | bytes 1572872 | tf_op jit(solution)/shard_map/ppermute | solution.py:28
  129.1 20.0 %collective-permute-done.23 = bf16[512,2048]{1,0:T(8,128)(2,1)} collective-permute-done((bf16[512,2048]{1,0:T(8,128)(2,1)S(1)}, bf16[512,2048]{1,0:T(8,128)(2,1)}, u32[]{:S(2)}, u32[]{:S(2)}) %collective-permute-start.23) | collective-permute-done | bytes 2097184 | tf_op jit(solution)/shard_map/ppermute | solution.py:34
  149.0 2.2 pad_maximum_fusion.up
  152.2 2.1 pad_maximum_fusion.1
  158.6 12.7 %collective-permute-done.22 = f32[1,1024]{1,0:T(1,128)S(1)} collective-permute-done((f32[1,1024]{1,0:T(1,128)S(1)}, f32[1,1024]{1,0:T(1,128)S(1)}, u32[]{:S(2)}, u32[]{:S(2)}) %collective-permute-start.22) | collective-permute-done | bytes 4128 | tf_op jit(solution)/shard_map/ppermute | solution.py:28
  173.6 14.2 %shard_map.95 = f32[1024,2048]{1,0:T(8,128)} custom-call(bf16[1024,2048]{1,0:T(8,128)(2,1)S(1)} %constant_dynamic-update-slice_fusion.rows, bf16[1024,2048]{1,0:T(8,128)(2,1)S(1)} %pad_maximum_fusion.up, bf16[1024,2048]{1,0:T(8,128)(2,1)S(1)} %bitcast.110), custom_call_target="tpu_custom_call" | custom-call | flops 8589934592 | bytes 20971520 | tf_op jit(solution)/shard_map/pallas_call | solution.py:174
  188.6 2.1 fusion.40
  190.7 3.0 %fusion.17 = (bf16[128,2048]{1,0:T(8,128)(2,1)S(1)}, bf16[128,2048]{1,0:T(8,128)(2,1)S(1)}, bf16[128,2048]{1,0:T(8,128)(2,1)S(1)}, bf16[128,2048]{1,0:T(8,128)(2,1)S(1)}) fusion(f32[512,2048]{1,0:T(8,128)S(1)} %fusion.40, f32[1024,2048]{1,0:T(8,128)} %shard_map.95), kind=kLoop, calls=%fused_computation.31 | loop fusion | flops 2097152 | bytes 10485760 | tf_op jit(solution)/shard_map/convert_element_type | solution.py:311
  196.0 2.1 collective-permute-start.37
  198.1 13.8 %collective-permute-done.37 = bf16[128,2048]{1,0:T(8,128)(2,1)S(1)} collective-permute-done((bf16[128,2048]{1,0:T(8,128)(2,1)S(1)}, bf16[128,2048]{1,0:T(8,128)(2,1)S(1)}, u32[]{:S(2)}, u32[]{:S(2)}) %collective-permute-start.37) | collective-permute-done | bytes 524320 | tf_op jit(solution)/shard_map/ppermute | solution.py:28
  212.3 14.9 %collective-permute-done.38 = bf16[128,2048]{1,0:T(8,128)(2,1)S(1)} collective-permute-done((bf16[128,2048]{1,0:T(8,128)(2,1)S(1)}, bf16[128,2048]{1,0:T(8,128)(2,1)S(1)}, u32[]{:S(2)}, u32[]{:S(2)}) %collective-permute-start.38) | collective-permute-done | bytes 524320 | tf_op jit(solution)/shard_map/ppermute | solution.py:28
  227.6 14.1 %collective-permute-done.39 = bf16[128,2048]{1,0:T(8,128)(2,1)S(1)} collective-permute-done((bf16[128,2048]{1,0:T(8,128)(2,1)S(1)}, bf16[128,2048]{1,0:T(8,128)(2,1)S(1)}, u32[]{:S(2)}, u32[]{:S(2)}) %collective-permute-start.39) | collective-permute-done | bytes 524320 | tf_op jit(solution)/shard_map/ppermute | solution.py:28
  (158 shorter events, 29.1 us)
Async XLA Ops:
  6.5 182.1 %all-gather.2.cloned.1.call-start = ((), (), s32[]{:S(2)}) async-start(), calls=%async_computation | async-start | bytes 1310720 | tf_op jit(solution)/shard_map/all_gather | solution.py:42
  6.5 29.8 %collective-permute-start.4 = (bf16[256,2048]{1,0:T(8,128)(2,1)}, bf16[256,2048]{1,0:T(8,128)(2,1)}, u32[]{:S(2)}, u32[]{:S(2)}) collective-permute-start(bf16[256,2048]{1,0:T(8,128)(2,1)} %param.16), channel_id=1, source_target_pairs={{0,8},{1,9},{2,10},{3,11},{4,12},{5,13},{6,14},{7,15},{8,0},{9,1},... | collective-permute-start | bytes 3145736 | tf_op jit(solution)/shard_map/ppermute | solution.py:34
  10.6 16.9 %collective-permute-start = (bf16[128,2048]{1,0:T(8,128)(2,1)S(1)}, bf16[128,2048]{1,0:T(8,128)(2,1)S(1)}, u32[]{:S(2)}, u32[]{:S(2)}) collective-permute-start(bf16[128,2048]{1,0:T(8,128)(2,1)S(1)} %slice.107.refs_0_), channel_id=1, source_target_pairs={{0,2},{1,3},{2,4},{3,5},{4,6},{5,7},{6,0},{7,1},{8,10},{9,11},{10,... | collective-permute-start | bytes 1572872 | tf_op jit(solution)/shard_map/ppermute | solution.py:28
  12.2 34.7 %collective-permute-start.2 = (bf16[128,2048]{1,0:T(8,128)(2,1)S(1)}, bf16[128,2048]{1,0:T(8,128)(2,1)S(1)}, u32[]{:S(2)}, u32[]{:S(2)}) collective-permute-start(bf16[128,2048]{1,0:T(8,128)(2,1)S(1)} %slice.107.refs_0_), channel_id=1, source_target_pairs={{0,1},{1,0},{2,3},{3,2},{4,5},{5,4},{6,7},{7,6},{8,9},{9,8},{10,11... | collective-permute-start | bytes 1572872 | tf_op jit(solution)/shard_map/ppermute | solution.py:21
  12.2 56.1 %collective-permute-start.32 = (bf16[64,2048]{1,0:T(8,128)(2,1)}, bf16[64,2048]{1,0:T(8,128)(2,1)S(1)}, u32[]{:S(2)}, u32[]{:S(2)}) collective-permute-start(bf16[64,2048]{1,0:T(8,128)(2,1)} %param.15), channel_id=1, source_target_pairs={{0,0},{1,8},{2,16},{3,24},{4,1},{5,9},{6,17},{7,25},{8,2},{9,10},{... | collective-permute-start | bytes 786440 | tf_op jit(solution)/shard_map/ppermute | solution.py:240
  13.8 30.2 %collective-permute-start.5 = (bf16[256,2048]{1,0:T(8,128)(2,1)}, bf16[256,2048]{1,0:T(8,128)(2,1)}, u32[]{:S(2)}, u32[]{:S(2)}) collective-permute-start(bf16[256,2048]{1,0:T(8,128)(2,1)} %param.17), channel_id=1, source_target_pairs={{0,16},{1,17},{2,18},{3,19},{4,20},{5,21},{6,22},{7,23},{8,24},{9,... | collective-permute-start | bytes 3145736 | tf_op jit(solution)/shard_map/ppermute | solution.py:34
  27.5 19.4 %collective-permute-start.1 = (bf16[128,2048]{1,0:T(8,128)(2,1)S(1)}, bf16[128,2048]{1,0:T(8,128)(2,1)}, u32[]{:S(2)}, u32[]{:S(2)}) collective-permute-start(bf16[128,2048]{1,0:T(8,128)(2,1)S(1)} %collective-permute-done.refs_1_), channel_id=1, source_target_pairs={{0,2},{1,3},{2,4},{3,5},{4,6},{5,7},{6,0},{7,1},{8,10},{9,11},{10,... | collective-permute-start | bytes 1572872 | tf_op jit(solution)/shard_map/ppermute | solution.py:28
  47.7 17.8 %collective-permute-start.6 = (bf16[128,2048]{1,0:T(8,128)(2,1)}, bf16[128,2048]{1,0:T(8,128)(2,1)}, u32[]{:S(2)}, u32[]{:S(2)}) collective-permute-start(bf16[128,2048]{1,0:T(8,128)(2,1)} %collective-permute-done.1.refs_2_), channel_id=1, source_target_pairs={{0,2},{1,3},{2,4},{3,5},{4,6},{5,7},{6,0},{7,1},{8,10},{9,11},{10,... | collective-permute-start | bytes 1572872 | tf_op jit(solution)/shard_map/ppermute | solution.py:28
  53.5 26.6 %collective-permute-start.11 = (bf16[128,2048]{1,0:T(8,128)(2,1)}, bf16[128,2048]{1,0:T(8,128)(2,1)}, u32[]{:S(2)}, u32[]{:S(2)}) collective-permute-start(bf16[128,2048]{1,0:T(8,128)(2,1)} %collective-permute-done.1.refs_2_), channel_id=1, source_target_pairs={{0,1},{1,0},{2,3},{3,2},{4,5},{5,4},{6,7},{7,6},{8,9},{9,8},{10,11... | collective-permute-start | bytes 1572872 | tf_op jit(solution)/shard_map/ppermute | solution.py:21
  65.5 14.5 %collective-permute-start.7 = (bf16[128,2048]{1,0:T(8,128)(2,1)}, bf16[128,2048]{1,0:T(8,128)(2,1)}, u32[]{:S(2)}, u32[]{:S(2)}) collective-permute-start(bf16[128,2048]{1,0:T(8,128)(2,1)} %fusion.4), channel_id=1, source_target_pairs={{0,2},{1,3},{2,4},{3,5},{4,6},{5,7},{6,0},{7,1},{8,10},{9,11},{10,... | collective-permute-start | bytes 1572872 | tf_op jit(solution)/shard_map/ppermute | solution.py:28
  65.5 14.5 %collective-permute-start.8 = (bf16[128,2048]{1,0:T(8,128)(2,1)}, bf16[128,2048]{1,0:T(8,128)(2,1)}, u32[]{:S(2)}, u32[]{:S(2)}) collective-permute-start(bf16[128,2048]{1,0:T(8,128)(2,1)} %fusion.4), channel_id=1, source_target_pairs={{0,1},{1,0},{2,3},{3,2},{4,5},{5,4},{6,7},{7,6},{8,9},{9,8},{10,11... | collective-permute-start | bytes 1572872 | tf_op jit(solution)/shard_map/ppermute | solution.py:21
  65.5 14.6 %collective-permute-start.12 = (bf16[128,2048]{1,0:T(8,128)(2,1)}, bf16[128,2048]{1,0:T(8,128)(2,1)}, u32[]{:S(2)}, u32[]{:S(2)}) collective-permute-start(bf16[128,2048]{1,0:T(8,128)(2,1)} %collective-permute-done.6.refs_3_), channel_id=1, source_target_pairs={{0,1},{1,0},{2,3},{3,2},{4,5},{5,4},{6,7},{7,6},{8,9},{9,8},{10,11... | collective-permute-start | bytes 1572872 | tf_op jit(solution)/shard_map/ppermute | solution.py:21
  80.1 22.5 %collective-permute-start.9 = (bf16[128,2048]{1,0:T(8,128)(2,1)}, bf16[128,2048]{1,0:T(8,128)(2,1)}, u32[]{:S(2)}, u32[]{:S(2)}) collective-permute-start(bf16[128,2048]{1,0:T(8,128)(2,1)} %collective-permute-done.7), channel_id=1, source_target_pairs={{0,2},{1,3},{2,4},{3,5},{4,6},{5,7},{6,0},{7,1},{8,10},{9,11},{10,... | collective-permute-start | bytes 1572872 | tf_op jit(solution)/shard_map/ppermute | solution.py:28
  80.1 25.8 %collective-permute-start.10 = (bf16[128,2048]{1,0:T(8,128)(2,1)}, bf16[128,2048]{1,0:T(8,128)(2,1)S(1)}, u32[]{:S(2)}, u32[]{:S(2)}) collective-permute-start(bf16[128,2048]{1,0:T(8,128)(2,1)} %collective-permute-done.7), channel_id=1, source_target_pairs={{0,1},{1,0},{2,3},{3,2},{4,5},{5,4},{6,7},{7,6},{8,9},{9,8},{10,11... | collective-permute-start | bytes 1572872 | tf_op jit(solution)/shard_map/ppermute | solution.py:21
  101.0 48.0 %collective-permute-start.23 = (bf16[512,2048]{1,0:T(8,128)(2,1)S(1)}, bf16[512,2048]{1,0:T(8,128)(2,1)}, u32[]{:S(2)}, u32[]{:S(2)}) collective-permute-start(bf16[512,2048]{1,0:T(8,128)(2,1)S(1)} %copy-done.11), channel_id=1, source_target_pairs={{0,16},{1,17},{2,18},{3,19},{4,20},{5,21},{6,22},{7,23},{8,24},{9,... | collective-permute-start | bytes 6291464 | tf_op jit(solution)/shard_map/ppermute | solution.py:34
  102.6 49.6 %collective-permute-start.24 = (bf16[512,2048]{1,0:T(8,128)(2,1)S(1)}, bf16[512,2048]{1,0:T(8,128)(2,1)}, u32[]{:S(2)}, u32[]{:S(2)}) collective-permute-start(bf16[512,2048]{1,0:T(8,128)(2,1)S(1)} %copy-done.10), channel_id=1, source_target_pairs={{0,8},{1,9},{2,10},{3,11},{4,12},{5,13},{6,14},{7,15},{8,0},{9,1},... | collective-permute-start | bytes 6291464 | tf_op jit(solution)/shard_map/ppermute | solution.py:34
  105.8 49.4 %collective-permute-start.29 = (bf16[128,2048]{1,0:T(8,128)(2,1)}, bf16[128,2048]{1,0:T(8,128)(2,1)}, u32[]{:S(2)}, u32[]{:S(2)}) collective-permute-start(bf16[128,2048]{1,0:T(8,128)(2,1)} %collective-permute-done.9), channel_id=1, source_target_pairs={{0,2},{1,3},{2,4},{3,5},{4,6},{5,7},{6,0},{7,1},{8,10},{9,11},{10,... | collective-permute-start | bytes 1572872 | tf_op jit(solution)/shard_map/ppermute | solution.py:28
  105.8 51.7 %collective-permute-start.30 = (bf16[128,2048]{1,0:T(8,128)(2,1)}, bf16[128,2048]{1,0:T(8,128)(2,1)S(1)}, u32[]{:S(2)}, u32[]{:S(2)}) collective-permute-start(bf16[128,2048]{1,0:T(8,128)(2,1)} %collective-permute-done.9), channel_id=1, source_target_pairs={{0,1},{1,0},{2,3},{3,2},{4,5},{5,4},{6,7},{7,6},{8,9},{9,8},{10,11... | collective-permute-start | bytes 1572872 | tf_op jit(solution)/shard_map/ppermute | solution.py:21
  106.1 18.9 %collective-permute-start.19 = (f32[1,1024]{1,0:T(1,128)S(1)}, f32[1,1024]{1,0:T(1,128)S(1)}, u32[]{:S(2)}, u32[]{:S(2)}) collective-permute-start(f32[1,1024]{1,0:T(1,128)S(1)} %get-tuple-element.64), channel_id=1, source_target_pairs={{0,2},{1,3},{2,4},{3,5},{4,6},{5,7},{6,0},{7,1},{8,10},{9,11},{10,... | collective-permute-start | bytes 12296 | tf_op jit(solution)/shard_map/ppermute | solution.py:28
  125.0 29.4 %collective-permute-start.20 = (bf16[256,1024]{1,0:T(8,128)(2,1)}, bf16[256,1024]{1,0:T(8,128)(2,1)S(1)}, u32[]{:S(2)}, u32[]{:S(2)}) collective-permute-start(bf16[256,1024]{1,0:T(8,128)(2,1)} %fusion.24), channel_id=1, source_target_pairs={{0,2},{1,3},{2,4},{3,5},{4,6},{5,7},{6,0},{7,1},{8,10},{9,11},{10,... | collective-permute-start | bytes 1572872 | tf_op jit(solution)/shard_map/ppermute | solution.py:28
  149.0 22.9 %collective-permute-start.27 = (bf16[256,1024]{1,0:T(8,128)(2,1)S(1)}, bf16[256,1024]{1,0:T(8,128)(2,1)S(1)}, u32[]{:S(2)}, u32[]{:S(2)}) collective-permute-start(bf16[256,1024]{1,0:T(8,128)(2,1)S(1)} %slice_bitcast_fusion), channel_id=1, source_target_pairs={{0,1},{1,0},{2,3},{3,2},{4,5},{5,4},{6,7},{7,6},{8,9},{9,8},{10,11... | collective-permute-start | bytes 1572872 | tf_op jit(solution)/shard_map/ppermute | solution.py:21
  152.2 19.7 %collective-permute-start.18 = (f32[1,1024]{1,0:T(1,128)S(1)}, f32[1,1024]{1,0:T(1,128)S(1)}, u32[]{:S(2)}, u32[]{:S(2)}) collective-permute-start(f32[1,1024]{1,0:T(1,128)S(1)} %slice_bitcast_fusion.5), channel_id=1, source_target_pairs={{0,1},{1,0},{2,3},{3,2},{4,5},{5,4},{6,7},{7,6},{8,9},{9,8},{10,11... | collective-permute-start | bytes 12296 | tf_op jit(solution)/shard_map/ppermute | solution.py:21
  154.3 33.7 %collective-permute-start.26 = (bf16[256,1024]{1,0:T(8,128)(2,1)S(1)}, bf16[256,1024]{1,0:T(8,128)(2,1)S(1)}, u32[]{:S(2)}, u32[]{:S(2)}) collective-permute-start(bf16[256,1024]{1,0:T(8,128)(2,1)S(1)} %slice_bitcast_fusion.1), channel_id=1, source_target_pairs={{0,1},{1,0},{2,3},{3,2},{4,5},{5,4},{6,7},{7,6},{8,9},{9,8},{10,11... | collective-permute-start | bytes 1572872 | tf_op jit(solution)/shard_map/ppermute | solution.py:21
  155.2 16.1 %collective-permute-start.21 = (bf16[256,1024]{1,0:T(8,128)(2,1)S(1)}, bf16[256,1024]{1,0:T(8,128)(2,1)S(1)}, u32[]{:S(2)}, u32[]{:S(2)}) collective-permute-start(bf16[256,1024]{1,0:T(8,128)(2,1)S(1)} %add_convert_fusion), channel_id=1, source_target_pairs={{0,2},{1,3},{2,4},{3,5},{4,6},{5,7},{6,0},{7,1},{8,10},{9,11},{10,... | collective-permute-start | bytes 1572872 | tf_op jit(solution)/shard_map/ppermute | solution.py:28
  171.3 16.6 %collective-permute-start.15 = (f32[1,1024]{1,0:T(1,128)S(1)}, f32[1,1024]{1,0:T(1,128)S(1)}, u32[]{:S(2)}, u32[]{:S(2)}) collective-permute-start(f32[1,1024]{1,0:T(1,128)S(1)} %slice_bitcast_fusion.7), channel_id=1, source_target_pairs={{0,1},{1,0},{2,3},{3,2},{4,5},{5,4},{6,7},{7,6},{8,9},{9,8},{10,11... | collective-permute-start | bytes 12296 | tf_op jit(solution)/shard_map/ppermute | solution.py:21
  172.2 15.9 %collective-permute-start.28 = (bf16[256,1024]{1,0:T(8,128)(2,1)S(1)}, bf16[256,1024]{1,0:T(8,128)(2,1)S(1)}, u32[]{:S(2)}, u32[]{:S(2)}) collective-permute-start(bf16[256,1024]{1,0:T(8,128)(2,1)S(1)} %fusion.22), channel_id=1, source_target_pairs={{0,2},{1,3},{2,4},{3,5},{4,6},{5,7},{6,0},{7,1},{8,10},{9,11},{10,... | collective-permute-start | bytes 1572872 | tf_op jit(solution)/shard_map/ppermute | solution.py:28
  172.3 15.7 %collective-permute-start.25 = (f32[1,1024]{1,0:T(1,128)S(1)}, f32[1,1024]{1,0:T(1,128)S(1)}, u32[]{:S(2)}, u32[]{:S(2)}) collective-permute-start(f32[1,1024]{1,0:T(1,128)S(1)} %get-tuple-element.83), channel_id=1, source_target_pairs={{0,2},{1,3},{2,4},{3,5},{4,6},{5,7},{6,0},{7,1},{8,10},{9,11},{10,... | collective-permute-start | bytes 12296 | tf_op jit(solution)/shard_map/ppermute | solution.py:28
  196.0 15.9 %collective-permute-start.37 = (bf16[128,2048]{1,0:T(8,128)(2,1)S(1)}, bf16[128,2048]{1,0:T(8,128)(2,1)S(1)}, u32[]{:S(2)}, u32[]{:S(2)}) collective-permute-start(bf16[128,2048]{1,0:T(8,128)(2,1)S(1)} %fusion.8), channel_id=1, source_target_pairs={{0,2},{1,3},{2,4},{3,5},{4,6},{5,7},{6,0},{7,1},{8,10},{9,11},{10,... | collective-permute-start | bytes 1572872 | tf_op jit(solution)/shard_map/ppermute | solution.py:28
  198.1 14.3 %collective-permute-start.34 = (bf16[128,2048]{1,0:T(8,128)(2,1)S(1)}, bf16[128,2048]{1,0:T(8,128)(2,1)S(1)}, u32[]{:S(2)}, u32[]{:S(2)}) collective-permute-start(bf16[128,2048]{1,0:T(8,128)(2,1)S(1)} %get-tuple-element.91), channel_id=1, source_target_pairs={{0,1},{1,0},{2,3},{3,2},{4,5},{5,4},{6,7},{7,6},{8,9},{9,8},{10,11... | collective-permute-start | bytes 1572872 | tf_op jit(solution)/shard_map/ppermute | solution.py:21
  212.1 15.1 %collective-permute-start.38 = (bf16[128,2048]{1,0:T(8,128)(2,1)S(1)}, bf16[128,2048]{1,0:T(8,128)(2,1)S(1)}, u32[]{:S(2)}, u32[]{:S(2)}) collective-permute-start(bf16[128,2048]{1,0:T(8,128)(2,1)S(1)} %fusion.12), channel_id=1, source_target_pairs={{0,2},{1,3},{2,4},{3,5},{4,6},{5,7},{6,0},{7,1},{8,10},{9,11},{10,... | collective-permute-start | bytes 1572872 | tf_op jit(solution)/shard_map/ppermute | solution.py:28
  212.3 15.2 %collective-permute-start.33 = (bf16[128,2048]{1,0:T(8,128)(2,1)S(1)}, bf16[128,2048]{1,0:T(8,128)(2,1)S(1)}, u32[]{:S(2)}, u32[]{:S(2)}) collective-permute-start(bf16[128,2048]{1,0:T(8,128)(2,1)S(1)} %get-tuple-element.88), channel_id=1, source_target_pairs={{0,1},{1,0},{2,3},{3,2},{4,5},{5,4},{6,7},{7,6},{8,9},{9,8},{10,11... | collective-permute-start | bytes 1572872 | tf_op jit(solution)/shard_map/ppermute | solution.py:21
  227.5 14.2 %collective-permute-start.39 = (bf16[128,2048]{1,0:T(8,128)(2,1)S(1)}, bf16[128,2048]{1,0:T(8,128)(2,1)S(1)}, u32[]{:S(2)}, u32[]{:S(2)}) collective-permute-start(bf16[128,2048]{1,0:T(8,128)(2,1)S(1)} %fusion.16), channel_id=1, source_target_pairs={{0,2},{1,3},{2,4},{3,5},{4,6},{5,7},{6,0},{7,1},{8,10},{9,11},{10,... | collective-permute-start | bytes 1572872 | tf_op jit(solution)/shard_map/ppermute | solution.py:28
  (33 other events, 408.7 us)
Sparse Core Ops, SparseCore 0:
  69.1 29.2 all-gather.1
